TPU v7x, 512 devices: a whole 4x4x16 slice. The times are simulated.
512 devices in a mesh: lat: 128 (over x, z_lo, y), lon: 4 (over z_hi, core).
Axes of the slice: x: 4, y: 4, z: 16 (z_hi: 2, z_lo: 8; z = z_hi * 8 + z_lo), core: 2. Of those that a mesh axis runs over, the one named last changes fastest.
Arguments:
- tokens: bfloat16 [2, 768, 96, 192], P(None, 'lat', 'lon'), may hold values from -6 to 6
- mask_ids: int32 [2, 768, 96], P(None, 'lat', 'lon'), may hold values from 0 to 2
- pos_index: int32 [144, 144], replicated, may hold values from 0 to 3311
- norm_gain: float32 [192], replicated, may hold values from 0.1 to 1.9
- w_qkv: bfloat16 [192, 576], replicated, may hold values from -0.4375 to 0.4375
- w_proj: bfloat16 [192, 192], replicated, may hold values from -0.4375 to 0.4375
- earth_bias: float32 [128, 6, 3312], P('lat'), may hold values from -300 to 300, as said below
- d_out: bfloat16 [2, 768, 96, 192], P(None, 'lat', 'lon'), may hold values from -6 to 6
Outputs:
- updated: bfloat16 [2, 768, 96, 192], P(None, 'lat', 'lon')
- d_tokens: bfloat16 [2, 768, 96, 192], P(None, 'lat', 'lon')
- grad_qkv: float32 [192, 576], replicated
- grad_proj: float32 [192, 192], replicated
- grad_gain: float32 [192], replicated
- grad_bias: float32 [128, 6, 3312], P('lat')
Inputs may be any that keep to these rules, and one draw needn't show every extreme that they name: `earth_bias`: the 2 levels form a single pressure window, so the bias is indexed by latitude window only.
All inputs are finite; a program needn't handle non-finite values.
Results may differ from a plain program's by a relative error of at most 0.019.
Values may be sent and summed in bfloat16 or wider, within the bound.
No kernel may reach another device: no remote copies, remote signals or barrier semaphores. Data moves between devices by JAX's collectives and lax.ppermute only.
A program may use at most 64 MiB of HBM per device.

v0:
```python
import jax
import jax.numpy as jnp
from jax import lax
from jax.sharding import PartitionSpec as P

WPL = 2
WLAT = 6
WLON = 12


epsilon = 1e-05


def shifted(block, axis, distance):
    devices = range(lax.axis_size(axis))
    route = [((i - distance) % len(devices), i) for i in devices]
    return lax.ppermute(block, axis, route)


def normalize(field, norm_gain):
    values = field.astype(jnp.float32)
    center = jnp.mean(values, axis=-1, keepdims=True)
    spread = jnp.mean((values - center) ** 2, axis=-1, keepdims=True)
    return ((values - center) * lax.rsqrt(spread + epsilon) * norm_gain).astype(jnp.bfloat16)


def windowed(field):
    levels, row_count, col_count, channels = field.shape
    blocked = field.reshape(levels, row_count // WLAT, WLAT, col_count // WLON, WLON, channels)
    blocked = blocked.transpose(1, 3, 0, 2, 4, 5)
    return blocked.reshape(row_count // WLAT, col_count // WLON, levels * WLAT * WLON, channels)


def unwindow(blocked, levels):
    lat_win, lon_win, entries, channels = blocked.shape
    field = blocked.reshape(lat_win, lon_win, levels, WLAT, WLON, channels)
    return field.transpose(2, 0, 3, 1, 4, 5).reshape(
        levels, lat_win * WLAT, lon_win * WLON, channels
    )


def attend(packed, region, table, pos_index):
    levels = packed.shape[0]
    channels = packed.shape[3] // 3
    head_count = table.shape[1]
    head_size = channels // head_count
    blocks = windowed(packed)
    lat_win, lon_win, entries, packed_width = blocks.shape
    split = blocks.reshape(lat_win, lon_win, entries, 3, head_count, head_size)
    queries = split[:, :, :, 0]
    keyset = split[:, :, :, 1]
    values = split[:, :, :, 2]
    scores = jnp.einsum(
        "abqhd,abkhd->abhqk", queries, keyset, preferred_element_type=jnp.float32
    ) * head_size ** (-0.5)
    scores = scores + table[:, :, pos_index][:, None]
    labels = windowed(region[..., None])[..., 0]
    same = labels[:, :, None, :, None] == labels[:, :, None, None, :]
    scores = jnp.where(same, scores, -1000000000.0)
    largest = lax.stop_gradient(jnp.max(scores, axis=-1, keepdims=True))
    expo = jnp.exp(scores - largest)
    weights = (expo / jnp.sum(expo, axis=-1, keepdims=True)).astype(jnp.bfloat16)
    mixed = jnp.einsum(
        "abhqk,abkhd->abqhd", weights, values, preferred_element_type=jnp.float32
    ).astype(jnp.bfloat16)
    return unwindow(mixed.reshape(lat_win, lon_win, entries, channels), levels)


def shift_frame(field, forward):
    step_by = -1 if forward else 1
    level_axis = field.ndim - 4
    field = jnp.roll(field, -(WPL // 2) if forward else WPL // 2, axis=level_axis)
    row_axis = level_axis + 1
    col_axis = level_axis + 2
    half_lat = WLAT // 2
    half_lon = WLON // 2
    row_count = field.shape[row_axis]
    col_count = field.shape[col_axis]
    if forward:
        sent = lax.slice_in_dim(field, 0, half_lat, axis=row_axis)
    else:
        sent = lax.slice_in_dim(field, row_count - half_lat, row_count, axis=row_axis)
    piece = shifted(sent, "lat", step_by)
    if forward:
        field = jnp.concatenate(
            [lax.slice_in_dim(field, half_lat, row_count, axis=row_axis), piece], axis=row_axis
        )
    else:
        field = jnp.concatenate(
            [piece, lax.slice_in_dim(field, 0, row_count - half_lat, axis=row_axis)], axis=row_axis
        )
    if forward:
        sent = lax.slice_in_dim(field, 0, half_lon, axis=col_axis)
    else:
        sent = lax.slice_in_dim(field, col_count - half_lon, col_count, axis=col_axis)
    piece = shifted(sent, "lon", step_by)
    if forward:
        field = jnp.concatenate(
            [lax.slice_in_dim(field, half_lon, col_count, axis=col_axis), piece], axis=col_axis
        )
    else:
        field = jnp.concatenate(
            [piece, lax.slice_in_dim(field, 0, col_count - half_lon, axis=col_axis)], axis=col_axis
        )
    return field


def per_device(tokens, mask_ids, pos_index, norm_gain, w_qkv, w_proj, earth_bias, d_out):
    channels = tokens.shape[3]
    rolled = shift_frame(tokens, True)
    d_proj = shift_frame(d_out, True)
    normed, norm_back = jax.vjp(normalize, rolled, norm_gain)
    flat_normed = normed.reshape(-1, channels)
    packed = jnp.dot(flat_normed, w_qkv, preferred_element_type=jnp.float32).astype(jnp.bfloat16)
    packed = packed.reshape(normed.shape[:3] + (3 * channels,))
    mixed, attend_back = jax.vjp(
        lambda first, second: attend(first, mask_ids, second, pos_index), packed, earth_bias
    )
    flat_mixed = mixed.reshape(-1, channels)
    proj = jnp.dot(flat_mixed, w_proj, preferred_element_type=jnp.float32).astype(jnp.bfloat16)
    back_proj = shift_frame(proj.reshape(mixed.shape), False)
    updated = (tokens.astype(jnp.float32) + back_proj.astype(jnp.float32)).astype(jnp.bfloat16)
    flat_dproj = d_proj.reshape(-1, channels)
    grad_proj = jnp.einsum("tc,tf->cf", flat_mixed, flat_dproj, preferred_element_type=jnp.float32)
    d_mixed = jnp.einsum(
        "tf,cf->tc", flat_dproj, w_proj, preferred_element_type=jnp.float32
    ).astype(jnp.bfloat16)
    d_packed, d_table = attend_back(d_mixed.reshape(mixed.shape))
    flat_dpacked = d_packed.reshape(-1, 3 * channels)
    grad_qkv = jnp.einsum(
        "tc,tf->cf", flat_normed, flat_dpacked, preferred_element_type=jnp.float32
    )
    d_normed = jnp.einsum(
        "tf,cf->tc", flat_dpacked, w_qkv, preferred_element_type=jnp.float32
    ).astype(jnp.bfloat16)
    d_rolled, d_gain = norm_back(d_normed.reshape(normed.shape))
    d_back = shift_frame(d_rolled, False)
    d_tokens = (d_out.astype(jnp.float32) + d_back.astype(jnp.float32)).astype(jnp.bfloat16)
    summed = lax.psum((grad_qkv, grad_proj, d_gain), ("lat", "lon"))
    bias_total = lax.psum(d_table.astype(jnp.bfloat16), "lon").astype(jnp.float32)
    cell_count = (
        tokens.shape[0]
        * tokens.shape[1]
        * tokens.shape[2]
        * lax.axis_size("lat")
        * lax.axis_size("lon")
    )
    scale = float(cell_count) ** (-0.5)
    return (updated, d_tokens, summed[0] * scale, summed[1] * scale, summed[2] * scale, bias_total)


def solution(mesh):
    placed = (
        P(None, "lat", "lon", None),
        P(None, "lat", "lon"),
        P(),
        P(),
        P(),
        P(),
        P("lat", None, None),
        P(None, "lat", "lon", None),
    )
    return jax.shard_map(
        per_device,
        mesh=mesh,
        in_specs=placed,
        out_specs=(
            P(None, "lat", "lon", None),
            P(None, "lat", "lon", None),
            P(),
            P(),
            P(),
            P("lat", None, None),
        ),
        check_vma=False,
    )
```

profile of v0, /device:TPU:1, one launch (start us, length us, event | category | flops | bytes accessed | tf_op | source)
XLA Modules:
  0.0 905.4 jit_solution(13052437551140190048)
XLA Ops:
  8.3 18.4 %collective-permute-start = (bf16[2,3,24,192]{3,2,1,0:T(8,128)(2,1)S(1)}, bf16[2,3,24,192]{3,2,1,0:T(8,128)(2,1)S(1)}, u32[]{:S(2)}, u32[]{:S(2)}) collective-permute-start(bf16[2,3,24,192]{3,2,1,0:T(8,128)(2,1)S(1)} %get-tuple-element.51), channel_id=1, source_target_pairs={{4,0},{8,4},{12,8},{16,12},{20,16},{24,20},{28,24},{32,28},{36,32}... | collective-permute-start | bytes 165896 | tf_op jit(solution)/shard_map/ppermute | solution.py:17
  27.6 2.4 collective-permute-start.4
  32.4 38.9 %gather_fusion = f32[20736,6]{1,0:T(8,128)} fusion(f32[6,3312]{0,1:T(8,128)S(1)} %bitcast.108, s32[21504]{0:T(1024)S(1)} %pad_clamp_fusion), kind=kCustom, calls=%fused_computation | custom fusion | bytes 1078272 | tf_op jit(solution)/shard_map/jvp()/gather | solution.py:56
  71.3 12.1 %copy.66 = f32[144,144,6]{0,1,2:T(8,128)} copy(f32[144,144,6]{2,1,0:T(8,128)} %bitcast.109) | data formatting | bytes 995328 | tf_op jit(solution)/shard_map/jvp()/gather | solution.py:56
  83.4 3.1 collective-permute-start.1
  87.2 7.1 collective-permute-start.5
  95.1 3.6 collective-permute-done.1
  103.3 2.1 copy.89
  105.9 2.2 fusion.65
  120.3 2.9 collective-permute-start.2
  124.2 2.0 copy.76
  126.2 1.5 reshape.285
  128.0 1.5 multiply_reduce_fusion
  130.2 2.1 collective-permute-start.6
  133.4 105.5 %psum.30 = f32[192]{0:T(256)S(1)} all-reduce(f32[192]{0:T(256)S(1)} %get-tuple-element.30), channel_id=1, replica_groups=mesh['lat'=128,'lon'=4] {'lat','lon'}, use_global_device_ids=true, to_apply=%region_11.12 | all-reduce | flops 192 | bytes 1536 | tf_op jit(solution)/shard_map/psum | solution.py:139
  238.9 10.4 %copy.85 = f32[144,144,6]{2,1,0:T(8,128)} copy(f32[144,144,6]{0,1,2:T(8,128)S(1)} %bitcast.111) | data formatting | bytes 995328 | tf_op jit(solution)/shard_map/transpose(jvp())/broadcast_in_dim | solution.py:56
  249.3 112.8 %scatter_custom_fusion = f32[6,3312]{0,1:T(8,128)S(1)} fusion(s32[20736]{0:T(1024)} %copy-done.13, f32[20736,6]{1,0:T(8,128)} %bitcast.110, f32[]{:T(128)} %constant.13.clone.1), kind=kCustom, calls=%fused_computation.33 | custom fusion | flops 124416 | bytes 80000 | tf_op jit(solution)/shard_map/transpose(jvp())/scatter-add | solution.py:56
  362.8 68.8 %psum.31 = bf16[1,6,3312]{1,2,0:T(8,128)(2,1)S(1)} all-reduce(bf16[1,6,3312]{1,2,0:T(8,128)(2,1)S(1)} %convert_bitcast_fusion), channel_id=1, replica_groups=mesh['lat'=128,'lon'=4] {'lon'}, use_global_device_ids=true, to_apply=%region_14.15 | all-reduce | flops 19872 | bytes 79488 | tf_op jit(solution)/shard_map/psum | solution.py:140
  433.4 11.6 %collective-permute-start.3 = (bf16[2,6,6,192]{3,2,1,0:T(8,128)(2,1)S(1)}, bf16[2,6,6,192]{3,2,1,0:T(8,128)(2,1)S(1)}, u32[]{:S(2)}, u32[]{:S(2)}) collective-permute-start(bf16[2,6,6,192]{3,2,1,0:T(8,128)(2,1)S(1)} %pad_maximum_fusion.10), channel_id=1, source_target_pairs={{3,0},{0,1},{1,2},{2,3},{7,4},{4,5},{5,6},{6,7},{11,8},{8,9},{9,10... | collective-permute-start | bytes 82952 | tf_op jit(solution)/shard_map/ppermute | solution.py:17
  445.1 1.9 collective-permute-start.7
  447.0 1.6 add_convert_fusion.2
  449.4 445.7 %all-reduce.6.cloned.1.call-done = (f32[192,576]{1,0:T(8,128)}, f32[192,192]{1,0:T(8,128)}) async-done(((f32[192,576]{1,0:T(8,128)}, f32[192,192]{1,0:T(8,128)}), (f32[192,576]{1,0:T(8,128)}, f32[192,192]{1,0:T(8,128)})) %all-reduce.6.cloned.1.call-update) | async-done | bytes 589840 | tf_op jit(solution)/shard_map/psum | solution.py:139
  895.1 1.9 broadcast_multiply_fusion
  897.0 1.6 broadcast_multiply_fusion.1
  (130 shorter events, 28.9 us)
Async XLA Ops:
  7.2 92.9 %copy-start = (bf16[192,576]{1,0:T(8,128)(2,1)S(1)}, bf16[192,576]{1,0:T(8,128)(2,1)}, u32[]{:S(2)}) copy-start(bf16[192,576]{1,0:T(8,128)(2,1)} %param.12) | copy-start | bytes 663556
  7.2 23.9 %copy-start.22 = (s32[2,6,24]{2,0,1:T(2,128)S(1)}, s32[2,6,24]{2,0,1:T(2,128)}, u32[]{:S(2)}) copy-start(s32[2,6,24]{2,0,1:T(2,128)} %param.9) | copy-start | bytes 3460
  7.2 24.6 %copy-start.21 = (f32[1,6,3312]{2,0,1:T(1,128)S(1)}, f32[1,6,3312]{2,0,1:T(1,128)}, u32[]{:S(2)}) copy-start(f32[1,6,3312]{2,0,1:T(1,128)} %param.14) | copy-start | bytes 238468
  7.2 887.9 %all-reduce.6.cloned.1.call-start = ((), (), s32[]{:S(2)}) async-start(), calls=%async_computation | async-start | bytes 1376256 | tf_op jit(solution)/shard_map/psum | solution.py:139
  8.3 75.2 %collective-permute-start = (bf16[2,3,24,192]{3,2,1,0:T(8,128)(2,1)S(1)}, bf16[2,3,24,192]{3,2,1,0:T(8,128)(2,1)S(1)}, u32[]{:S(2)}, u32[]{:S(2)}) collective-permute-start(bf16[2,3,24,192]{3,2,1,0:T(8,128)(2,1)S(1)} %get-tuple-element.51), channel_id=1, source_target_pairs={{4,0},{8,4},{12,8},{16,12},{20,16},{24,20},{28,24},{32,28},{36,32}... | collective-permute-start | bytes 165896 | tf_op jit(solution)/shard_map/ppermute | solution.py:17
  27.6 59.0 %collective-permute-start.4 = (bf16[2,3,24,192]{3,2,1,0:T(8,128)(2,1)S(1)}, bf16[2,3,24,192]{3,2,1,0:T(8,128)(2,1)S(1)}, u32[]{:S(2)}, u32[]{:S(2)}) collective-permute-start(bf16[2,3,24,192]{3,2,1,0:T(8,128)(2,1)S(1)} %get-tuple-element.45), channel_id=1, source_target_pairs={{4,0},{8,4},{12,8},{16,12},{20,16},{24,20},{28,24},{32,28},{36,32}... | collective-permute-start | bytes 165896 | tf_op jit(solution)/shard_map/ppermute | solution.py:17
  31.8 74.1 %copy-start.14 = (pred[2,144,144]{1,2,0:T(8,128)(4,1)}, pred[2,144,144]{1,2,0:T(8,128)(4,1)S(1)}, u32[]{:S(2)}) copy-start(pred[2,144,144]{1,2,0:T(8,128)(4,1)S(1)} %broadcast_compare_fusion) | copy-start | bytes 124420
  83.4 16.6 %copy-start.23 = (f32[192]{0:T(256)S(1)}, f32[192]{0:T(256)}, u32[]{:S(2)}) copy-start(f32[192]{0:T(256)} %param.11) | copy-start | bytes 2308
  83.4 15.2 %collective-permute-start.1 = (bf16[2,6,6,192]{3,2,1,0:T(8,128)(2,1)S(1)}, bf16[2,6,6,192]{3,2,1,0:T(8,128)(2,1)S(1)}, u32[]{:S(2)}, u32[]{:S(2)}) collective-permute-start(bf16[2,6,6,192]{3,2,1,0:T(8,128)(2,1)S(1)} %pad_maximum_fusion.11), channel_id=1, source_target_pairs={{1,0},{2,1},{3,2},{0,3},{5,4},{6,5},{7,6},{4,7},{9,8},{10,9},{11,1... | collective-permute-start | bytes 82952 | tf_op jit(solution)/shard_map/ppermute | solution.py:17
  87.2 20.9 %collective-permute-start.5 = (bf16[2,6,6,192]{3,2,1,0:T(8,128)(2,1)}, bf16[2,6,6,192]{3,2,1,0:T(8,128)(2,1)}, u32[]{:S(2)}, u32[]{:S(2)}) collective-permute-start(bf16[2,6,6,192]{3,2,1,0:T(8,128)(2,1)} %pad_maximum_fusion.9), channel_id=1, source_target_pairs={{1,0},{2,1},{3,2},{0,3},{5,4},{6,5},{7,6},{4,7},{9,8},{10,9},{11,1... | collective-permute-start | bytes 82952 | tf_op jit(solution)/shard_map/ppermute | solution.py:17
  105.9 3.2 copy-start.11
  109.0 3.9 copy-start.1
  117.5 5.8 copy-start.16
  117.5 5.8 copy-start.17
  119.6 3.6 copy-start.3
  119.7 3.6 copy-start.5
  120.3 312.3 %collective-permute-start.2 = (bf16[2,3,24,192]{3,2,1,0:T(8,128)(2,1)}, bf16[2,3,24,192]{3,2,1,0:T(8,128)(2,1)}, u32[]{:S(2)}, u32[]{:S(2)}) collective-permute-start(bf16[2,3,24,192]{3,2,1,0:T(8,128)(2,1)} %fusion.41), channel_id=1, source_target_pairs={{508,0},{0,4},{4,8},{8,12},{12,16},{16,20},{20,24},{24,28},{28,32}... | collective-permute-start | bytes 165896 | tf_op jit(solution)/shard_map/ppermute | solution.py:17
  130.2 314.9 %collective-permute-start.6 = (bf16[2,3,24,192]{3,2,1,0:T(8,128)(2,1)S(1)}, bf16[2,3,24,192]{3,2,1,0:T(8,128)(2,1)S(1)}, u32[]{:S(2)}, u32[]{:S(2)}) collective-permute-start(bf16[2,3,24,192]{3,2,1,0:T(8,128)(2,1)S(1)} %fusion.39), channel_id=1, source_target_pairs={{508,0},{0,4},{4,8},{8,12},{12,16},{16,20},{20,24},{24,28},{28,32}... | collective-permute-start | bytes 165896 | tf_op jit(solution)/shard_map/ppermute | solution.py:17
  362.2 70.4 %copy-start.4 = (bf16[144,192]{1,0:T(8,128)(2,1)S(1)}, bf16[144,192]{1,0:T(8,128)(2,1)}, u32[]{:S(2)}) copy-start(bf16[144,192]{1,0:T(8,128)(2,1)} %copy-done.3) | copy-start | bytes 165892
  362.2 70.4 %copy-start.6 = (bf16[144,192]{1,0:T(8,128)(2,1)S(1)}, bf16[144,192]{1,0:T(8,128)(2,1)}, u32[]{:S(2)}) copy-start(bf16[144,192]{1,0:T(8,128)(2,1)} %copy-done.5) | copy-start | bytes 165892
  362.8 84.2 %copy-start.8 = (bf16[2,6,24,192]{3,2,1,0:T(8,128)(2,1)S(1)}, bf16[2,6,24,192]{3,2,1,0:T(8,128)(2,1)}, u32[]{:S(2)}) copy-start(bf16[2,6,24,192]{3,2,1,0:T(8,128)(2,1)} %param.8) | copy-start | bytes 331780
  431.6 17.0 %copy-start.9 = (bf16[2,6,24,192]{3,2,1,0:T(8,128)(2,1)S(1)}, bf16[2,6,24,192]{3,2,1,0:T(8,128)(2,1)}, u32[]{:S(2)}) copy-start(bf16[2,6,24,192]{3,2,1,0:T(8,128)(2,1)} %param.15) | copy-start | bytes 331780
  433.4 13.6 %collective-permute-start.3 = (bf16[2,6,6,192]{3,2,1,0:T(8,128)(2,1)S(1)}, bf16[2,6,6,192]{3,2,1,0:T(8,128)(2,1)S(1)}, u32[]{:S(2)}, u32[]{:S(2)}) collective-permute-start(bf16[2,6,6,192]{3,2,1,0:T(8,128)(2,1)S(1)} %pad_maximum_fusion.10), channel_id=1, source_target_pairs={{3,0},{0,1},{1,2},{2,3},{7,4},{4,5},{5,6},{6,7},{11,8},{8,9},{9,10... | collective-permute-start | bytes 82952 | tf_op jit(solution)/shard_map/ppermute | solution.py:17
  445.1 3.6 collective-permute-start.7
  (10 other events, 13.7 us)
Sparse Core Ops, SparseCore 0:
  432.8 462.3 all-reduce.5
where the time goes:
time: 906 us; the launch traced here: 905 us
  waiting for transfers between devices  449 us (50%)
  blocking collectives  174 us (19%)
  other arithmetic  127 us (14%)
  local copies, waits for them, and re-layouts  80.8 us (9%)
  starting transfers between devices  49.5 us (5%)
  between operations  14.8 us (2%)
  matrix products  10.1 us (1%)
    psum x1, waiting for transfers between devices, per_device(): summed = lax.psum((grad_qkv, grad_proj, d_gain), ('lat', 'lon'))  446 us
    scatter-add x1, other arithmetic, attend(): scores = scores + table[:, :, pos_index][:, None]  113 us
    psum x1, blocking collectives, per_device(): summed = lax.psum((grad_qkv, grad_proj, d_gain), ('lat', 'lon'))  106 us
    psum x1, blocking collectives, per_device(): lax.psum(d_table.astype(jnp.bfloat16), 'lon').astype(jnp.float32)  68.8 us
    gather x2, local copies, waits for them, and re-layouts, attend(): scores = scores + table[:, :, pos_index][:, None]  51.1 us
    ppermute x8, starting transfers between devices, shifted(): return lax.ppermute(block, axis, route)  49.5 us
  transfers between devices with their start and end apart: 9, of which 2 were waited for; matrix products, arithmetic and copies ran while one was open for 22% of the time, Pallas kernels for 0%

commit v1 on v0

v1 whole, which is shorter than its diff:
```python
import jax
import jax.numpy as jnp
import numpy as np
from jax import lax
from jax.experimental import pallas as pl
from jax.experimental.pallas import tpu as pltpu
from jax.sharding import PartitionSpec as P

BF = jnp.bfloat16
F32 = jnp.float32

WPL, WLAT, WLON = 2, 6, 12
HALF_LAT, HALF_LON = WLAT // 2, WLON // 2
ROWS, COLS = 6, 24
C = 192
HEADS = 6
HEAD = C // HEADS
WIN = WPL * WLAT * WLON
WINDOWS = COLS // WLON
NPOS = 3312
HI = -(-NPOS // 128)
HIP = 32
EDGE = 8
N_OWN = WPL * ROWS * COLS
N_LAT = WPL * HALF_LAT * COLS
N_EDGE = WPL * HALF_LAT * EDGE
N_ALL = N_OWN + N_LAT + 2 * N_EDGE
MAIN = 128
REST = WIN - MAIN
PAIRS = HEADS * MAIN + 128
EPS = 1e-05
SCALE = HEAD**-0.5
NEG = -1000000000.0
G_ROWS = 1280
VMEM_LIMIT = 48 * 1024 * 1024

SPLIT = (4, 8, 4, 2, 2)
AXES = ("x", "zl", "y", "zh", "c")
LAT_AXES = ("x", "zl", "y")
LON_AXES = ("zh", "c")
PLANE = ("x", "y", "c")
LINE = ("zh", "zl")


def source_rows():
    at = np.zeros((WINDOWS, WIN), np.int32)
    for level in range(WPL):
        for row in range(ROWS):
            for col in range(COLS):
                from_level = (level + WPL // 2) % WPL
                r, c = row + HALF_LAT, col + HALF_LON
                if r < ROWS and c < COLS:
                    src = from_level * ROWS * COLS + r * COLS + c
                elif c < COLS:
                    src = N_OWN + from_level * HALF_LAT * COLS + (r - ROWS) * COLS + c
                elif r < ROWS:
                    src = N_OWN + N_LAT + from_level * HALF_LAT * EDGE + (r - HALF_LAT) * EDGE + c - COLS
                else:
                    src = N_OWN + N_LAT + N_EDGE + from_level * HALF_LAT * EDGE + (r - ROWS) * EDGE + c - COLS
                at[col // WLON, level * WLAT * WLON + row * WLON + col % WLON] = src
    return at


def constants():
    at = source_rows()
    pick = np.zeros((WINDOWS, WIN, N_ALL), np.float32)
    for w in range(WINDOWS):
        pick[w, np.arange(WIN), at[w]] = 1.0
    back = pick.transpose(0, 2, 1)
    spread = np.zeros((256, WIN), np.float32)
    for lane in range(MAIN):
        spread[lane, lane] = 1.0
    for lane in range(HEADS * REST):
        spread[MAIN + lane, MAIN + lane % REST] = 1.0
    return pick.astype(BF), back.astype(BF), spread.astype(BF)


def dot(a, b, dims):
    return lax.dot_general(a, b, ((dims[:1], dims[1:]), ((), ())), preferred_element_type=F32)


def nn(a, b):
    return dot(a, b, (1, 0))


def nt(a, b):
    return dot(a, b, (1, 1))


def eye(n):
    return (lax.broadcasted_iota(jnp.int32, (n, n), 0) == lax.broadcasted_iota(jnp.int32, (n, n), 1)).astype(F32).astype(BF)


def cut_kernel(tokens, d_out, lat, lon, diag):
    for i, ref in enumerate((tokens, d_out)):
        top = ref[:, :HALF_LAT]
        lat[i] = top
        diag[i] = top[:, :, :EDGE]
        lon[i] = ref[:, HALF_LAT:, :, :][:, :, :EDGE]


def tables_kernel(pos, table, spread, w_qkv, w_proj, mask, bias, hi_out, lo_out, w3, w3t, wpt, blocked, lo_scr):
    one = eye(WIN)
    idx = pos[...]
    hi = lax.shift_right_logical(idx, 7)
    lo = lax.bitwise_and(idx, 127)
    sp = spread[...]
    hi2 = nt(nt(one, hi.astype(F32).astype(BF)).astype(BF), sp)
    lo2 = nt(nt(one, lo.astype(F32).astype(BF)).astype(BF), sp)
    hi2 = hi2.astype(jnp.int32)
    lo2 = lo2.astype(jnp.int32)
    hi_out[...] = hi2
    lo_out[...] = lo2

    def step(block, carry):
        rows = pl.ds(pl.multiple_of(block * 8, 8), 8)
        lane = lax.broadcasted_iota(jnp.int32, (8, 128), 1)
        for tile in range(2):
            cols = pl.ds(tile * 128, 128)
            h_idx = hi_out[rows, cols]
            l_idx = lo_out[rows, cols]
            if tile == 0:
                acc = [jnp.zeros((8, 128), F32) for _ in range(HEADS)]
            else:
                acc = [jnp.zeros((8, 128), F32)]
            for part in range(HI):
                width = min(128, NPOS - part * 128)
                hit = h_idx == part
                for head in range(HEADS):
                    row = jnp.broadcast_to(lo_scr[head : head + 1, pl.ds(part * 128, 128)], (8, 128))
                    got = jnp.take_along_axis(row, l_idx, axis=1, mode="promise_in_bounds")
                    if tile == 0:
                        acc[head] = jnp.where(hit, got, acc[head])
                    else:
                        mine = hit & (lax.shift_right_logical(lane, 4) == head)
                        acc[0] = jnp.where(mine, got, acc[0])
            if tile == 0:
                for head in range(HEADS):
                    bias[rows, pl.ds(head * MAIN, 128)] = acc[head]
            else:
                bias[rows, pl.ds(HEADS * MAIN, 128)] = acc[0]
        return carry

    lo_scr[:, : HI * 128] = jnp.zeros((HEADS, HI * 128), F32)
    lo_scr[:, :NPOS] = table[0]
    lax.fori_loop(0, WIN // 8, step, 0)

    one = eye(C)
    for i in range(3):
        w = w_qkv[:, C * i : C * (i + 1)]
        w3[i] = w
        w3t[i] = nt(one, w).astype(BF)
    wpt[...] = nt(one, w_proj[...]).astype(BF)

    lab = mask[...].astype(F32).reshape(WPL * ROWS, COLS).astype(BF)
    for w in range(WINDOWS):
        lane = lax.broadcasted_iota(jnp.int32, (COLS, WIN), 1)
        col = lax.broadcasted_iota(jnp.int32, (COLS, WIN), 0)
        across = (lax.rem(lane, WLON) + w * WLON == col).astype(F32).astype(BF)
        wide = nn(lab, across)
        r = lax.broadcasted_iota(jnp.int32, (WPL * ROWS, WIN), 0)
        a = lax.broadcasted_iota(jnp.int32, (WPL * ROWS, WIN), 1)
        row = jnp.sum(jnp.where(lax.div(a, WLON) == r, wide, 0.0), axis=0, keepdims=True)
        row = jnp.broadcast_to(row, (WIN, WIN)).astype(BF)
        down = nt(eye(WIN), row)
        over = nt(row, sp)
        blocked[w] = jnp.where(over == jnp.broadcast_to(down[:, :1], (WIN, 256)), 0.0, NEG)


def by_head(x):
    lane = lax.broadcasted_iota(jnp.int32, (1, C), 1)
    keep = [((lane >= HEAD * h) & (lane < HEAD * (h + 1))).astype(F32).astype(BF) for h in range(HEADS)]
    parts = [x[:MAIN] * keep[h] for h in range(HEADS)]
    parts += [x[MAIN:] * keep[h] for h in range(HEADS)]
    parts.append(jnp.zeros((PAIRS - HEADS * WIN, C), BF))
    return jnp.concatenate(parts, axis=0)


def heads_apart(left, right, scale):
    main = [
        nn(left[HEAD * h : HEAD * (h + 1)], right[:, MAIN * h : MAIN * (h + 1)]) for h in range(HEADS)
    ]
    main = (jnp.concatenate(main, axis=0) * scale).astype(BF)
    rest = nn(left, right[:, HEADS * MAIN :]) * scale
    row = lax.broadcasted_iota(jnp.int32, (C, 128), 0)
    lane = lax.broadcasted_iota(jnp.int32, (C, 128), 1)
    rest = jnp.where(lax.div(row, HEAD) == lax.div(lane, REST), rest, 0.0).astype(BF)
    fold_l = lax.broadcasted_iota(jnp.int32, (128, REST), 0)
    fold_a = lax.broadcasted_iota(jnp.int32, (128, REST), 1)
    fold = (lax.rem(fold_l, REST) == fold_a).astype(F32).astype(BF)
    rest = nn(rest, fold).astype(BF)
    return jnp.concatenate([main, rest], axis=1)


def block_kernel(
    own_x, own_d, lat, lon, diag, pick, back, gain, w3, w3t, wp, wpt, bias, blocked,
    base_x, base_d, out_lat, out_lon, out_diag, grads, d_bias,
):
    x_all = jnp.concatenate([own_x[...], lat[0], lon[0], diag[0]], axis=0)
    d_all = jnp.concatenate([own_d[...], lat[1], lon[1], diag[1]], axis=0)
    eye_c = eye(C)
    eye_w = eye(WIN)
    g = gain[...]
    sums = [jnp.zeros((C, C), F32) for _ in range(4)]
    d_gain = jnp.zeros((C, 1), F32)
    x_back = jnp.zeros((N_ALL, C), F32)
    d_back = jnp.zeros((N_ALL, C), F32)
    for w in range(WINDOWS):
        x = nn(pick[w], x_all).astype(BF)
        d_proj = nn(pick[w], d_all).astype(BF)
        xt = nt(eye_c, x)
        mean = jnp.sum(xt, axis=0, keepdims=True) * (1.0 / C)
        centered = xt - mean
        var = jnp.sum(centered * centered, axis=0, keepdims=True) * (1.0 / C)
        rstd = lax.rsqrt(var + EPS)
        xhat = centered * rstd
        nt_w = (xhat * g).astype(BF)
        n_w = nt(eye_w, nt_w).astype(BF)
        q = nn(n_w, w3[0]).astype(BF)
        k = nn(n_w, w3[1]).astype(BF)
        v = nn(n_w, w3[2]).astype(BF)
        kt = nn(w3t[1], nt_w).astype(BF)
        vt = nn(w3t[2], nt_w).astype(BF)
        qm = by_head(q)
        dm = by_head(nt(d_proj, wp[...]).astype(BF))
        far = jnp.concatenate([blocked[w, :, :MAIN]] * HEADS + [blocked[w, :, MAIN:]], axis=1)
        s = nt(k, qm) * SCALE + bias[...] + far
        e = jnp.exp(s - jnp.max(s, axis=0, keepdims=True))
        p = e * (1.0 / jnp.sum(e, axis=0, keepdims=True))
        attn = p.astype(BF)
        d_attn = nt(v, dm)
        pd = p * d_attn
        ds = pd - p * jnp.sum(pd, axis=0, keepdims=True)
        dsb = ds.astype(BF)
        if w == 0:
            d_bias[...] = ds
        else:
            d_bias[...] += ds
        mixed_t = heads_apart(vt, attn, 1.0)
        dq_t = heads_apart(kt, dsb, SCALE)
        dk = (nn(dsb, qm) * SCALE).astype(BF)
        dv = nn(attn, dm).astype(BF)
        proj_t = nn(wpt[...], mixed_t).astype(BF)
        x_back = x_back + nt(back[w], proj_t)
        sums[0] = sums[0] + nt(nt_w, dq_t)
        sums[1] = sums[1] + nn(nt_w, dk)
        sums[2] = sums[2] + nn(nt_w, dv)
        sums[3] = sums[3] + nn(mixed_t, d_proj)
        dn = nn(w3[0], dq_t) + nt(w3[1], dk) + nt(w3[2], dv)
        dn = dn.astype(BF).astype(F32)
        d_gain = d_gain + jnp.sum(dn * xhat, axis=1, keepdims=True)
        dy = dn * g
        m1 = jnp.sum(dy, axis=0, keepdims=True) * (1.0 / C)
        m2 = jnp.sum(dy * xhat, axis=0, keepdims=True) * (1.0 / C)
        dx = (rstd * (dy - m1 - xhat * m2)).astype(BF)
        d_back = d_back + nt(back[w], dx)
    for i in range(4):
        grads[C * i : C * (i + 1), :] = sums[i][:, :128].astype(BF)
    for i in range(2):
        pair = jnp.concatenate([sums[2 * i][:, 128:], sums[2 * i + 1][:, 128:]], axis=1)
        grads[C * (4 + i) : C * (5 + i), :] = pair.astype(BF)
    lane = lax.broadcasted_iota(jnp.int32, (128, 128), 1)
    tail = jnp.concatenate([d_gain[128:], jnp.zeros((256 - C, 1), F32)], axis=0)
    both = jnp.where(lane == 0, d_gain[:128], jnp.where(lane == 1, tail, 0.0))
    grads[6 * C :, :] = both.astype(BF)
    for i, (total, own, base) in enumerate(((x_back, own_x, base_x), (d_back, own_d, base_d))):
        base[...] = (own[...].astype(F32) + total[:N_OWN]).astype(BF)
        out_lat[i] = total[N_OWN : N_OWN + N_LAT].astype(BF)
        out_lon[i] = total[N_OWN + N_LAT : N_OWN + N_LAT + N_EDGE].astype(BF)
        out_diag[i] = total[N_OWN + N_LAT + N_EDGE :].astype(BF)


def scatter_kernel(d_bias, hi, lo, out, acc):
    acc[...] = jnp.zeros_like(acc)

    def step(block, carry):
        rows = pl.ds(pl.multiple_of(block * 8, 8), 8)
        h_all = hi[rows, :]
        l_all = lo[rows, :]
        d_all = d_bias[rows, :]
        part = lax.broadcasted_iota(jnp.int32, (HIP, 256), 0)
        group = lax.shift_right_logical(lax.broadcasted_iota(jnp.int32, (HIP, 128), 1), 4)
        place = lax.broadcasted_iota(jnp.int32, (128, 256), 0)
        total = acc[...]
        for i in range(8):
            hit = jnp.broadcast_to(h_all[i : i + 1], (HIP, 256)) == part
            rest = jnp.broadcast_to(d_all[i : i + 1, HEADS * MAIN :], (HIP, 128))
            rest = jnp.where(hit[:, 128:], rest, 0.0)
            many = []
            for head in range(HEADS):
                main = jnp.broadcast_to(d_all[i : i + 1, MAIN * head : MAIN * (head + 1)], (HIP, 128))
                main = jnp.where(hit[:, :128], main, 0.0)
                many.append(jnp.concatenate([main, jnp.where(group == head, rest, 0.0)], axis=1))
            many = jnp.concatenate(many, axis=0).astype(BF)
            spot = (jnp.broadcast_to(l_all[i : i + 1], (128, 256)) == place).astype(F32).astype(BF)
            total = total + nt(many, spot)
        acc[...] = total
        return carry

    lax.fori_loop(0, WIN // 8, step, 0)
    out[...] = acc[...].astype(BF)


def finish_kernel(base_x, base_d, lat, lon, diag, tabs, out_x, out_d, out_t):
    for i, (base, out) in enumerate(((base_x, out_x), (base_d, out_d))):
        a = base[...].astype(F32)
        edge = jnp.concatenate([diag[i].astype(F32), lon[i].astype(F32)], axis=1)
        pad = jnp.zeros((WPL, ROWS, COLS - EDGE, C), F32)
        far = jnp.concatenate([lat[i].astype(F32), jnp.zeros((WPL, HALF_LAT, COLS, C), F32)], axis=1)
        out[...] = (a + jnp.concatenate([edge, pad], axis=2) + far).astype(BF)
    t = jnp.sum(tabs[...].astype(F32), axis=0)
    for part in range(HI):
        width = min(128, NPOS - part * 128)
        for head in range(HEADS):
            row = head * HIP + part
            out_t[0, head : head + 1, part * 128 : part * 128 + width] = t[row : row + 1, :width]


def unpack_kernel(g, scale, qkv, proj, gain):
    k = scale
    full = [g[C * i : C * (i + 1), :].astype(F32) * k for i in range(6)]
    qkv[:, 0:128] = full[0]
    qkv[:, 128:256] = jnp.concatenate([full[4][:, :64], full[1][:, :64]], axis=1)
    qkv[:, 256:384] = jnp.concatenate([full[1][:, 64:], full[4][:, 64:]], axis=1)
    qkv[:, 384:512] = full[2]
    qkv[:, 512:576] = full[5][:, :64]
    proj[:, 0:128] = full[3]
    proj[:, 128:192] = full[5][:, 64:]
    gain[...] = g[6 * C :, :].astype(F32) * k


def call(kernel, out_shape, *args, scratch=(), cost=(0, 0)):
    return pl.pallas_call(
        kernel,
        out_shape=out_shape,
        scratch_shapes=list(scratch),
        compiler_params=pltpu.CompilerParams(vmem_limit_bytes=VMEM_LIMIT),
        cost_estimate=pl.CostEstimate(flops=cost[0], bytes_accessed=cost[1], transcendentals=0),
    )(*args)


def sds(shape, dtype):
    return jax.ShapeDtypeStruct(shape, dtype)


def make(sizes):
    n_lat = sizes[0] * sizes[1] * sizes[2]
    n_lon = sizes[3] * sizes[4]
    n_plane = sizes[0] * sizes[2] * sizes[4]
    n_line = sizes[1] * sizes[3]
    piece = G_ROWS // n_plane

    def route(d_lat, d_lon):
        return [
            (a * n_lon + b, (a + d_lat) % n_lat * n_lon + (b + d_lon) % n_lon)
            for a in range(n_lat)
            for b in range(n_lon)
        ]

    def per_device(tokens, mask_ids, pos_index, norm_gain, w_qkv, w_proj, earth_bias, d_out):
        pick, back, spread = (jnp.asarray(c) for c in constants())
        lat, lon, diag = call(
            cut_kernel,
            (
                sds((2, WPL, HALF_LAT, COLS, C), BF),
                sds((2, WPL, HALF_LAT, EDGE, C), BF),
                sds((2, WPL, HALF_LAT, EDGE, C), BF),
            ),
            tokens,
            d_out,
        )
        lat = lax.ppermute(lat, AXES, route(-1, 0))
        lon = lax.ppermute(lon, AXES, route(0, -1))
        diag = lax.ppermute(diag, AXES, route(-1, -1))
        bias, hi, lo, w3, w3t, wpt, blocked = call(
            tables_kernel,
            (
                sds((WIN, PAIRS), F32),
                sds((WIN, 256), jnp.int32),
                sds((WIN, 256), jnp.int32),
                sds((3, C, C), BF),
                sds((3, C, C), BF),
                sds((C, C), BF),
                sds((WINDOWS, WIN, 256), F32),
            ),
            pos_index,
            earth_bias,
            spread,
            w_qkv,
            w_proj,
            mask_ids,
            scratch=[pltpu.VMEM((HEADS, HI * 128), F32)],
            cost=(10**9, 10**6),
        )
        base_x, base_d, out_lat, out_lon, out_diag, grads, d_bias = call(
            block_kernel,
            (
                sds((N_OWN, C), BF),
                sds((N_OWN, C), BF),
                sds((2, N_LAT, C), BF),
                sds((2, N_EDGE, C), BF),
                sds((2, N_EDGE, C), BF),
                sds((G_ROWS, 128), BF),
                sds((WIN, PAIRS), F32),
            ),
            tokens.reshape(N_OWN, C),
            d_out.reshape(N_OWN, C),
            lat.reshape(2, N_LAT, C),
            lon.reshape(2, N_EDGE, C),
            diag.reshape(2, N_EDGE, C),
            pick,
            back,
            norm_gain.reshape(C, 1),
            w3,
            w3t,
            w_proj,
            wpt,
            bias,
            blocked,
        )
        parts = lax.all_to_all(grads.reshape(n_plane, piece, 128), PLANE, 0, 0)
        part = jnp.sum(parts.astype(F32), axis=0).astype(BF)
        line = lax.all_gather(part, LINE)

        table = call(
            scatter_kernel,
            sds((HEADS * HIP, 128), BF),
            d_bias,
            hi,
            lo,
            scratch=[pltpu.VMEM((HEADS * HIP, 128), F32)],
        )
        tabs = lax.all_to_all(jnp.broadcast_to(table, (n_lon,) + table.shape), LON_AXES, 0, 0)
        out_lat = lax.ppermute(out_lat, AXES, route(1, 0))
        out_diag = lax.ppermute(out_diag, AXES, route(1, 1))
        out_lon = lax.ppermute(out_lon, AXES, route(0, 1))
        updated, d_tokens, d_table = call(
            finish_kernel,
            (
                sds((WPL, ROWS, COLS, C), BF),
                sds((WPL, ROWS, COLS, C), BF),
                sds((1, HEADS, NPOS), F32),
            ),
            base_x.reshape(WPL, ROWS, COLS, C),
            base_d.reshape(WPL, ROWS, COLS, C),
            out_lat.reshape(2, WPL, HALF_LAT, COLS, C),
            out_lon.reshape(2, WPL, HALF_LAT, EDGE, C),
            out_diag.reshape(2, WPL, HALF_LAT, EDGE, C),
            tabs,
        )
        total = jnp.sum(line.astype(F32), axis=0).astype(BF)
        whole = lax.all_to_all(jnp.broadcast_to(total, (n_plane,) + total.shape), PLANE, 0, 0)
        scale = float(n_lat * n_lon * N_OWN) ** -0.5
        qkv, proj, gain = call(
            lambda g, a, b, c: unpack_kernel(g, scale, a, b, c),
            (sds((C, 3 * C), F32), sds((C, C), F32), sds((128, 128), F32)),
            whole.reshape(G_ROWS, 128),
        )
        gain = jnp.concatenate([gain[:, 0], gain[: C - 128, 1]])
        return updated, d_tokens, qkv, proj, gain, d_table

    return per_device


def solution(mesh):
    fine = jax.sharding.Mesh(mesh.devices.reshape(SPLIT), AXES)
    placed = (
        P(None, LAT_AXES, LON_AXES, None),
        P(None, LAT_AXES, LON_AXES),
        P(),
        P(),
        P(),
        P(),
        P(LAT_AXES, None, None),
        P(None, LAT_AXES, LON_AXES, None),
    )
    return jax.shard_map(
        make(SPLIT),
        mesh=fine,
        in_specs=placed,
        out_specs=(
            P(None, LAT_AXES, LON_AXES, None),
            P(None, LAT_AXES, LON_AXES, None),
            P(),
            P(),
            P(),
            P(LAT_AXES, None, None),
        ),
        check_vma=False,
    )
```

time: 906 us -> 152 us (0.17)
  waiting for transfers between devices: 449 us -> 17.6 us
  blocking collectives: 174 us -> 27.1 us
  other arithmetic: 127 us -> 0.67 us
  local copies, waits for them, and re-layouts: 80.8 us -> 16.7 us
  Pallas kernels: 0 us -> 22.6 us
  starting transfers between devices: 49.5 us -> 65.2 us
  between operations: 14.8 us -> 0.92 us
  matrix products: 10.1 us -> 0 us
    psum x1 -> x0, waiting for transfers between devices: 446 us -> none  [per_device(): summed = lax.psum((grad_qkv, grad_proj, d_gain), ('lat', 'lon'))]
    psum x2 -> x0, blocking collectives: 174 us -> none  [the longest x1 106 us: per_device(): summed = lax.psum((grad_qkv, grad_proj, d_gain), ('lat', 'lon'))]
    scatter-add x1 -> x0, other arithmetic: 113 us -> none  [attend(): scores = scores + table[:, :, pos_index][:, None]]
    gather x2 -> x0, local copies, waits for them, and re-layouts: 51.1 us -> none  [attend(): scores = scores + table[:, :, pos_index][:, None]]
    all_gather x0 -> x1, blocking collectives: none -> 27.1 us  [per_device(): line = lax.all_gather(part, LINE)]
    pallas_call x0 -> x6, Pallas kernels: none -> 22.6 us  [call(): pl.pallas_call(kernel, out_shape=out_shape, scratch_shapes=list(scratch),...]
    all_to_all x0 -> x3, starting transfers between devices: none -> 20.6 us  [the longest x1 10.9 us: per_device(): lax.all_to_all(jnp.broadcast_to(total, (n_plane,) + total.shape), PLANE,...]
    ppermute x8 -> x6, waiting for transfers between devices: 3.6 us -> 14.7 us  [the longest x1 14.7 us: per_device(): out_diag = lax.ppermute(out_diag, AXES, route(1, 1))]
  transfers between devices with their start and end apart: 9 -> 9, of which waited for: 2 -> 2; matrix products, arithmetic and copies ran while one was open for 22% -> 2% of each run, Pallas kernels for 0% -> 11%
where the time goes in v1:
time: 152 us; the launch traced here: 151 us
  starting transfers between devices  65.2 us (43%)
  blocking collectives  27.1 us (18%)
  Pallas kernels  22.6 us (15%)
  waiting for transfers between devices  17.6 us (12%)
  local copies, waits for them, and re-layouts  16.7 us (11%)
    all_gather x1, blocking collectives, per_device(): line = lax.all_gather(part, LINE)  27.1 us
    pallas_call x6, Pallas kernels, call(): pl.pallas_call(kernel, out_shape=out_shape, scratch_shapes=list(scratch),...  22.6 us
    ppermute x1, starting transfers between devices, per_device(): lat = lax.ppermute(lat, AXES, route(-1, 0))  18.5 us
    unnamed x63, local copies, waits for them, and re-layouts  14.9 us
    ppermute x1, waiting for transfers between devices, per_device(): out_diag = lax.ppermute(out_diag, AXES, route(1, 1))  14.7 us
    all_to_all x1, starting transfers between devices, per_device(): lax.all_to_all(jnp.broadcast_to(total, (n_plane,) + total.shape), PLANE,...  10.9 us
    ppermute x1, starting transfers between devices, per_device(): out_lon = lax.ppermute(out_lon, AXES, route(0, 1))  9.22 us
    ppermute x1, starting transfers between devices, per_device(): diag = lax.ppermute(diag, AXES, route(-1, -1))  7.86 us
  transfers between devices with their start and end apart: 9, of which 2 were waited for; matrix products, arithmetic and copies ran while one was open for 2% of the time, Pallas kernels for 11%

profile of v1, /device:TPU:1, one launch (start us, length us, event | category | flops | bytes accessed | tf_op | source)
XLA Modules:
  0.0 150.7 jit_solution(9902228197912154867)
XLA Ops:
  0.6 0.9 copy-done
  1.5 0.9 copy-done.2
  2.5 18.5 %collective-permute-start = (bf16[2,2,3,24,192]{4,3,2,1,0:T(8,128)(2,1)S(1)}, bf16[2,2,3,24,192]{4,3,2,1,0:T(8,128)(2,1)S(1)}, u32[]{:S(2)}, u32[]{:S(2)}) collective-permute-start(bf16[2,2,3,24,192]{4,3,2,1,0:T(8,128)(2,1)S(1)} %get-tuple-element.29), channel_id=1, source_target_pairs={{0,508},{1,509},{2,510},{3,511},{4,0},{5,1},{6,2},{7,3},{8,4},{9,5... | collective-permute-start | bytes 331784 | tf_op jit(solution)/shard_map/ppermute | solution.py:372
  21.0 2.9 %collective-permute-start.1 = (bf16[2,2,3,8,192]{4,3,2,1,0:T(8,128)(2,1)S(1)}, bf16[2,2,3,8,192]{4,3,2,1,0:T(8,128)(2,1)S(1)}, u32[]{:S(2)}, u32[]{:S(2)}) collective-permute-start(bf16[2,2,3,8,192]{4,3,2,1,0:T(8,128)(2,1)S(1)} %get-tuple-element.30), channel_id=1, source_target_pairs={{0,3},{1,0},{2,1},{3,2},{4,7},{5,4},{6,5},{7,6},{8,11},{9,8},{10,9... | collective-permute-start | bytes 110600 | tf_op jit(solution)/shard_map/ppermute | solution.py:373
  23.9 7.9 %collective-permute-start.2 = (bf16[2,2,3,8,192]{4,3,2,1,0:T(8,128)(2,1)S(1)}, bf16[2,2,3,8,192]{4,3,2,1,0:T(8,128)(2,1)S(1)}, u32[]{:S(2)}, u32[]{:S(2)}) collective-permute-start(bf16[2,2,3,8,192]{4,3,2,1,0:T(8,128)(2,1)S(1)} %get-tuple-element.31), channel_id=1, source_target_pairs={{0,511},{1,508},{2,509},{3,510},{4,3},{5,0},{6,1},{7,2},{8,7},{9,4... | collective-permute-start | bytes 110600 | tf_op jit(solution)/shard_map/ppermute | solution.py:374
  32.4 0.9 copy.24.table
  33.4 0.9 copy-done.28
  34.3 8.5 %shard_map.155 = (f32[144,896]{1,0:T(8,128)S(1)}, s32[144,256]{1,0:T(8,128)S(1)}, s32[144,256]{1,0:T(8,128)S(1)}, bf16[3,192,192]{2,1,0:T(8,128)(2,1)S(1)}, bf16...) custom-call(s32[144,144]{1,0:T(8,128)S(1)} %copy-done.21, ...), custom_call_target="tpu_custom_call" | custom-call | flops 1000000000 | bytes 1000000 | tf_op jit(solution)/shard_map/pallas_call | solution.py:333
  46.8 0.9 copy-done.13
  47.7 0.9 copy-done.15
  48.6 0.8 copy-done.17
  49.4 0.8 copy-done.19
  50.2 5.6 %shard_map.156 = (bf16[288,192]{1,0:T(8,128)(2,1)S(1)}, bf16[288,192]{1,0:T(8,128)(2,1)S(1)}, bf16[2,144,192]{2,1,0:T(8,128)(2,1)S(1)}, bf16[2,48,192]{2,1,0:T(8...) custom-call(bf16[288,192]{1,0:T(8,128)(2,1)S(1)} %bitcast.15, ...), custom_call_target="tpu_custom_call" | custom-call | tf_op jit(solution)/shard_map/pallas_call | solution.py:333
  58.4 3.9 %all-to-all-start.1 = ((bf16[32,40,128]{2,1,0:T(8,128)(2,1)}), bf16[32,40,128]{2,1,0:T(8,128)(2,1)S(1)}, u32[]{:S(2)}, u32[]{:S(2)}) async-start(bf16[32,40,128]{2,1,0:T(8,128)(2,1)} %bitcast.11), calls=%async_computation.1 | async-start | bytes 655360 | tf_op jit(solution)/shard_map/all_to_all | solution.py:421
  62.3 6.8 %shard_map.157 = bf16[192,128]{1,0:T(8,128)(2,1)S(1)} custom-call(f32[144,896]{1,0:T(8,128)S(1)} %get-tuple-element.42.d_bias, s32[144,256]{1,0:T(8,128)S(1)} %copy-done.9, s32[144,256]{1,0:T(8,128)S(1)} %copy-done.11), custom_call_target="tpu_custom_call" | custom-call | tf_op jit(solution)/shard_map/pallas_call | solution.py:333
  69.1 2.9 %all-to-all-done.1 = bf16[32,40,128]{2,1,0:T(8,128)(2,1)S(1)} async-done(((bf16[32,40,128]{2,1,0:T(8,128)(2,1)}), bf16[32,40,128]{2,1,0:T(8,128)(2,1)S(1)}, u32[]{:S(2)}, u32[]{:S(2)}) %all-to-all-start.1) | async-done | bytes 327712 | tf_op jit(solution)/shard_map/all_to_all | solution.py:421
  72.7 5.8 %all-to-all-start = ((bf16[4,192,128]{2,1,0:T(8,128)(2,1)}), bf16[4,192,128]{2,1,0:T(8,128)(2,1)S(1)}, u32[]{:S(2)}, u32[]{:S(2)}) async-start(bf16[4,192,128]{2,1,0:T(8,128)(2,1)} %broadcast_in_dim.6), calls=%async_computation | async-start | bytes 393216 | tf_op jit(solution)/shard_map/all_to_all | solution.py:433
  78.5 27.1 %all-gather = bf16[640,128]{1,0:T(8,128)(2,1)S(1)} all-gather(bf16[40,128]{1,0:T(8,128)(2,1)S(1)} %reduce_sum.24), channel_id=2, replica_groups=mesh['x'=4,'zl'=8,'y'=4,'zh'=2,'c'=2] {'zh','zl'}, dimensions={0}, use_global_device_ids=true | all-gather | bytes 174080 | tf_op jit(solution)/shard_map/all_gather | solution.py:423
  106.4 10.9 %all-to-all-start.2 = ((bf16[32,40,128]{2,1,0:T(8,128)(2,1)}), bf16[32,40,128]{2,1,0:T(8,128)(2,1)S(1)}, u32[]{:S(2)}, u32[]{:S(2)}) async-start(bf16[32,40,128]{2,1,0:T(8,128)(2,1)} %broadcast_in_dim.7), calls=%async_computation.2 | async-start | bytes 655360 | tf_op jit(solution)/shard_map/all_to_all | solution.py:452
  117.4 3.3 %collective-permute-start.3 = (bf16[2,144,192]{2,1,0:T(8,128)(2,1)S(1)}, bf16[2,144,192]{2,1,0:T(8,128)(2,1)S(1)}, u32[]{:S(2)}, u32[]{:S(2)}) collective-permute-start(bf16[2,144,192]{2,1,0:T(8,128)(2,1)S(1)} %copy-done.23), channel_id=1, source_target_pairs={{0,4},{1,5},{2,6},{3,7},{4,8},{5,9},{6,10},{7,11},{8,12},{9,13},{1... | collective-permute-start | bytes 331784 | tf_op jit(solution)/shard_map/ppermute | solution.py:434
  120.7 9.2 %collective-permute-start.4 = (bf16[2,48,192]{2,1,0:T(8,128)(2,1)S(1)}, bf16[2,48,192]{2,1,0:T(8,128)(2,1)S(1)}, u32[]{:S(2)}, u32[]{:S(2)}) collective-permute-start(bf16[2,48,192]{2,1,0:T(8,128)(2,1)S(1)} %copy-done.27), channel_id=1, source_target_pairs={{0,1},{1,2},{2,3},{3,0},{4,5},{5,6},{6,7},{7,4},{8,9},{9,10},{10,1... | collective-permute-start | bytes 110600 | tf_op jit(solution)/shard_map/ppermute | solution.py:436
  129.9 2.8 %collective-permute-start.5 = (bf16[2,48,192]{2,1,0:T(8,128)(2,1)S(1)}, bf16[2,48,192]{2,1,0:T(8,128)(2,1)S(1)}, u32[]{:S(2)}, u32[]{:S(2)}) collective-permute-start(bf16[2,48,192]{2,1,0:T(8,128)(2,1)S(1)} %copy-done.25), channel_id=1, source_target_pairs={{0,5},{1,6},{2,7},{3,4},{4,9},{5,10},{6,11},{7,8},{8,13},{9,14},{1... | collective-permute-start | bytes 110600 | tf_op jit(solution)/shard_map/ppermute | solution.py:435
  132.8 14.7 %collective-permute-done.5 = bf16[2,48,192]{2,1,0:T(8,128)(2,1)S(1)} collective-permute-done((bf16[2,48,192]{2,1,0:T(8,128)(2,1)S(1)}, bf16[2,48,192]{2,1,0:T(8,128)(2,1)S(1)}, u32[]{:S(2)}, u32[]{:S(2)}) %collective-permute-start.5) | collective-permute-done | bytes 36896 | tf_op jit(solution)/shard_map/ppermute | solution.py:435
  148.9 0.9 shard_map.159
  (72 shorter events, 11.2 us)
Async XLA Ops:
  0.6 0.9 copy-start
  1.5 0.9 copy-start.2
  2.5 30.9 %copy-start.20 = (bf16[192,576]{1,0:T(8,128)(2,1)S(1)}, bf16[192,576]{1,0:T(8,128)(2,1)}, u32[]{:S(2)}) copy-start(bf16[192,576]{1,0:T(8,128)(2,1)} %w_qkv.1) | copy-start | bytes 663556
  2.5 30.9 %copy-start.21 = (s32[144,144]{1,0:T(8,128)S(1)}, s32[144,144]{1,0:T(8,128)}, u32[]{:S(2)}) copy-start(s32[144,144]{1,0:T(8,128)} %pos.1) | copy-start | bytes 248836
  2.5 44.3 %collective-permute-start = (bf16[2,2,3,24,192]{4,3,2,1,0:T(8,128)(2,1)S(1)}, bf16[2,2,3,24,192]{4,3,2,1,0:T(8,128)(2,1)S(1)}, u32[]{:S(2)}, u32[]{:S(2)}) collective-permute-start(bf16[2,2,3,24,192]{4,3,2,1,0:T(8,128)(2,1)S(1)} %get-tuple-element.29), channel_id=1, source_target_pairs={{0,508},{1,509},{2,510},{3,511},{4,0},{5,1},{6,2},{7,3},{8,4},{9,5... | collective-permute-start | bytes 331784 | tf_op jit(solution)/shard_map/ppermute | solution.py:372
  21.0 24.6 %collective-permute-start.1 = (bf16[2,2,3,8,192]{4,3,2,1,0:T(8,128)(2,1)S(1)}, bf16[2,2,3,8,192]{4,3,2,1,0:T(8,128)(2,1)S(1)}, u32[]{:S(2)}, u32[]{:S(2)}) collective-permute-start(bf16[2,2,3,8,192]{4,3,2,1,0:T(8,128)(2,1)S(1)} %get-tuple-element.30), channel_id=1, source_target_pairs={{0,3},{1,0},{2,1},{3,2},{4,7},{5,4},{6,5},{7,6},{8,11},{9,8},{10,9... | collective-permute-start | bytes 110600 | tf_op jit(solution)/shard_map/ppermute | solution.py:373
  23.8 9.5 %copy-start.12 = (bf16[192,192]{1,0:T(8,128)(2,1)S(1)}, bf16[192,192]{1,0:T(8,128)(2,1)}, u32[]{:S(2)}) copy-start(bf16[192,192]{1,0:T(8,128)(2,1)} %wp.1) | copy-start | bytes 221188
  23.9 22.3 %collective-permute-start.2 = (bf16[2,2,3,8,192]{4,3,2,1,0:T(8,128)(2,1)S(1)}, bf16[2,2,3,8,192]{4,3,2,1,0:T(8,128)(2,1)S(1)}, u32[]{:S(2)}, u32[]{:S(2)}) collective-permute-start(bf16[2,2,3,8,192]{4,3,2,1,0:T(8,128)(2,1)S(1)} %get-tuple-element.31), channel_id=1, source_target_pairs={{0,511},{1,508},{2,509},{3,510},{4,3},{5,0},{6,1},{7,2},{8,7},{9,4... | collective-permute-start | bytes 110600 | tf_op jit(solution)/shard_map/ppermute | solution.py:374
  34.3 12.5 %copy-start.1 = (bf16[2,6,24,192]{3,2,1,0:T(8,128)(2,1)S(1)}, bf16[2,6,24,192]{3,2,1,0:T(8,128)(2,1)}, u32[]{:S(2)}) copy-start(bf16[2,6,24,192]{3,2,1,0:T(8,128)(2,1)} %tokens.1) | copy-start | bytes 331780
  34.3 12.5 %copy-start.3 = (bf16[2,6,24,192]{3,2,1,0:T(8,128)(2,1)S(1)}, bf16[2,6,24,192]{3,2,1,0:T(8,128)(2,1)}, u32[]{:S(2)}) copy-start(bf16[2,6,24,192]{3,2,1,0:T(8,128)(2,1)} %d_out.1) | copy-start | bytes 331780
  34.3 12.5 %copy-start.4 = (bf16[2,528,144]{2,1,0:T(8,128)(2,1)S(1)}, bf16[2,528,144]{2,1,0:T(8,128)(2,1)}, u32[]{:S(2)}) copy-start(bf16[2,528,144]{2,1,0:T(8,128)(2,1)} %constant.11.clone.back) | copy-start | bytes 912388
  34.3 12.6 %copy-start.5 = (bf16[2,144,528]{2,1,0:T(8,128)(2,1)S(1)}, bf16[2,144,528]{2,1,0:T(8,128)(2,1)}, u32[]{:S(2)}) copy-start(bf16[2,144,528]{2,1,0:T(8,128)(2,1)} %constant.10.clone.pick) | copy-start | bytes 912388
  58.4 3.9 %copy-start.9 = (s32[144,256]{1,0:T(8,128)S(1)}, s32[144,256]{1,0:T(8,128)}, u32[]{:S(2)}) copy-start(s32[144,256]{1,0:T(8,128)} %copy-done.8) | copy-start | bytes 442372
  58.4 3.9 %copy-start.11 = (s32[144,256]{1,0:T(8,128)S(1)}, s32[144,256]{1,0:T(8,128)}, u32[]{:S(2)}) copy-start(s32[144,256]{1,0:T(8,128)} %copy-done.10) | copy-start | bytes 442372
  58.4 13.6 %all-to-all-start.1 = ((bf16[32,40,128]{2,1,0:T(8,128)(2,1)}), bf16[32,40,128]{2,1,0:T(8,128)(2,1)S(1)}, u32[]{:S(2)}, u32[]{:S(2)}) async-start(bf16[32,40,128]{2,1,0:T(8,128)(2,1)} %bitcast.11), calls=%async_computation.1 | async-start | bytes 655360 | tf_op jit(solution)/shard_map/all_to_all | solution.py:421
  72.7 33.0 %all-to-all-start = ((bf16[4,192,128]{2,1,0:T(8,128)(2,1)}), bf16[4,192,128]{2,1,0:T(8,128)(2,1)S(1)}, u32[]{:S(2)}, u32[]{:S(2)}) async-start(bf16[4,192,128]{2,1,0:T(8,128)(2,1)} %broadcast_in_dim.6), calls=%async_computation | async-start | bytes 393216 | tf_op jit(solution)/shard_map/all_to_all | solution.py:433
  106.4 10.9 %copy-start.23 = (bf16[2,144,192]{2,1,0:T(8,128)(2,1)S(1)}, bf16[2,144,192]{2,1,0:T(8,128)(2,1)}, u32[]{:S(2)}) copy-start(bf16[2,144,192]{2,1,0:T(8,128)(2,1)} %copy-done.22) | copy-start | bytes 331780
  106.4 14.3 %copy-start.27 = (bf16[2,48,192]{2,1,0:T(8,128)(2,1)S(1)}, bf16[2,48,192]{2,1,0:T(8,128)(2,1)}, u32[]{:S(2)}) copy-start(bf16[2,48,192]{2,1,0:T(8,128)(2,1)} %copy-done.26) | copy-start | bytes 110596
  106.4 23.5 %copy-start.25 = (bf16[2,48,192]{2,1,0:T(8,128)(2,1)S(1)}, bf16[2,48,192]{2,1,0:T(8,128)(2,1)}, u32[]{:S(2)}) copy-start(bf16[2,48,192]{2,1,0:T(8,128)(2,1)} %copy-done.24) | copy-start | bytes 110596
  106.4 41.0 %copy-start.7 = (bf16[288,192]{1,0:T(8,128)(2,1)S(1)}, bf16[288,192]{1,0:T(8,128)(2,1)}, u32[]{:S(2)}) copy-start(bf16[288,192]{1,0:T(8,128)(2,1)} %copy-done.6) | copy-start | bytes 331780
  106.4 42.5 %all-to-all-start.2 = ((bf16[32,40,128]{2,1,0:T(8,128)(2,1)}), bf16[32,40,128]{2,1,0:T(8,128)(2,1)S(1)}, u32[]{:S(2)}, u32[]{:S(2)}) async-start(bf16[32,40,128]{2,1,0:T(8,128)(2,1)} %broadcast_in_dim.7), calls=%async_computation.2 | async-start | bytes 655360 | tf_op jit(solution)/shard_map/all_to_all | solution.py:452
  117.4 30.1 %collective-permute-start.3 = (bf16[2,144,192]{2,1,0:T(8,128)(2,1)S(1)}, bf16[2,144,192]{2,1,0:T(8,128)(2,1)S(1)}, u32[]{:S(2)}, u32[]{:S(2)}) collective-permute-start(bf16[2,144,192]{2,1,0:T(8,128)(2,1)S(1)} %copy-done.23), channel_id=1, source_target_pairs={{0,4},{1,5},{2,6},{3,7},{4,8},{5,9},{6,10},{7,11},{8,12},{9,13},{1... | collective-permute-start | bytes 331784 | tf_op jit(solution)/shard_map/ppermute | solution.py:434
  120.7 12.1 %collective-permute-start.4 = (bf16[2,48,192]{2,1,0:T(8,128)(2,1)S(1)}, bf16[2,48,192]{2,1,0:T(8,128)(2,1)S(1)}, u32[]{:S(2)}, u32[]{:S(2)}) collective-permute-start(bf16[2,48,192]{2,1,0:T(8,128)(2,1)S(1)} %copy-done.27), channel_id=1, source_target_pairs={{0,1},{1,2},{2,3},{3,0},{4,5},{5,6},{6,7},{7,4},{8,9},{9,10},{10,1... | collective-permute-start | bytes 110600 | tf_op jit(solution)/shard_map/ppermute | solution.py:436
  129.9 17.5 %collective-permute-start.5 = (bf16[2,48,192]{2,1,0:T(8,128)(2,1)S(1)}, bf16[2,48,192]{2,1,0:T(8,128)(2,1)S(1)}, u32[]{:S(2)}, u32[]{:S(2)}) collective-permute-start(bf16[2,48,192]{2,1,0:T(8,128)(2,1)S(1)} %copy-done.25), channel_id=1, source_target_pairs={{0,5},{1,6},{2,7},{3,4},{4,9},{5,10},{6,11},{7,8},{8,13},{9,14},{1... | collective-permute-start | bytes 110600 | tf_op jit(solution)/shard_map/ppermute | solution.py:435
  (15 other events, 10.7 us)

commit v2 on v1

--- a/solution.py
+++ b/solution.py
@@ -32,7 +32,10 @@
 SCALE = HEAD**-0.5
 NEG = -1000000000.0
 G_ROWS = 1280
-VMEM_LIMIT = 48 * 1024 * 1024
+CUT = WPL * ROWS * HALF_LON
+EDGE_ROWS = 3 * CUT
+TAB_ROWS = 160
+MSG = EDGE_ROWS + TAB_ROWS
 
 SPLIT = (4, 8, 4, 2, 2)
 AXES = ("x", "zl", "y", "zh", "c")
@@ -66,13 +69,26 @@
     pick = np.zeros((WINDOWS, WIN, N_ALL), np.float32)
     for w in range(WINDOWS):
         pick[w, np.arange(WIN), at[w]] = 1.0
-    back = pick.transpose(0, 2, 1)
+    back = np.zeros((WINDOWS, N_OWN + N_LAT + CUT, WIN), np.float32)
+    back[:, : N_OWN + N_LAT] = pick.transpose(0, 2, 1)[:, : N_OWN + N_LAT]
+    place = np.zeros((N_OWN + N_LAT, CUT), np.float32)
+    for level in range(WPL):
+        for row in range(ROWS):
+            for col in range(HALF_LON):
+                edge = N_OWN + N_LAT + level * HALF_LAT * EDGE + (row % HALF_LAT) * EDGE + col
+                edge += 0 if row >= HALF_LAT else N_EDGE
+                to = level * ROWS * HALF_LON + row * HALF_LON + col
+                back[:, N_OWN + N_LAT + to] = pick[:, :, edge]
+                if row >= HALF_LAT:
+                    place[level * ROWS * COLS + row * COLS + col, to] = 1.0
+                else:
+                    place[N_OWN + level * HALF_LAT * COLS + row * COLS + col, to] = 1.0
     spread = np.zeros((256, WIN), np.float32)
     for lane in range(MAIN):
         spread[lane, lane] = 1.0
     for lane in range(HEADS * REST):
         spread[MAIN + lane, MAIN + lane % REST] = 1.0
-    return pick.astype(BF), back.astype(BF), spread.astype(BF)
+    return pick.astype(BF), back.astype(BF), spread.astype(BF), place.astype(BF)
 
 
 def dot(a, b, dims):
@@ -99,7 +115,7 @@
         lon[i] = ref[:, HALF_LAT:, :, :][:, :, :EDGE]
 
 
-def tables_kernel(pos, table, spread, w_qkv, w_proj, mask, bias, hi_out, lo_out, w3, w3t, wpt, blocked, lo_scr):
+def tables_kernel(pos, table, spread, w_qkv, w_proj, mask, gain, bias, hi_out, lo_out, w3, w3t, wpt, blocked, gain_out, scr):
     one = eye(WIN)
     idx = pos[...]
     hi = lax.shift_right_logical(idx, 7)
@@ -112,38 +128,53 @@
     hi_out[...] = hi2
     lo_out[...] = lo2
 
+    steps = []
+    for pair in range(HEADS // 2):
+        words = []
+        for head in (2 * pair, 2 * pair + 1):
+            row = table[head]
+            unit = jnp.maximum(jnp.max(jnp.abs(row), axis=1, keepdims=True), 1e-20) * (1.0 / 32767.0)
+            fixed = row * (1.0 / unit)
+            fixed = jnp.floor(jnp.clip(fixed + 0.5, -32767.0, 32767.0)).astype(jnp.int32)
+            steps.append(unit)
+            words.append(fixed)
+        scr[pair : pair + 1, :NPOS] = lax.shift_left(words[0], 16) | lax.bitwise_and(words[1], 65535)
+    scr[:, NPOS:] = jnp.zeros((HEADS // 2, HI * 128 - NPOS), jnp.int32)
+
+    def look(h_idx, l_idx):
+        acc = [[jnp.zeros((8, 128), jnp.int32) for _ in h_idx] for _ in range(HEADS // 2)]
+        for part in range(HI):
+            hit = [h == part for h in h_idx]
+            for pair in range(HEADS // 2):
+                row = jnp.broadcast_to(scr[pair : pair + 1, part * 128 : part * 128 + 128], (8, 128))
+                for i, l in enumerate(l_idx):
+                    got = jnp.take_along_axis(row, l, axis=1, mode="promise_in_bounds")
+                    acc[pair][i] = jnp.where(hit[i], got, acc[pair][i])
+        out = []
+        for pair in range(HEADS // 2):
+            high = [lax.shift_right_arithmetic(v, 16) for v in acc[pair]]
+            low = [lax.shift_right_arithmetic(lax.shift_left(v, 16), 16) for v in acc[pair]]
+            out.append([v.astype(F32) * steps[2 * pair] for v in high])
+            out.append([v.astype(F32) * steps[2 * pair + 1] for v in low])
+        return out
+
     def step(block, carry):
-        rows = pl.ds(pl.multiple_of(block * 8, 8), 8)
-        lane = lax.broadcasted_iota(jnp.int32, (8, 128), 1)
-        for tile in range(2):
-            cols = pl.ds(tile * 128, 128)
-            h_idx = hi_out[rows, cols]
-            l_idx = lo_out[rows, cols]
-            if tile == 0:
-                acc = [jnp.zeros((8, 128), F32) for _ in range(HEADS)]
-            else:
-                acc = [jnp.zeros((8, 128), F32)]
-            for part in range(HI):
-                width = min(128, NPOS - part * 128)
-                hit = h_idx == part
-                for head in range(HEADS):
-                    row = jnp.broadcast_to(lo_scr[head : head + 1, pl.ds(part * 128, 128)], (8, 128))
-                    got = jnp.take_along_axis(row, l_idx, axis=1, mode="promise_in_bounds")
-                    if tile == 0:
-                        acc[head] = jnp.where(hit, got, acc[head])
-                    else:
-                        mine = hit & (lax.shift_right_logical(lane, 4) == head)
-                        acc[0] = jnp.where(mine, got, acc[0])
-            if tile == 0:
-                for head in range(HEADS):
-                    bias[rows, pl.ds(head * MAIN, 128)] = acc[head]
-            else:
-                bias[rows, pl.ds(HEADS * MAIN, 128)] = acc[0]
+        rows = [pl.ds(pl.multiple_of(block * 24 + 8 * i, 8), 8) for i in range(3)]
+        acc = look([hi_out[r, :128] for r in rows], [lo_out[r, :128] for r in rows])
+        for head in range(HEADS):
+            for i, r in enumerate(rows):
+                bias[r, MAIN * head : MAIN * (head + 1)] = acc[head][i]
         return carry
 
-    lo_scr[:, : HI * 128] = jnp.zeros((HEADS, HI * 128), F32)
-    lo_scr[:, :NPOS] = table[0]
-    lax.fori_loop(0, WIN // 8, step, 0)
+    lax.fori_loop(0, WIN // 24, step, 0)
+    pad = jnp.zeros((REST, 256 - WIN), jnp.int32)
+    h_rest = jnp.concatenate([hi[MAIN:], pad], axis=1)
+    l_rest = jnp.concatenate([lo[MAIN:], pad], axis=1)
+    tiles = [(slice(8 * i, 8 * i + 8), slice(128 * j, 128 * j + 128)) for i in range(2) for j in range(2)]
+    acc = look([h_rest[t] for t in tiles], [l_rest[t] for t in tiles])
+    rest = [jnp.concatenate([jnp.concatenate(a[2 * i : 2 * i + 2], axis=1) for i in range(2)], axis=0) for a in acc]
+    rest = jnp.concatenate(rest + [jnp.zeros((128 - HEADS * REST, 256), F32)], axis=0)
+    bias[:, HEADS * MAIN :] = rest.T[:WIN]
 
     one = eye(C)
     for i in range(3):
@@ -151,8 +182,10 @@
         w3[i] = w
         w3t[i] = nt(one, w).astype(BF)
     wpt[...] = nt(one, w_proj[...]).astype(BF)
-
-    lab = mask[...].astype(F32).reshape(WPL * ROWS, COLS).astype(BF)
+    gain_out[...] = jnp.sum(one.astype(F32) * gain[...], axis=1, keepdims=True)
+
+    lab = [mask[row, level : level + 1, :].astype(F32) for level in range(WPL) for row in range(ROWS)]
+    lab = jnp.concatenate(lab, axis=0).astype(BF)
     for w in range(WINDOWS):
         lane = lax.broadcasted_iota(jnp.int32, (COLS, WIN), 1)
         col = lax.broadcasted_iota(jnp.int32, (COLS, WIN), 0)
@@ -194,7 +227,7 @@
 
 def block_kernel(
     own_x, own_d, lat, lon, diag, pick, back, gain, w3, w3t, wp, wpt, bias, blocked,
-    base_x, base_d, out_lat, out_lon, out_diag, grads, d_bias,
+    base_x, base_d, out_lat, out_edge, grads, d_bias,
 ):
     x_all = jnp.concatenate([own_x[...], lat[0], lon[0], diag[0]], axis=0)
     d_all = jnp.concatenate([own_d[...], lat[1], lon[1], diag[1]], axis=0)
@@ -203,8 +236,8 @@
     g = gain[...]
     sums = [jnp.zeros((C, C), F32) for _ in range(4)]
     d_gain = jnp.zeros((C, 1), F32)
-    x_back = jnp.zeros((N_ALL, C), F32)
-    d_back = jnp.zeros((N_ALL, C), F32)
+    x_back = jnp.zeros((N_OWN + N_LAT + CUT, C), F32)
+    d_back = jnp.zeros((N_OWN + N_LAT + CUT, C), F32)
     for w in range(WINDOWS):
         x = nn(pick[w], x_all).astype(BF)
         d_proj = nn(pick[w], d_all).astype(BF)
@@ -259,18 +292,18 @@
     for i in range(2):
         pair = jnp.concatenate([sums[2 * i][:, 128:], sums[2 * i + 1][:, 128:]], axis=1)
         grads[C * (4 + i) : C * (5 + i), :] = pair.astype(BF)
-    lane = lax.broadcasted_iota(jnp.int32, (128, 128), 1)
-    tail = jnp.concatenate([d_gain[128:], jnp.zeros((256 - C, 1), F32)], axis=0)
-    both = jnp.where(lane == 0, d_gain[:128], jnp.where(lane == 1, tail, 0.0))
-    grads[6 * C :, :] = both.astype(BF)
+    row = jnp.sum(eye_c.astype(F32) * d_gain, axis=0, keepdims=True)
+    tail = jnp.concatenate([row[:, 128:], jnp.zeros((1, 256 - C), F32)], axis=1)
+    grads[6 * C :, :] = jnp.concatenate([row[:, :128], tail, jnp.zeros((126, 128), F32)], axis=0).astype(BF)
     for i, (total, own, base) in enumerate(((x_back, own_x, base_x), (d_back, own_d, base_d))):
         base[...] = (own[...].astype(F32) + total[:N_OWN]).astype(BF)
         out_lat[i] = total[N_OWN : N_OWN + N_LAT].astype(BF)
-        out_lon[i] = total[N_OWN + N_LAT : N_OWN + N_LAT + N_EDGE].astype(BF)
-        out_diag[i] = total[N_OWN + N_LAT + N_EDGE :].astype(BF)
-
-
-def scatter_kernel(d_bias, hi, lo, out, acc):
+    edge = jnp.concatenate([x_back[N_OWN + N_LAT :], d_back[N_OWN + N_LAT :]], axis=0)
+    out_edge[: 2 * CUT, :] = edge[:, :128].astype(BF)
+    out_edge[2 * CUT :, :] = jnp.concatenate([edge[:CUT, 128:], edge[CUT:, 128:]], axis=1).astype(BF)
+
+
+def scatter_kernel(d_bias, hi, lo, edge, out, acc):
     acc[...] = jnp.zeros_like(acc)
 
     def step(block, carry):
@@ -298,22 +331,37 @@
         return carry
 
     lax.fori_loop(0, WIN // 8, step, 0)
-    out[...] = acc[...].astype(BF)
-
-
-def finish_kernel(base_x, base_d, lat, lon, diag, tabs, out_x, out_d, out_t):
+    out[:EDGE_ROWS, :] = edge[...].astype(F32).astype(BF)
+    rows = [acc[HIP * h : HIP * h + HI] for h in range(HEADS)] + [jnp.zeros((TAB_ROWS - HEADS * HI, 128), F32)]
+    out[EDGE_ROWS:, :] = jnp.concatenate(rows, axis=0).astype(BF)
+
+
+def pair_kernel(own, near, out):
+    out[...] = jnp.concatenate(
+        [own[:EDGE_ROWS, :].astype(F32), own[EDGE_ROWS:, :].astype(F32) + near[EDGE_ROWS:, :].astype(F32)], axis=0
+    ).astype(BF)
+
+
+def middle_kernel(core, pair, near, far, base_x, base_d, lat, place, out_x, out_d, out_lat, out_t):
+    from_near = jnp.broadcast_to(core[...], (EDGE_ROWS, 128)) == 1
+    edge = jnp.where(from_near, near[:EDGE_ROWS, :].astype(F32), far[:EDGE_ROWS, :].astype(F32))
     for i, (base, out) in enumerate(((base_x, out_x), (base_d, out_d))):
-        a = base[...].astype(F32)
-        edge = jnp.concatenate([diag[i].astype(F32), lon[i].astype(F32)], axis=1)
-        pad = jnp.zeros((WPL, ROWS, COLS - EDGE, C), F32)
-        far = jnp.concatenate([lat[i].astype(F32), jnp.zeros((WPL, HALF_LAT, COLS, C), F32)], axis=1)
-        out[...] = (a + jnp.concatenate([edge, pad], axis=2) + far).astype(BF)
-    t = jnp.sum(tabs[...].astype(F32), axis=0)
+        wide = jnp.concatenate([edge[CUT * i : CUT * (i + 1)], edge[2 * CUT :, 64 * i : 64 * (i + 1)]], axis=1)
+        add = nn(place[...], wide.astype(BF))
+        out[...] = (base[...].astype(F32) + add[:N_OWN]).astype(BF)
+        out_lat[i] = (lat[i].astype(F32) + add[N_OWN:]).astype(BF)
+    t = pair[EDGE_ROWS:, :].astype(F32) + far[EDGE_ROWS:, :].astype(F32)
     for part in range(HI):
         width = min(128, NPOS - part * 128)
         for head in range(HEADS):
-            row = head * HIP + part
-            out_t[0, head : head + 1, part * 128 : part * 128 + width] = t[row : row + 1, :width]
+            row = head * HI + part
+            out_t[head, :, part * 128 : part * 128 + width] = t[row : row + 1, :width]
+
+
+def finish_kernel(base_x, base_d, lat, out_x, out_d):
+    for i, (base, out) in enumerate(((base_x, out_x), (base_d, out_d))):
+        out[:, HALF_LAT:] = base[:, HALF_LAT:]
+        out[:, :HALF_LAT] = (base[:, :HALF_LAT].astype(F32) + lat[i].astype(F32)).astype(BF)
 
 
 def unpack_kernel(g, scale, qkv, proj, gain):
@@ -326,15 +374,17 @@
     qkv[:, 512:576] = full[5][:, :64]
     proj[:, 0:128] = full[3]
     proj[:, 128:192] = full[5][:, 64:]
-    gain[...] = g[6 * C :, :].astype(F32) * k
-
-
-def call(kernel, out_shape, *args, scratch=(), cost=(0, 0)):
+    tail = g[6 * C : 6 * C + 16, :].astype(F32) * k
+    gain[:, :128] = tail[0:1]
+    gain[:, 128:] = tail[1:2, : C - 128]
+
+
+def call(kernel, out_shape, *args, scratch=(), cost=(0, 0), vmem=60):
     return pl.pallas_call(
         kernel,
         out_shape=out_shape,
         scratch_shapes=list(scratch),
-        compiler_params=pltpu.CompilerParams(vmem_limit_bytes=VMEM_LIMIT),
+        compiler_params=pltpu.CompilerParams(vmem_limit_bytes=vmem * 2**20),
         cost_estimate=pl.CostEstimate(flops=cost[0], bytes_accessed=cost[1], transcendentals=0),
     )(*args)
 
@@ -357,8 +407,16 @@
             for b in range(n_lon)
         ]
 
+    def hop(to):
+        return [
+            (a * n_lon + zh * sizes[4] + c, a * n_lon + to(zh, c)[0] * sizes[4] + to(zh, c)[1])
+            for a in range(n_lat)
+            for zh in range(sizes[3])
+            for c in range(sizes[4])
+        ]
+
     def per_device(tokens, mask_ids, pos_index, norm_gain, w_qkv, w_proj, earth_bias, d_out):
-        pick, back, spread = (jnp.asarray(c) for c in constants())
+        pick, back, spread, place = (jnp.asarray(c) for c in constants())
         lat, lon, diag = call(
             cut_kernel,
             (
@@ -372,7 +430,7 @@
         lat = lax.ppermute(lat, AXES, route(-1, 0))
         lon = lax.ppermute(lon, AXES, route(0, -1))
         diag = lax.ppermute(diag, AXES, route(-1, -1))
-        bias, hi, lo, w3, w3t, wpt, blocked = call(
+        bias, hi, lo, w3, w3t, wpt, blocked, gain_col = call(
             tables_kernel,
             (
                 sds((WIN, PAIRS), F32),
@@ -382,24 +440,25 @@
                 sds((3, C, C), BF),
                 sds((C, C), BF),
                 sds((WINDOWS, WIN, 256), F32),
+                sds((C, 1), F32),
             ),
             pos_index,
-            earth_bias,
+            earth_bias.transpose(1, 0, 2),
             spread,
             w_qkv,
             w_proj,
-            mask_ids,
-            scratch=[pltpu.VMEM((HEADS, HI * 128), F32)],
-            cost=(10**9, 10**6),
-        )
-        base_x, base_d, out_lat, out_lon, out_diag, grads, d_bias = call(
+            mask_ids.transpose(1, 0, 2),
+            norm_gain.reshape(1, C),
+            scratch=[pltpu.VMEM((HEADS // 2, HI * 128), jnp.int32)],
+            cost=(6 * 10**9, 10**6),
+        )
+        base_x, base_d, out_lat, out_edge, grads, d_bias = call(
             block_kernel,
             (
                 sds((N_OWN, C), BF),
                 sds((N_OWN, C), BF),
                 sds((2, N_LAT, C), BF),
-                sds((2, N_EDGE, C), BF),
-                sds((2, N_EDGE, C), BF),
+                sds((EDGE_ROWS, 128), BF),
                 sds((G_ROWS, 128), BF),
                 sds((WIN, PAIRS), F32),
             ),
@@ -410,54 +469,71 @@
             diag.reshape(2, N_EDGE, C),
             pick,
             back,
-            norm_gain.reshape(C, 1),
+            gain_col,
             w3,
             w3t,
             w_proj,
             wpt,
             bias,
             blocked,
+            cost=(6 * 10**9, 10**6),
         )
         parts = lax.all_to_all(grads.reshape(n_plane, piece, 128), PLANE, 0, 0)
-        part = jnp.sum(parts.astype(F32), axis=0).astype(BF)
-        line = lax.all_gather(part, LINE)
-
-        table = call(
+        own = call(
             scatter_kernel,
-            sds((HEADS * HIP, 128), BF),
+            sds((MSG, 128), BF),
             d_bias,
             hi,
             lo,
+            out_edge,
             scratch=[pltpu.VMEM((HEADS * HIP, 128), F32)],
-        )
-        tabs = lax.all_to_all(jnp.broadcast_to(table, (n_lon,) + table.shape), LON_AXES, 0, 0)
+            cost=(8 * 10**9, 10**6),
+        )
+        parts, own = lax.optimization_barrier((parts, own))
+        near = lax.ppermute(own, AXES, hop(lambda zh, c: (zh, 1 - c)))
+        part = jnp.sum(parts.astype(F32), axis=0).astype(BF)
+        line = lax.all_to_all(jnp.broadcast_to(part, (n_line,) + part.shape), LINE, 0, 0)
+        pair = call(pair_kernel, sds((MSG, 128), BF), own, near)
+        far = lax.ppermute(pair, AXES, hop(lambda zh, c: (1 - zh, 1 - c)))
+        line, pair = lax.optimization_barrier((line, pair))
+        total = jnp.sum(line.astype(F32), axis=0).astype(BF)
+        whole = lax.all_to_all(jnp.broadcast_to(total, (n_plane,) + total.shape), PLANE, 0, 0)
+        core = jnp.full((1, 128), lax.axis_index("c"), jnp.int32)
+        base_x, base_d, out_lat, d_table = call(
+            middle_kernel,
+            (
+                sds((N_OWN, C), BF),
+                sds((N_OWN, C), BF),
+                sds((2, N_LAT, C), BF),
+                sds((HEADS, 1, NPOS), F32),
+            ),
+            core,
+            pair,
+            near,
+            far,
+            base_x,
+            base_d,
+            out_lat,
+            place,
+            cost=(20 * 10**9, 10**6),
+        )
         out_lat = lax.ppermute(out_lat, AXES, route(1, 0))
-        out_diag = lax.ppermute(out_diag, AXES, route(1, 1))
-        out_lon = lax.ppermute(out_lon, AXES, route(0, 1))
-        updated, d_tokens, d_table = call(
+        scale = float(n_lat * n_lon * N_OWN) ** -0.5
+        qkv, proj, gain = call(
+            lambda g, a, b, c: unpack_kernel(g, scale, a, b, c),
+            (sds((C, 3 * C), F32), sds((C, C), F32), sds((1, C), F32)),
+            whole.reshape(G_ROWS, 128),
+        )
+        base_x, qkv = lax.optimization_barrier((base_x, qkv))
+        updated, d_tokens = call(
             finish_kernel,
-            (
-                sds((WPL, ROWS, COLS, C), BF),
-                sds((WPL, ROWS, COLS, C), BF),
-                sds((1, HEADS, NPOS), F32),
-            ),
+            (sds((WPL, ROWS, COLS, C), BF), sds((WPL, ROWS, COLS, C), BF)),
             base_x.reshape(WPL, ROWS, COLS, C),
             base_d.reshape(WPL, ROWS, COLS, C),
             out_lat.reshape(2, WPL, HALF_LAT, COLS, C),
-            out_lon.reshape(2, WPL, HALF_LAT, EDGE, C),
-            out_diag.reshape(2, WPL, HALF_LAT, EDGE, C),
-            tabs,
-        )
-        total = jnp.sum(line.astype(F32), axis=0).astype(BF)
-        whole = lax.all_to_all(jnp.broadcast_to(total, (n_plane,) + total.shape), PLANE, 0, 0)
-        scale = float(n_lat * n_lon * N_OWN) ** -0.5
-        qkv, proj, gain = call(
-            lambda g, a, b, c: unpack_kernel(g, scale, a, b, c),
-            (sds((C, 3 * C), F32), sds((C, C), F32), sds((128, 128), F32)),
-            whole.reshape(G_ROWS, 128),
-        )
-        gain = jnp.concatenate([gain[:, 0], gain[: C - 128, 1]])
-        return updated, d_tokens, qkv, proj, gain, d_table
+            cost=(20 * 10**9, 10**6),
+        )
+        return updated, d_tokens, qkv, proj, gain.reshape(C), d_table.transpose(1, 0, 2)
 
     return per_device
 

time: 152 us -> 117 us (0.77)
  blocking collectives: 27.1 us -> 0 us
  local copies, waits for them, and re-layouts: 16.7 us -> 4.79 us
  Pallas kernels: 22.6 us -> 33.3 us
  waiting for transfers between devices: 17.6 us -> 13.2 us
    all_gather x1 -> x0, blocking collectives: 27.1 us -> none  [per_device(): line = lax.all_gather(part, LINE)]
    ppermute x2, waiting for transfers between devices: 14.7 us -> 0.99 us  [the longest x1 0.99 us: per_device(): near = lax.ppermute(own, AXES, hop(lambda zh, c: (zh, 1 - c)))]
    unnamed x63 -> x16, local copies, waits for them, and re-layouts: 14.9 us -> 2.8 us
    pallas_call x6 -> x8, Pallas kernels: 22.6 us -> 33.3 us  [call(): pl.pallas_call(kernel, out_shape=out_shape, scratch_shapes=list(scratch),...]
    ppermute x1, waiting for transfers between devices: 0.01 us -> 7.54 us  [per_device(): out_lat = lax.ppermute(out_lat, AXES, route(1, 0))]
    all_to_all x1, starting transfers between devices: 10.9 us -> 6.45 us  [per_device(): lax.all_to_all(jnp.broadcast_to(total, (n_plane,) + total.shape), PLANE,...]
    all_to_all x1, waiting for transfers between devices: 0.01 us -> 3.44 us  [per_device(): lax.all_to_all(jnp.broadcast_to(total, (n_plane,) + total.shape), PLANE,...]
    ppermute x2, starting transfers between devices: 12 us -> 14.6 us  [the longest x1 12.4 us: per_device(): far = lax.ppermute(pair, AXES, hop(lambda zh, c: (1 - zh, 1 - c)))]
  transfers between devices with their start and end apart: 9 -> 9, of which waited for: 2 -> 5; matrix products, arithmetic and copies ran while one was open for 2% -> 1% of each run, Pallas kernels for 11% -> 19%
where the time goes in v2:
time: 117 us; the launch traced here: 116 us
  starting transfers between devices  63.8 us (55%)
  Pallas kernels  33.3 us (28%)
  waiting for transfers between devices  13.2 us (11%)
  local copies, waits for them, and re-layouts  4.79 us (4%)
    pallas_call x8, Pallas kernels, call(): pl.pallas_call(kernel, out_shape=out_shape, scratch_shapes=list(scratch),...  33.3 us
    ppermute x1, starting transfers between devices, per_device(): lat = lax.ppermute(lat, AXES, route(-1, 0))  18.3 us
    ppermute x1, starting transfers between devices, per_device(): far = lax.ppermute(pair, AXES, hop(lambda zh, c: (1 - zh, 1 - c)))  12.4 us
    ppermute x1, starting transfers between devices, per_device(): diag = lax.ppermute(diag, AXES, route(-1, -1))  7.73 us
    ppermute x1, waiting for transfers between devices, per_device(): out_lat = lax.ppermute(out_lat, AXES, route(1, 0))  7.54 us
    all_to_all x1, starting transfers between devices, per_device(): lax.all_to_all(jnp.broadcast_to(part, (n_line,) + part.shape), LINE, 0, 0)  6.83 us
    all_to_all x1, starting transfers between devices, per_device(): lax.all_to_all(jnp.broadcast_to(total, (n_plane,) + total.shape), PLANE,...  6.45 us
    all_to_all x1, starting transfers between devices, per_device(): parts = lax.all_to_all(grads.reshape(n_plane, piece, 128), PLANE, 0, 0)  3.66 us
  transfers between devices with their start and end apart: 9, of which 5 were waited for; matrix products, arithmetic and copies ran while one was open for 1% of the time, Pallas kernels for 19%

profile of v2, /device:TPU:1, one launch (start us, length us, event | category | flops | bytes accessed | tf_op | source)
XLA Modules:
  0.0 115.9 jit_solution(13949235023456663203)
XLA Ops:
  0.6 1.7 %shard_map.163 = (bf16[2,2,3,24,192]{4,3,2,1,0:T(8,128)(2,1)}, bf16[2,2,3,8,192]{4,3,2,1,0:T(8,128)(2,1)}, bf16[2,2,3,8,192]{4,3,2,1,0:T(8,128)(2,1)}) custom-call(bf16[2,6,24,192]{3,2,1,0:T(8,128)(2,1)} %tokens.1, bf16[2,6,24,192]{3,2,1,0:T(8,128)(2,1)} %d_out.1), custom_call_target="tpu_custom_call" | custom-call | tf_op jit(solution)/shard_map/pallas_call | solution.py:383
  2.3 18.3 %collective-permute-start = (bf16[2,2,3,24,192]{4,3,2,1,0:T(8,128)(2,1)}, bf16[2,2,3,24,192]{4,3,2,1,0:T(8,128)(2,1)S(1)}, u32[]{:S(2)}, u32[]{:S(2)}) collective-permute-start(bf16[2,2,3,24,192]{4,3,2,1,0:T(8,128)(2,1)} %get-tuple-element.38), channel_id=1, source_target_pairs={{0,508},{1,509},{2,510},{3,511},{4,0},{5,1},{6,2},{7,3},{8,4},{9,5... | collective-permute-start | bytes 331784 | tf_op jit(solution)/shard_map/ppermute | solution.py:430
  20.7 2.9 %collective-permute-start.1 = (bf16[2,2,3,8,192]{4,3,2,1,0:T(8,128)(2,1)}, bf16[2,2,3,8,192]{4,3,2,1,0:T(8,128)(2,1)S(1)}, u32[]{:S(2)}, u32[]{:S(2)}) collective-permute-start(bf16[2,2,3,8,192]{4,3,2,1,0:T(8,128)(2,1)} %get-tuple-element.39), channel_id=1, source_target_pairs={{0,3},{1,0},{2,1},{3,2},{4,7},{5,4},{6,5},{7,6},{8,11},{9,8},{10,9... | collective-permute-start | bytes 110600 | tf_op jit(solution)/shard_map/ppermute | solution.py:431
  23.5 7.7 %collective-permute-start.2 = (bf16[2,2,3,8,192]{4,3,2,1,0:T(8,128)(2,1)}, bf16[2,2,3,8,192]{4,3,2,1,0:T(8,128)(2,1)S(1)}, u32[]{:S(2)}, u32[]{:S(2)}) collective-permute-start(bf16[2,2,3,8,192]{4,3,2,1,0:T(8,128)(2,1)} %get-tuple-element.40), channel_id=1, source_target_pairs={{0,511},{1,508},{2,509},{3,510},{4,3},{5,0},{6,1},{7,2},{8,7},{9,4... | collective-permute-start | bytes 110600 | tf_op jit(solution)/shard_map/ppermute | solution.py:432
  31.3 7.7 %shard_map.164 = (f32[144,896]{1,0:T(8,128)}, s32[144,256]{1,0:T(8,128)}, s32[144,256]{1,0:T(8,128)}, bf16[3,192,192]{2,1,0:T(8,128)(2,1)}, bf16[3,192,192]{2,1,...) custom-call(s32[144,144]{1,0:T(8,128)} %pos.1, f32[6,1,3312]{2,1,0:T(1,128)} %bitcast.21, ...), custom_call_target="tpu_custom_call" | custom-call | flops 6000000000 | bytes 1000000 | tf_op jit(solution)/shard_map/pallas_call | solution.py:383
  40.0 7.8 %shard_map.165 = (bf16[288,192]{1,0:T(8,128)(2,1)}, bf16[288,192]{1,0:T(8,128)(2,1)}, bf16[2,144,192]{2,1,0:T(8,128)(2,1)}, bf16[216,128]{1,0:T(8,128)(2,1)}, bf...) custom-call(bf16[288,192]{1,0:T(8,128)(2,1)} %bitcast.17, bf16[288,192]{1,0:T(8,128)(2,1)} %bitcast.18, ...), custom_call_target="tpu_custom_call" | custom-call | flops 6000000000 | bytes 1000000 | tf_op jit(solution)/shard_map/pallas_call | solution.py:383
  47.8 3.7 %all-to-all-start = ((bf16[32,40,128]{2,1,0:T(8,128)(2,1)}), bf16[32,40,128]{2,1,0:T(8,128)(2,1)S(1)}, u32[]{:S(2)}, u32[]{:S(2)}) async-start(bf16[32,40,128]{2,1,0:T(8,128)(2,1)} %bitcast.16), calls=%async_computation | async-start | bytes 655360 | tf_op jit(solution)/shard_map/all_to_all | solution.py:481
  51.4 8.5 %shard_map.166.own = bf16[376,128]{1,0:T(8,128)(2,1)} custom-call(f32[144,896]{1,0:T(8,128)} %get-tuple-element.48.d_bias, s32[144,256]{1,0:T(8,128)} %get-tuple-element.49.hi, s32[144,256]{1,0:T(8,128)} %get-tuple-element.50.lo, bf16[216,128]{1,0:T(8,128)(2,1)} %get-tuple-element.51.edge), custom_call_target="tpu_custom_call" | custom-call | flops 8000000000 | bytes 1000000 | tf_op jit(solution)/shard_map/pallas_call | solution.py:383
  60.0 0.9 all-to-all-done
  60.9 0.7 broadcast_in_dim.10
  61.6 6.8 %all-to-all-start.1 = ((bf16[16,40,128]{2,1,0:T(8,128)(2,1)}), bf16[16,40,128]{2,1,0:T(8,128)(2,1)S(1)}, u32[]{:S(2)}, u32[]{:S(2)}) async-start(bf16[16,40,128]{2,1,0:T(8,128)(2,1)} %broadcast_in_dim.10), calls=%async_computation.1 | async-start | bytes 327680 | tf_op jit(solution)/shard_map/all_to_all | solution.py:495
  68.5 2.2 %collective-permute-start.3 = (bf16[376,128]{1,0:T(8,128)(2,1)S(1)}, bf16[376,128]{1,0:T(8,128)(2,1)S(1)}, u32[]{:S(2)}, u32[]{:S(2)}) collective-permute-start(bf16[376,128]{1,0:T(8,128)(2,1)S(1)} %copy-done.2), channel_id=1, source_target_pairs={{0,1},{1,0},{2,3},{3,2},{4,5},{5,4},{6,7},{7,6},{8,9},{9,8},{10,11... | collective-permute-start | bytes 288776 | tf_op jit(solution)/shard_map/ppermute | solution.py:493
  70.7 1.0 collective-permute-done.3.near
  72.3 1.6 %shard_map.167.pair = bf16[376,128]{1,0:T(8,128)(2,1)} custom-call(bf16[376,128]{1,0:T(8,128)(2,1)} %shard_map.166.own, bf16[376,128]{1,0:T(8,128)(2,1)} %copy-done.1), custom_call_target="tpu_custom_call" | custom-call | tf_op jit(solution)/shard_map/pallas_call | solution.py:383
  73.9 12.4 %collective-permute-start.4 = (bf16[376,128]{1,0:T(8,128)(2,1)}, bf16[376,128]{1,0:T(8,128)(2,1)S(1)}, u32[]{:S(2)}, u32[]{:S(2)}) collective-permute-start(bf16[376,128]{1,0:T(8,128)(2,1)} %shard_map.167.pair), channel_id=1, source_target_pairs={{0,3},{1,2},{2,1},{3,0},{4,7},{5,6},{6,5},{7,4},{8,11},{9,10},{10,... | collective-permute-start | bytes 288776 | tf_op jit(solution)/shard_map/ppermute | solution.py:497
  86.4 0.8 broadcast_in_dim.11
  87.2 6.4 %all-to-all-start.2 = ((bf16[32,40,128]{2,1,0:T(8,128)(2,1)}), bf16[32,40,128]{2,1,0:T(8,128)(2,1)S(1)}, u32[]{:S(2)}, u32[]{:S(2)}) async-start(bf16[32,40,128]{2,1,0:T(8,128)(2,1)} %broadcast_in_dim.11), calls=%async_computation.2 | async-start | bytes 655360 | tf_op jit(solution)/shard_map/all_to_all | solution.py:500
  94.3 2.3 %shard_map.168 = (bf16[288,192]{1,0:T(8,128)(2,1)}, bf16[288,192]{1,0:T(8,128)(2,1)}, bf16[2,144,192]{2,1,0:T(8,128)(2,1)}, f32[6,1,3312]{2,1,0:T(1,128)}) custom-call(s32[1,128]{1,0:T(1,128)} %broadcast_in_dim.9.core, bf16[376,128]{1,0:T(8,128)(2,1)} %shard_map.167.pair, bf16[376,128]{1,0:T(8,128)(2,1)} %copy-done.1, bf16[376,128]{1,0:T(8,128)(2,1)} %copy-done.5, ...), custom_call_target="tpu_custom_call" | custom-call | flops 20000000000 | bytes 1000000 | tf_op jit(solution)/shard_map/pallas_call | solution.py:383
  96.6 3.3 %collective-permute-start.5 = (bf16[2,144,192]{2,1,0:T(8,128)(2,1)}, bf16[2,144,192]{2,1,0:T(8,128)(2,1)S(1)}, u32[]{:S(2)}, u32[]{:S(2)}) collective-permute-start(bf16[2,144,192]{2,1,0:T(8,128)(2,1)} %get-tuple-element.63), channel_id=1, source_target_pairs={{0,4},{1,5},{2,6},{3,7},{4,8},{5,9},{6,10},{7,11},{8,12},{9,13},{1... | collective-permute-start | bytes 331784 | tf_op jit(solution)/shard_map/ppermute | solution.py:520
  99.8 3.4 %all-to-all-done.2 = bf16[32,40,128]{2,1,0:T(8,128)(2,1)S(1)} async-done(((bf16[32,40,128]{2,1,0:T(8,128)(2,1)}), bf16[32,40,128]{2,1,0:T(8,128)(2,1)S(1)}, u32[]{:S(2)}, u32[]{:S(2)}) %all-to-all-start.2) | async-done | bytes 327712 | tf_op jit(solution)/shard_map/all_to_all | solution.py:500
  103.3 0.7 copy-done
  104.0 1.9 %shard_map.169 = (f32[192,576]{1,0:T(8,128)}, f32[192,192]{1,0:T(8,128)}, f32[1,192]{1,0:T(1,128)}) custom-call(bf16[1280,128]{1,0:T(8,128)(2,1)} %bitcast.15), custom_call_target="tpu_custom_call" | custom-call | tf_op jit(solution)/shard_map/pallas_call | solution.py:383
  105.9 7.5 %collective-permute-done.5 = bf16[2,144,192]{2,1,0:T(8,128)(2,1)S(1)} collective-permute-done((bf16[2,144,192]{2,1,0:T(8,128)(2,1)}, bf16[2,144,192]{2,1,0:T(8,128)(2,1)S(1)}, u32[]{:S(2)}, u32[]{:S(2)}) %collective-permute-start.5) | collective-permute-done | bytes 110624 | tf_op jit(solution)/shard_map/ppermute | solution.py:520
  114.1 1.8 %shard_map.170 = (bf16[2,6,24,192]{3,2,1,0:T(8,128)(2,1)}, bf16[2,6,24,192]{3,2,1,0:T(8,128)(2,1)}) custom-call(bf16[2,6,24,192]{3,2,1,0:T(8,128)(2,1)} %bitcast.27, bf16[2,6,24,192]{3,2,1,0:T(8,128)(2,1)} %bitcast.28, bf16[2,2,3,24,192]{4,3,2,1,0:T(8,128)(2,1)} %bitcast.20), custom_call_target="tpu_custom_call" | custom-call | flops 20000000000 | bytes 1000000 | tf_op jit(solution)/shard_map/pallas_call | solution.py:383
  (23 shorter events, 3.0 us)
Async XLA Ops:
  2.3 37.0 %collective-permute-start = (bf16[2,2,3,24,192]{4,3,2,1,0:T(8,128)(2,1)}, bf16[2,2,3,24,192]{4,3,2,1,0:T(8,128)(2,1)S(1)}, u32[]{:S(2)}, u32[]{:S(2)}) collective-permute-start(bf16[2,2,3,24,192]{4,3,2,1,0:T(8,128)(2,1)} %get-tuple-element.38), channel_id=1, source_target_pairs={{0,508},{1,509},{2,510},{3,511},{4,0},{5,1},{6,2},{7,3},{8,4},{9,5... | collective-permute-start | bytes 331784 | tf_op jit(solution)/shard_map/ppermute | solution.py:430
  20.7 18.3 %collective-permute-start.1 = (bf16[2,2,3,8,192]{4,3,2,1,0:T(8,128)(2,1)}, bf16[2,2,3,8,192]{4,3,2,1,0:T(8,128)(2,1)S(1)}, u32[]{:S(2)}, u32[]{:S(2)}) collective-permute-start(bf16[2,2,3,8,192]{4,3,2,1,0:T(8,128)(2,1)} %get-tuple-element.39), channel_id=1, source_target_pairs={{0,3},{1,0},{2,1},{3,2},{4,7},{5,4},{6,5},{7,6},{8,11},{9,8},{10,9... | collective-permute-start | bytes 110600 | tf_op jit(solution)/shard_map/ppermute | solution.py:431
  23.5 15.8 %collective-permute-start.2 = (bf16[2,2,3,8,192]{4,3,2,1,0:T(8,128)(2,1)}, bf16[2,2,3,8,192]{4,3,2,1,0:T(8,128)(2,1)S(1)}, u32[]{:S(2)}, u32[]{:S(2)}) collective-permute-start(bf16[2,2,3,8,192]{4,3,2,1,0:T(8,128)(2,1)} %get-tuple-element.40), channel_id=1, source_target_pairs={{0,511},{1,508},{2,509},{3,510},{4,3},{5,0},{6,1},{7,2},{8,7},{9,4... | collective-permute-start | bytes 110600 | tf_op jit(solution)/shard_map/ppermute | solution.py:432
  39.0 0.6 copy-start.6
  39.3 0.6 copy-start.7
  39.4 0.7 copy-start.3
  47.8 13.1 %all-to-all-start = ((bf16[32,40,128]{2,1,0:T(8,128)(2,1)}), bf16[32,40,128]{2,1,0:T(8,128)(2,1)S(1)}, u32[]{:S(2)}, u32[]{:S(2)}) async-start(bf16[32,40,128]{2,1,0:T(8,128)(2,1)} %bitcast.16), calls=%async_computation | async-start | bytes 655360 | tf_op jit(solution)/shard_map/all_to_all | solution.py:481
  61.6 6.8 %copy-start.2 = (bf16[376,128]{1,0:T(8,128)(2,1)S(1)}, bf16[376,128]{1,0:T(8,128)(2,1)}, u32[]{:S(2)}) copy-start(bf16[376,128]{1,0:T(8,128)(2,1)} %shard_map.166.own) | copy-start | bytes 288772
  61.6 24.7 %all-to-all-start.1 = ((bf16[16,40,128]{2,1,0:T(8,128)(2,1)}), bf16[16,40,128]{2,1,0:T(8,128)(2,1)S(1)}, u32[]{:S(2)}, u32[]{:S(2)}) async-start(bf16[16,40,128]{2,1,0:T(8,128)(2,1)} %broadcast_in_dim.10), calls=%async_computation.1 | async-start | bytes 327680 | tf_op jit(solution)/shard_map/all_to_all | solution.py:495
  68.5 3.2 %collective-permute-start.3 = (bf16[376,128]{1,0:T(8,128)(2,1)S(1)}, bf16[376,128]{1,0:T(8,128)(2,1)S(1)}, u32[]{:S(2)}, u32[]{:S(2)}) collective-permute-start(bf16[376,128]{1,0:T(8,128)(2,1)S(1)} %copy-done.2), channel_id=1, source_target_pairs={{0,1},{1,0},{2,3},{3,2},{4,5},{5,4},{6,7},{7,6},{8,9},{9,8},{10,11... | collective-permute-start | bytes 288776 | tf_op jit(solution)/shard_map/ppermute | solution.py:493
  71.7 0.6 copy-start.1
  73.9 19.7 %collective-permute-start.4 = (bf16[376,128]{1,0:T(8,128)(2,1)}, bf16[376,128]{1,0:T(8,128)(2,1)S(1)}, u32[]{:S(2)}, u32[]{:S(2)}) collective-permute-start(bf16[376,128]{1,0:T(8,128)(2,1)} %shard_map.167.pair), channel_id=1, source_target_pairs={{0,3},{1,2},{2,1},{3,0},{4,7},{5,6},{6,5},{7,4},{8,11},{9,10},{10,... | collective-permute-start | bytes 288776 | tf_op jit(solution)/shard_map/ppermute | solution.py:497
  87.2 16.1 %all-to-all-start.2 = ((bf16[32,40,128]{2,1,0:T(8,128)(2,1)}), bf16[32,40,128]{2,1,0:T(8,128)(2,1)S(1)}, u32[]{:S(2)}, u32[]{:S(2)}) async-start(bf16[32,40,128]{2,1,0:T(8,128)(2,1)} %broadcast_in_dim.11), calls=%async_computation.2 | async-start | bytes 655360 | tf_op jit(solution)/shard_map/all_to_all | solution.py:500
  93.6 0.6 copy-start.5
  96.6 16.9 %collective-permute-start.5 = (bf16[2,144,192]{2,1,0:T(8,128)(2,1)}, bf16[2,144,192]{2,1,0:T(8,128)(2,1)S(1)}, u32[]{:S(2)}, u32[]{:S(2)}) collective-permute-start(bf16[2,144,192]{2,1,0:T(8,128)(2,1)} %get-tuple-element.63), channel_id=1, source_target_pairs={{0,4},{1,5},{2,6},{3,7},{4,8},{5,9},{6,10},{7,11},{8,12},{9,13},{1... | collective-permute-start | bytes 331784 | tf_op jit(solution)/shard_map/ppermute | solution.py:520
  103.3 0.7 copy-start
  113.5 0.6 copy-start.4

commit v3 on v2

--- a/solution.py
+++ b/solution.py
@@ -33,9 +33,13 @@
 NEG = -1000000000.0
 G_ROWS = 1280
 CUT = WPL * ROWS * HALF_LON
-EDGE_ROWS = 3 * CUT
+EDGE_ROWS = 3 * CUT + 8
 TAB_ROWS = 160
 MSG = EDGE_ROWS + TAB_ROWS
+LAT_ROWS = 3 * N_LAT
+CORNER_ROWS = 3 * N_EDGE
+SIDE_ROWS = 2 * CORNER_ROWS
+LINE_ROWS = 2 * LAT_ROWS + CORNER_ROWS
 
 SPLIT = (4, 8, 4, 2, 2)
 AXES = ("x", "zl", "y", "zh", "c")
@@ -43,6 +47,9 @@
 LON_AXES = ("zh", "c")
 PLANE = ("x", "y", "c")
 LINE = ("zh", "zl")
+
+
+N_BACK = N_OWN + 2 * N_LAT + CUT
 
 
 def source_rows():
@@ -69,7 +76,7 @@
     pick = np.zeros((WINDOWS, WIN, N_ALL), np.float32)
     for w in range(WINDOWS):
         pick[w, np.arange(WIN), at[w]] = 1.0
-    back = np.zeros((WINDOWS, N_OWN + N_LAT + CUT, WIN), np.float32)
+    back = np.zeros((WINDOWS, N_BACK, WIN), np.float32)
     back[:, : N_OWN + N_LAT] = pick.transpose(0, 2, 1)[:, : N_OWN + N_LAT]
     place = np.zeros((N_OWN + N_LAT, CUT), np.float32)
     for level in range(WPL):
@@ -82,13 +89,10 @@
                 if row >= HALF_LAT:
                     place[level * ROWS * COLS + row * COLS + col, to] = 1.0
                 else:
-                    place[N_OWN + level * HALF_LAT * COLS + row * COLS + col, to] = 1.0
-    spread = np.zeros((256, WIN), np.float32)
-    for lane in range(MAIN):
-        spread[lane, lane] = 1.0
-    for lane in range(HEADS * REST):
-        spread[MAIN + lane, MAIN + lane % REST] = 1.0
-    return pick.astype(BF), back.astype(BF), spread.astype(BF), place.astype(BF)
+                    at_lat = level * HALF_LAT * COLS + row * COLS + col
+                    place[N_OWN + at_lat, to] = 1.0
+                    back[:, N_OWN + N_LAT + CUT + at_lat] = pick[:, :, edge]
+    return pick.astype(BF), back.astype(BF), place.astype(BF)
 
 
 def dot(a, b, dims):
@@ -107,20 +111,62 @@
     return (lax.broadcasted_iota(jnp.int32, (n, n), 0) == lax.broadcasted_iota(jnp.int32, (n, n), 1)).astype(F32).astype(BF)
 
 
-def cut_kernel(tokens, d_out, lat, lon, diag):
-    for i, ref in enumerate((tokens, d_out)):
-        top = ref[:, :HALF_LAT]
-        lat[i] = top
-        diag[i] = top[:, :, :EDGE]
-        lon[i] = ref[:, HALF_LAT:, :, :][:, :, :EDGE]
-
-
-def tables_kernel(pos, table, spread, w_qkv, w_proj, mask, gain, bias, hi_out, lo_out, w3, w3t, wpt, blocked, gain_out, scr):
+def spread():
+    lane = lax.broadcasted_iota(jnp.int32, (256, WIN), 0)
+    query = lax.broadcasted_iota(jnp.int32, (256, WIN), 1)
+    held = jnp.where(lane < MAIN, lane, MAIN + lax.bitwise_and(lane, REST - 1))
+    return ((held == query) & (lane < MAIN + HEADS * REST)).astype(F32).astype(BF)
+
+
+def fold(a, b):
+    return jnp.concatenate([a[:, :128], b[:, :128], jnp.concatenate([a[:, 128:], b[:, 128:]], axis=1)], axis=0)
+
+
+def unfold(both, n):
+    return [
+        jnp.concatenate([both[n * i : n * (i + 1)], both[2 * n : 3 * n, 64 * i : 64 * (i + 1)]], axis=1) for i in range(2)
+    ]
+
+
+def core_is(core, rows):
+    return lax.broadcasted_iota(jnp.int32, (rows, 128), 0) * 0 + lax.axis_index("c") == core
+
+
+def band_is(first, rows):
+    at = lax.axis_index("zl") * lax.axis_size("y") + lax.axis_index("y")
+    want = 0 if first else lax.axis_size("zl") * lax.axis_size("y") - 1
+    return lax.broadcasted_iota(jnp.int32, (rows, 128), 0) * 0 + at == want
+
+
+def cut_kernel(tokens, d_out, to_core, lat, edge):
+    both = (tokens[...].astype(F32), d_out[...].astype(F32))
+    top = fold(*(a[:, :HALF_LAT].reshape(N_LAT, C) for a in both))
+    corner = fold(*(a[:, :HALF_LAT, :EDGE].reshape(N_EDGE, C) for a in both))
+    lon = fold(*(a[:, HALF_LAT:, :EDGE].reshape(N_EDGE, C) for a in both))
+    side = jnp.concatenate([corner, lon], axis=0)
+    lat[...] = top.astype(BF)
+    edge[...] = side.astype(BF)
+    spare = jnp.zeros((LAT_ROWS - SIDE_ROWS, 128), F32)
+    to_core[...] = jnp.where(core_is(1, LAT_ROWS), jnp.concatenate([side, spare], axis=0), top).astype(BF)
+
+
+def join_kernel(lat, edge, sibling, to_lon, to_lat, to_line):
+    corner = edge[:CORNER_ROWS, :]
+    to_lon[...] = edge[...]
+    to_lat[:LAT_ROWS, :] = lat[...]
+    theirs = sibling[:CORNER_ROWS, :].astype(F32)
+    to_lat[LAT_ROWS:, :] = jnp.where(band_is(True, CORNER_ROWS), corner.astype(F32), theirs).astype(BF)
+    to_line[:LAT_ROWS, :] = lat[...]
+    to_line[LAT_ROWS : 2 * LAT_ROWS, :] = sibling[...]
+    to_line[2 * LAT_ROWS :, :] = corner
+
+
+def tables_kernel(pos, table, bias, hi_out, lo_out, scr):
     one = eye(WIN)
     idx = pos[...]
     hi = lax.shift_right_logical(idx, 7)
     lo = lax.bitwise_and(idx, 127)
-    sp = spread[...]
+    sp = spread()
     hi2 = nt(nt(one, hi.astype(F32).astype(BF)).astype(BF), sp)
     lo2 = nt(nt(one, lo.astype(F32).astype(BF)).astype(BF), sp)
     hi2 = hi2.astype(jnp.int32)
@@ -176,29 +222,6 @@
     rest = jnp.concatenate(rest + [jnp.zeros((128 - HEADS * REST, 256), F32)], axis=0)
     bias[:, HEADS * MAIN :] = rest.T[:WIN]
 
-    one = eye(C)
-    for i in range(3):
-        w = w_qkv[:, C * i : C * (i + 1)]
-        w3[i] = w
-        w3t[i] = nt(one, w).astype(BF)
-    wpt[...] = nt(one, w_proj[...]).astype(BF)
-    gain_out[...] = jnp.sum(one.astype(F32) * gain[...], axis=1, keepdims=True)
-
-    lab = [mask[row, level : level + 1, :].astype(F32) for level in range(WPL) for row in range(ROWS)]
-    lab = jnp.concatenate(lab, axis=0).astype(BF)
-    for w in range(WINDOWS):
-        lane = lax.broadcasted_iota(jnp.int32, (COLS, WIN), 1)
-        col = lax.broadcasted_iota(jnp.int32, (COLS, WIN), 0)
-        across = (lax.rem(lane, WLON) + w * WLON == col).astype(F32).astype(BF)
-        wide = nn(lab, across)
-        r = lax.broadcasted_iota(jnp.int32, (WPL * ROWS, WIN), 0)
-        a = lax.broadcasted_iota(jnp.int32, (WPL * ROWS, WIN), 1)
-        row = jnp.sum(jnp.where(lax.div(a, WLON) == r, wide, 0.0), axis=0, keepdims=True)
-        row = jnp.broadcast_to(row, (WIN, WIN)).astype(BF)
-        down = nt(eye(WIN), row)
-        over = nt(row, sp)
-        blocked[w] = jnp.where(over == jnp.broadcast_to(down[:, :1], (WIN, 256)), 0.0, NEG)
-
 
 def by_head(x):
     lane = lax.broadcasted_iota(jnp.int32, (1, C), 1)
@@ -225,19 +248,53 @@
     return jnp.concatenate([main, rest], axis=1)
 
 
+def regions(mask):
+    sp = spread()
+    out = []
+    lab = [mask[row, level : level + 1, :].astype(F32) for level in range(WPL) for row in range(ROWS)]
+    lab = jnp.concatenate(lab, axis=0).astype(BF)
+    for w in range(WINDOWS):
+        lane = lax.broadcasted_iota(jnp.int32, (COLS, WIN), 1)
+        col = lax.broadcasted_iota(jnp.int32, (COLS, WIN), 0)
+        across = (lax.rem(lane, WLON) + w * WLON == col).astype(F32).astype(BF)
+        wide = nn(lab, across)
+        r = lax.broadcasted_iota(jnp.int32, (WPL * ROWS, WIN), 0)
+        a = lax.broadcasted_iota(jnp.int32, (WPL * ROWS, WIN), 1)
+        row = jnp.sum(jnp.where(lax.div(a, WLON) == r, wide, 0.0), axis=0, keepdims=True)
+        row = jnp.broadcast_to(row, (WIN, WIN)).astype(BF)
+        down = nt(eye(WIN), row)
+        over = nt(row, sp)
+        out.append(jnp.where(over == jnp.broadcast_to(down[:, :1], (WIN, 256)), 0.0, NEG))
+    return out
+
+
 def block_kernel(
-    own_x, own_d, lat, lon, diag, pick, back, gain, w3, w3t, wp, wpt, bias, blocked,
-    base_x, base_d, out_lat, out_edge, grads, d_bias,
+    own_x, own_d, sibling, from_lon, from_lat, from_line, from_side, from_corner, pick, back, gain, w_qkv, wp, mask, bias,
+    base_x, base_d, out_lat, out_corner, out_edge, grads, d_bias,
 ):
-    x_all = jnp.concatenate([own_x[...], lat[0], lon[0], diag[0]], axis=0)
-    d_all = jnp.concatenate([own_d[...], lat[1], lon[1], diag[1]], axis=0)
+    f32 = lambda ref, start, size: ref[start : start + size, :].astype(F32)
+    over = f32(from_line, 0, LAT_ROWS) + f32(from_side, LAT_ROWS, LAT_ROWS)
+    lat = unfold(jnp.where(band_is(False, LAT_ROWS), over, f32(from_lat, 0, LAT_ROWS)), N_LAT)
+    lon = f32(sibling, CORNER_ROWS, CORNER_ROWS), f32(from_lon, CORNER_ROWS, CORNER_ROWS)
+    lon = unfold(jnp.where(core_is(0, CORNER_ROWS), *lon), N_EDGE)
+    direct = core_is(0, CORNER_ROWS) != band_is(False, CORNER_ROWS)
+    diag = f32(from_side, 2 * LAT_ROWS, CORNER_ROWS) + f32(from_corner, 0, CORNER_ROWS)
+    diag = unfold(jnp.where(direct, f32(from_lat, LAT_ROWS, CORNER_ROWS), diag), N_EDGE)
+    x_all, d_all = (
+        jnp.concatenate([own[...], lat[i].astype(BF), lon[i].astype(BF), diag[i].astype(BF)], axis=0)
+        for i, own in enumerate((own_x, own_d))
+    )
     eye_c = eye(C)
     eye_w = eye(WIN)
-    g = gain[...]
+    g = jnp.sum(eye_c.astype(F32) * gain[...], axis=1, keepdims=True)
+    w3 = [w_qkv[:, C * i : C * (i + 1)] for i in range(3)]
+    w3t = [None] + [nt(eye_c, w).astype(BF) for w in w3[1:]]
+    wpt = nt(eye_c, wp[...]).astype(BF)
+    blocked = regions(mask)
     sums = [jnp.zeros((C, C), F32) for _ in range(4)]
     d_gain = jnp.zeros((C, 1), F32)
-    x_back = jnp.zeros((N_OWN + N_LAT + CUT, C), F32)
-    d_back = jnp.zeros((N_OWN + N_LAT + CUT, C), F32)
+    x_back = jnp.zeros((N_BACK, C), F32)
+    d_back = jnp.zeros((N_BACK, C), F32)
     for w in range(WINDOWS):
         x = nn(pick[w], x_all).astype(BF)
         d_proj = nn(pick[w], d_all).astype(BF)
@@ -256,7 +313,7 @@
         vt = nn(w3t[2], nt_w).astype(BF)
         qm = by_head(q)
         dm = by_head(nt(d_proj, wp[...]).astype(BF))
-        far = jnp.concatenate([blocked[w, :, :MAIN]] * HEADS + [blocked[w, :, MAIN:]], axis=1)
+        far = jnp.concatenate([blocked[w][:, :MAIN]] * HEADS + [blocked[w][:, MAIN:]], axis=1)
         s = nt(k, qm) * SCALE + bias[...] + far
         e = jnp.exp(s - jnp.max(s, axis=0, keepdims=True))
         p = e * (1.0 / jnp.sum(e, axis=0, keepdims=True))
@@ -273,7 +330,7 @@
         dq_t = heads_apart(kt, dsb, SCALE)
         dk = (nn(dsb, qm) * SCALE).astype(BF)
         dv = nn(attn, dm).astype(BF)
-        proj_t = nn(wpt[...], mixed_t).astype(BF)
+        proj_t = nn(wpt, mixed_t).astype(BF)
         x_back = x_back + nt(back[w], proj_t)
         sums[0] = sums[0] + nt(nt_w, dq_t)
         sums[1] = sums[1] + nn(nt_w, dk)
@@ -297,13 +354,16 @@
     grads[6 * C :, :] = jnp.concatenate([row[:, :128], tail, jnp.zeros((126, 128), F32)], axis=0).astype(BF)
     for i, (total, own, base) in enumerate(((x_back, own_x, base_x), (d_back, own_d, base_d))):
         base[...] = (own[...].astype(F32) + total[:N_OWN]).astype(BF)
-        out_lat[i] = total[N_OWN : N_OWN + N_LAT].astype(BF)
-    edge = jnp.concatenate([x_back[N_OWN + N_LAT :], d_back[N_OWN + N_LAT :]], axis=0)
-    out_edge[: 2 * CUT, :] = edge[:, :128].astype(BF)
-    out_edge[2 * CUT :, :] = jnp.concatenate([edge[:CUT, 128:], edge[CUT:, 128:]], axis=1).astype(BF)
-
-
-def scatter_kernel(d_bias, hi, lo, edge, out, acc):
+    parts = ((out_lat, N_OWN, N_LAT), (out_edge, N_OWN + N_LAT, CUT), (out_corner, N_OWN + N_LAT + CUT, N_LAT))
+    for out, start, size in parts:
+        both = fold(x_back[start : start + size], d_back[start : start + size])
+        spare = out.shape[0] - both.shape[0]
+        if spare:
+            both = jnp.concatenate([both, jnp.zeros((spare, 128), F32)], axis=0)
+        out[...] = both.astype(BF)
+
+
+def scatter_kernel(d_bias, hi, lo, edge, lat, out, acc):
     acc[...] = jnp.zeros_like(acc)
 
     def step(block, carry):
@@ -331,37 +391,51 @@
         return carry
 
     lax.fori_loop(0, WIN // 8, step, 0)
-    out[:EDGE_ROWS, :] = edge[...].astype(F32).astype(BF)
+    out[:EDGE_ROWS, :] = edge[...]
     rows = [acc[HIP * h : HIP * h + HI] for h in range(HEADS)] + [jnp.zeros((TAB_ROWS - HEADS * HI, 128), F32)]
-    out[EDGE_ROWS:, :] = jnp.concatenate(rows, axis=0).astype(BF)
-
-
-def pair_kernel(own, near, out):
-    out[...] = jnp.concatenate(
-        [own[:EDGE_ROWS, :].astype(F32), own[EDGE_ROWS:, :].astype(F32) + near[EDGE_ROWS:, :].astype(F32)], axis=0
-    ).astype(BF)
-
-
-def middle_kernel(core, pair, near, far, base_x, base_d, lat, place, out_x, out_d, out_lat, out_t):
-    from_near = jnp.broadcast_to(core[...], (EDGE_ROWS, 128)) == 1
-    edge = jnp.where(from_near, near[:EDGE_ROWS, :].astype(F32), far[:EDGE_ROWS, :].astype(F32))
-    for i, (base, out) in enumerate(((base_x, out_x), (base_d, out_d))):
-        wide = jnp.concatenate([edge[CUT * i : CUT * (i + 1)], edge[2 * CUT :, 64 * i : 64 * (i + 1)]], axis=1)
-        add = nn(place[...], wide.astype(BF))
+    out[EDGE_ROWS:MSG, :] = jnp.concatenate(rows, axis=0).astype(BF)
+    out[MSG:, :] = lat[...]
+
+
+def pair_kernel(own, near, lat, corner, out, across):
+    out[:EDGE_ROWS, :] = own[:EDGE_ROWS, :]
+    out[EDGE_ROWS:, :] = (own[EDGE_ROWS:MSG, :].astype(F32) + near[EDGE_ROWS:MSG, :].astype(F32)).astype(BF)
+    across[:LAT_ROWS, :] = lat[...]
+    across[LAT_ROWS:, :] = (near[MSG:, :].astype(F32) + corner[...].astype(F32)).astype(BF)
+
+
+def total_kernel(parts, out):
+    total = parts[0].astype(F32)
+    for i in range(1, parts.shape[0]):
+        total = total + parts[i].astype(F32)
+    total = total.astype(BF)
+    for i in range(out.shape[0]):
+        out[i] = total
+
+
+def middle_kernel(pair, near, far, base_x, base_d, lat, corner, across, place, out_x, out_d, out_lat, out_near):
+    edge = jnp.where(core_is(1, 3 * CUT), near[: 3 * CUT, :].astype(F32), far[: 3 * CUT, :].astype(F32))
+    adds = [nn(place[...], e.astype(BF)) for e in unfold(edge, CUT)]
+    for add, base, out in ((adds[0], base_x, out_x), (adds[1], base_d, out_d)):
         out[...] = (base[...].astype(F32) + add[:N_OWN]).astype(BF)
-        out_lat[i] = (lat[i].astype(F32) + add[N_OWN:]).astype(BF)
-    t = pair[EDGE_ROWS:, :].astype(F32) + far[EDGE_ROWS:, :].astype(F32)
+    whole = lat[...].astype(F32) + fold(adds[0][N_OWN:], adds[1][N_OWN:])
+    out_lat[...] = jnp.where(band_is(False, LAT_ROWS), corner[...].astype(F32), whole).astype(BF)
+    out_near[:LAT_ROWS, :] = across[LAT_ROWS:, :]
+    out_near[LAT_ROWS:, :] = (pair[EDGE_ROWS:, :].astype(F32) + far[EDGE_ROWS:, :].astype(F32)).astype(BF)
+
+
+def finish_kernel(base_x, base_d, lat, across, near, own, out_x, out_d, out_t):
+    got = lat[...].astype(F32) + across[:LAT_ROWS, :].astype(F32) + near[:LAT_ROWS, :].astype(F32)
+    for add, base, out in zip(unfold(got, N_LAT), (base_x, base_d), (out_x, out_d)):
+        out[:, HALF_LAT:] = base[:, HALF_LAT:]
+        add = add.reshape(WPL, HALF_LAT, COLS, C)
+        out[:, :HALF_LAT] = (base[:, :HALF_LAT].astype(F32) + add).astype(BF)
+    t = jnp.where(core_is(1, TAB_ROWS), near[LAT_ROWS:, :].astype(F32), own[LAT_ROWS:, :].astype(F32))
     for part in range(HI):
         width = min(128, NPOS - part * 128)
         for head in range(HEADS):
             row = head * HI + part
             out_t[head, :, part * 128 : part * 128 + width] = t[row : row + 1, :width]
-
-
-def finish_kernel(base_x, base_d, lat, out_x, out_d):
-    for i, (base, out) in enumerate(((base_x, out_x), (base_d, out_d))):
-        out[:, HALF_LAT:] = base[:, HALF_LAT:]
-        out[:, :HALF_LAT] = (base[:, :HALF_LAT].astype(F32) + lat[i].astype(F32)).astype(BF)
 
 
 def unpack_kernel(g, scale, qkv, proj, gain):
@@ -379,7 +453,7 @@
     gain[:, 128:] = tail[1:2, : C - 128]
 
 
-def call(kernel, out_shape, *args, scratch=(), cost=(0, 0), vmem=60):
+def call(kernel, out_shape, *args, scratch=(), cost=(0, 0), vmem=8):
     return pl.pallas_call(
         kernel,
         out_shape=out_shape,
@@ -399,6 +473,7 @@
     n_plane = sizes[0] * sizes[2] * sizes[4]
     n_line = sizes[1] * sizes[3]
     piece = G_ROWS // n_plane
+    band = sizes[1] * sizes[2]
 
     def route(d_lat, d_lon):
         return [
@@ -407,117 +482,134 @@
             for b in range(n_lon)
         ]
 
-    def hop(to):
+    def first(pair):
+        return pair[0] // n_lon % band == 0
+
+    def last(pair):
+        return pair[0] // n_lon % band == band - 1
+
+    def hop(to, cores):
         return [
             (a * n_lon + zh * sizes[4] + c, a * n_lon + to(zh, c)[0] * sizes[4] + to(zh, c)[1])
             for a in range(n_lat)
             for zh in range(sizes[3])
-            for c in range(sizes[4])
+            for c in cores
         ]
 
     def per_device(tokens, mask_ids, pos_index, norm_gain, w_qkv, w_proj, earth_bias, d_out):
-        pick, back, spread, place = (jnp.asarray(c) for c in constants())
-        lat, lon, diag = call(
+        pick, back, place = (jnp.asarray(c) for c in constants())
+        to_core, lat, edge = call(
             cut_kernel,
-            (
-                sds((2, WPL, HALF_LAT, COLS, C), BF),
-                sds((2, WPL, HALF_LAT, EDGE, C), BF),
-                sds((2, WPL, HALF_LAT, EDGE, C), BF),
-            ),
+            (sds((LAT_ROWS, 128), BF), sds((LAT_ROWS, 128), BF), sds((SIDE_ROWS, 128), BF)),
             tokens,
             d_out,
         )
-        lat = lax.ppermute(lat, AXES, route(-1, 0))
-        lon = lax.ppermute(lon, AXES, route(0, -1))
-        diag = lax.ppermute(diag, AXES, route(-1, -1))
-        bias, hi, lo, w3, w3t, wpt, blocked, gain_col = call(
+        sibling = lax.ppermute(to_core, AXES, hop(lambda zh, c: (zh, 1 - c), (0, 1)))
+        to_lon, to_lat, to_line = call(
+            join_kernel,
+            (sds((SIDE_ROWS, 128), BF), sds((LAT_ROWS + CORNER_ROWS, 128), BF), sds((LINE_ROWS, 128), BF)),
+            lat,
+            edge,
+            sibling,
+        )
+        south = route(-1, 0)
+        from_lon = lax.ppermute(to_lon, AXES, hop(lambda zh, c: (1 - zh, 1), (0,)))
+        corners = [r for r in route(-1, -1) if first(r) and r[0] % sizes[4] == 0]
+        from_lat = lax.ppermute(to_lat, AXES, [r for r in south if not first(r)] + corners)
+        from_line = lax.ppermute(to_line, AXES, [r for r in south if first(r) and r[0] % sizes[4] == 1])
+        bias, hi, lo = call(
             tables_kernel,
-            (
-                sds((WIN, PAIRS), F32),
-                sds((WIN, 256), jnp.int32),
-                sds((WIN, 256), jnp.int32),
-                sds((3, C, C), BF),
-                sds((3, C, C), BF),
-                sds((C, C), BF),
-                sds((WINDOWS, WIN, 256), F32),
-                sds((C, 1), F32),
-            ),
+            (sds((WIN, PAIRS), F32), sds((WIN, 256), jnp.int32), sds((WIN, 256), jnp.int32)),
             pos_index,
             earth_bias.transpose(1, 0, 2),
-            spread,
-            w_qkv,
-            w_proj,
-            mask_ids.transpose(1, 0, 2),
-            norm_gain.reshape(1, C),
             scratch=[pltpu.VMEM((HEADS // 2, HI * 128), jnp.int32)],
             cost=(6 * 10**9, 10**6),
         )
-        base_x, base_d, out_lat, out_edge, grads, d_bias = call(
+        from_lon, from_lat, bias = lax.optimization_barrier((from_lon, from_lat, bias))
+        from_corner = lax.ppermute(from_lon, AXES, [r for r in south if not first(r) and r[0] % sizes[4] == 1])
+        from_line, from_corner = lax.optimization_barrier((from_line, from_corner))
+        from_side = lax.ppermute(from_line, AXES, [r for r in hop(lambda zh, c: (zh, 0), (1,)) if last(r)])
+        base_x, base_d, out_lat, out_corner, out_edge, grads, d_bias = call(
             block_kernel,
             (
                 sds((N_OWN, C), BF),
                 sds((N_OWN, C), BF),
-                sds((2, N_LAT, C), BF),
+                sds((LAT_ROWS, 128), BF),
+                sds((LAT_ROWS, 128), BF),
                 sds((EDGE_ROWS, 128), BF),
                 sds((G_ROWS, 128), BF),
                 sds((WIN, PAIRS), F32),
             ),
             tokens.reshape(N_OWN, C),
             d_out.reshape(N_OWN, C),
-            lat.reshape(2, N_LAT, C),
-            lon.reshape(2, N_EDGE, C),
-            diag.reshape(2, N_EDGE, C),
+            sibling,
+            from_lon,
+            from_lat,
+            from_line,
+            from_side,
+            from_corner,
             pick,
             back,
-            gain_col,
-            w3,
-            w3t,
+            norm_gain.reshape(1, C),
+            w_qkv,
             w_proj,
-            wpt,
+            mask_ids.transpose(1, 0, 2),
             bias,
-            blocked,
+            vmem=20,
             cost=(6 * 10**9, 10**6),
         )
         parts = lax.all_to_all(grads.reshape(n_plane, piece, 128), PLANE, 0, 0)
         own = call(
             scatter_kernel,
-            sds((MSG, 128), BF),
+            sds((MSG + LAT_ROWS, 128), BF),
             d_bias,
             hi,
             lo,
             out_edge,
+            out_lat,
             scratch=[pltpu.VMEM((HEADS * HIP, 128), F32)],
             cost=(8 * 10**9, 10**6),
         )
         parts, own = lax.optimization_barrier((parts, own))
-        near = lax.ppermute(own, AXES, hop(lambda zh, c: (zh, 1 - c)))
-        part = jnp.sum(parts.astype(F32), axis=0).astype(BF)
-        line = lax.all_to_all(jnp.broadcast_to(part, (n_line,) + part.shape), LINE, 0, 0)
-        pair = call(pair_kernel, sds((MSG, 128), BF), own, near)
-        far = lax.ppermute(pair, AXES, hop(lambda zh, c: (1 - zh, 1 - c)))
+        near = lax.ppermute(own, AXES, hop(lambda zh, c: (zh, 1 - c), (0, 1)))
+        part = call(total_kernel, sds((n_line, piece, 128), BF), parts, cost=(10**9, 10**6))
+        line = lax.all_to_all(part, LINE, 0, 0)
+        pair, across = call(
+            pair_kernel,
+            (sds((MSG, 128), BF), sds((2 * LAT_ROWS, 128), BF)),
+            own,
+            near,
+            out_lat,
+            out_corner,
+            cost=(10**9, 10**6),
+        )
+        far = lax.ppermute(pair, AXES, hop(lambda zh, c: (1 - zh, 0), (1,)))
+        across = lax.ppermute(across, AXES, [r for r in route(1, 0) if last(r) and r[0] % sizes[4] == 0])
         line, pair = lax.optimization_barrier((line, pair))
-        total = jnp.sum(line.astype(F32), axis=0).astype(BF)
-        whole = lax.all_to_all(jnp.broadcast_to(total, (n_plane,) + total.shape), PLANE, 0, 0)
-        core = jnp.full((1, 128), lax.axis_index("c"), jnp.int32)
-        base_x, base_d, out_lat, d_table = call(
+        total = call(total_kernel, sds((n_plane, piece, 128), BF), line, cost=(10**9, 10**6))
+        whole = lax.all_to_all(total, PLANE, 0, 0)
+        base_x, base_d, to_lat, to_near = call(
             middle_kernel,
             (
                 sds((N_OWN, C), BF),
                 sds((N_OWN, C), BF),
-                sds((2, N_LAT, C), BF),
-                sds((HEADS, 1, NPOS), F32),
+                sds((LAT_ROWS, 128), BF),
+                sds((LAT_ROWS + TAB_ROWS, 128), BF),
             ),
-            core,
             pair,
             near,
             far,
             base_x,
             base_d,
             out_lat,
+            out_corner,
+            across,
             place,
             cost=(20 * 10**9, 10**6),
         )
-        out_lat = lax.ppermute(out_lat, AXES, route(1, 0))
+        corners = [r for r in route(1, 1) if last(r) and r[0] % sizes[4] == 1]
+        from_lat = lax.ppermute(to_lat, AXES, [r for r in route(1, 0) if not last(r)] + corners)
+        from_near = lax.ppermute(to_near, AXES, hop(lambda zh, c: (zh, 1), (0,)))
         scale = float(n_lat * n_lon * N_OWN) ** -0.5
         qkv, proj, gain = call(
             lambda g, a, b, c: unpack_kernel(g, scale, a, b, c),
@@ -525,12 +617,19 @@
             whole.reshape(G_ROWS, 128),
         )
         base_x, qkv = lax.optimization_barrier((base_x, qkv))
-        updated, d_tokens = call(
+        updated, d_tokens, d_table = call(
             finish_kernel,
-            (sds((WPL, ROWS, COLS, C), BF), sds((WPL, ROWS, COLS, C), BF)),
+            (
+                sds((WPL, ROWS, COLS, C), BF),
+                sds((WPL, ROWS, COLS, C), BF),
+                sds((HEADS, 1, NPOS), F32),
+            ),
             base_x.reshape(WPL, ROWS, COLS, C),
             base_d.reshape(WPL, ROWS, COLS, C),
-            out_lat.reshape(2, WPL, HALF_LAT, COLS, C),
+            from_lat,
+            across,
+            from_near,
+            to_near,
             cost=(20 * 10**9, 10**6),
         )
         return updated, d_tokens, qkv, proj, gain.reshape(C), d_table.transpose(1, 0, 2)

time: 117 us -> 106 us (0.906)
  the two profiles are of different devices: /device:TPU:1 before, /device:TPU:256 now
where the time goes in v3:
time: 106 us
  starting transfers between devices  51.4 us (48%)
  waiting for transfers between devices  29 us (27%)
  Pallas kernels  21.9 us (21%)
  local copies, waits for them, and re-layouts  2.48 us (2%)
    pallas_call x11, Pallas kernels, call(): pl.pallas_call(kernel, out_shape=out_shape, scratch_shapes=list(scratch),...  21.9 us
    all_to_all x1, starting transfers between devices, per_device(): parts = lax.all_to_all(grads.reshape(n_plane, piece, 128), PLANE, 0, 0)  15.4 us
    all_to_all x1, starting transfers between devices, per_device(): line = lax.all_to_all(part, LINE, 0, 0)  12 us
    ppermute x1, waiting for transfers between devices, per_device(): lax.ppermute(to_lat, AXES, [r for r in route(1, 0) if not last(r)] + corn...  8.62 us
    ppermute x1, waiting for transfers between devices, per_device(): lax.ppermute(across, AXES, [r for r in route(1, 0) if last(r) and r[0] %...  6.83 us
    ppermute x1, waiting for transfers between devices, per_device(): far = lax.ppermute(pair, AXES, hop(lambda zh, c: (1 - zh, 0), (1,)))  5.54 us
    all_to_all x1, starting transfers between devices, per_device(): whole = lax.all_to_all(total, PLANE, 0, 0)  4.51 us
    ppermute x1, starting transfers between devices, per_device(): from_lon = lax.ppermute(to_lon, AXES, hop(lambda zh, c: (1 - zh, 1), (0,)))  4.09 us
  transfers between devices with their start and end apart: 14, of which 7 were waited for; matrix products, arithmetic and copies ran while one was open for 0% of the time, Pallas kernels for 13%

profile of v3, /device:TPU:256, one launch (start us, length us, event | category | flops | bytes accessed | tf_op | source)
XLA Modules:
  0.0 105.7 jit_solution(1806686027905148596)
XLA Ops:
  0.6 0.9 copy-done
  1.5 0.9 copy-done.2
  2.5 1.9 %collective-permute-start = (bf16[432,128]{1,0:T(8,128)(2,1)S(1)}, bf16[432,128]{1,0:T(8,128)(2,1)S(1)}, u32[]{:S(2)}, u32[]{:S(2)}) collective-permute-start(bf16[432,128]{1,0:T(8,128)(2,1)S(1)} %get-tuple-element.45), channel_id=1, source_target_pairs={{0,1},{1,0},{2,3},{3,2},{4,5},{5,4},{6,7},{7,6},{8,9},{9,8},{10,11... | collective-permute-start | bytes 331784 | tf_op jit(solution)/shard_map/ppermute | solution.py:507
  4.5 1.3 %collective-permute-done.sibling = bf16[432,128]{1,0:T(8,128)(2,1)S(1)} collective-permute-done((bf16[432,128]{1,0:T(8,128)(2,1)S(1)}, bf16[432,128]{1,0:T(8,128)(2,1)S(1)}, u32[]{:S(2)}, u32[]{:S(2)}) %collective-permute-start) | collective-permute-done | bytes 110624 | tf_op jit(solution)/shard_map/ppermute | solution.py:507
  5.8 4.1 %collective-permute-start.1 = (bf16[288,128]{1,0:T(8,128)(2,1)S(1)}, bf16[288,128]{1,0:T(8,128)(2,1)S(1)}, u32[]{:S(2)}, u32[]{:S(2)}) collective-permute-start(bf16[288,128]{1,0:T(8,128)(2,1)S(1)} %get-tuple-element.48), channel_id=1, source_target_pairs={{0,3},{2,1},{4,7},{6,5},{8,11},{10,9},{12,15},{14,13},{16,19},{18,... | collective-permute-start | bytes 221192 | tf_op jit(solution)/shard_map/ppermute | solution.py:516
  9.9 3.7 %collective-permute-start.2 = (bf16[576,128]{1,0:T(8,128)(2,1)S(1)}, bf16[576,128]{1,0:T(8,128)(2,1)S(1)}, u32[]{:S(2)}, u32[]{:S(2)}) collective-permute-start(bf16[576,128]{1,0:T(8,128)(2,1)S(1)} %get-tuple-element.49), channel_id=1, source_target_pairs={{4,0},{5,1},{6,2},{7,3},{8,4},{9,5},{10,6},{11,7},{12,8},{13,9},{1... | collective-permute-start | bytes 442376 | tf_op jit(solution)/shard_map/ppermute | solution.py:518
  14.5 5.2 %shard_map.156 = (f32[144,896]{1,0:T(8,128)S(1)}, s32[144,256]{1,0:T(8,128)S(1)}, s32[144,256]{1,0:T(8,128)S(1)}) custom-call(s32[144,144]{1,0:T(8,128)S(1)} %copy-done.5, f32[6,1,3312]{2,1,0:T(1,128)S(1)} %bitcast.14), custom_call_target="tpu_custom_call" | custom-call | flops 6000000000 | bytes 1000000 | tf_op jit(solution)/shard_map/pallas_call | solution.py:457
  21.8 6.0 %shard_map.157 = (bf16[288,192]{1,0:T(8,128)(2,1)S(1)}, bf16[288,192]{1,0:T(8,128)(2,1)S(1)}, bf16[432,128]{1,0:T(8,128)(2,1)S(1)}, bf16[432,128]{1,0:T(8,128)(2...) custom-call(bf16[288,192]{1,0:T(8,128)(2,1)S(1)} %bitcast.12, ...), custom_call_target="tpu_custom_call" | custom-call | flops 6000000000 | bytes 1000000 | tf_op jit(solution)/shard_map/pallas_call | solution.py:457
  27.8 15.4 %all-to-all-start = ((bf16[32,40,128]{2,1,0:T(8,128)(2,1)}), bf16[32,40,128]{2,1,0:T(8,128)(2,1)S(1)}, u32[]{:S(2)}, u32[]{:S(2)}) async-start(bf16[32,40,128]{2,1,0:T(8,128)(2,1)} %bitcast.5), calls=%async_computation | async-start | bytes 655360 | tf_op jit(solution)/shard_map/all_to_all | solution.py:561
  43.3 6.8 %shard_map.158.own = bf16[816,128]{1,0:T(8,128)(2,1)S(1)} custom-call(f32[144,896]{1,0:T(8,128)S(1)} %get-tuple-element.58.d_bias, s32[144,256]{1,0:T(8,128)S(1)} %get-tuple-element.59.hi, s32[144,256]{1,0:T(8,128)S(1)} %get-tuple-element.60.lo, bf16[224,128]{1,0:T(8,128)(2,1)S(1)} %get-tuple-element.61.edge, bf16[432,128]{1,0:T(8,128)(2,1)S(1)} %get-tuple-element.62.lat), custom_call_target="tpu_custom_call" | custom-call | flops 8000000000 | bytes 1000000 | tf_op jit(solution)/shard_map/pallas_call | solution.py:457
  50.0 2.7 %all-to-all-done.parts = bf16[32,40,128]{2,1,0:T(8,128)(2,1)S(1)} async-done(((bf16[32,40,128]{2,1,0:T(8,128)(2,1)}), bf16[32,40,128]{2,1,0:T(8,128)(2,1)S(1)}, u32[]{:S(2)}, u32[]{:S(2)}) %all-to-all-start) | async-done | bytes 327712 | tf_op jit(solution)/shard_map/all_to_all | solution.py:561
  53.4 12.0 %all-to-all-start.1 = ((bf16[16,40,128]{2,1,0:T(8,128)(2,1)}), bf16[16,40,128]{2,1,0:T(8,128)(2,1)S(1)}, u32[]{:S(2)}, u32[]{:S(2)}) async-start(bf16[16,40,128]{2,1,0:T(8,128)(2,1)} %shard_map.159), calls=%async_computation.1 | async-start | bytes 327680 | tf_op jit(solution)/shard_map/all_to_all | solution.py:576
  65.4 1.9 %collective-permute-start.6 = (bf16[816,128]{1,0:T(8,128)(2,1)S(1)}, bf16[816,128]{1,0:T(8,128)(2,1)S(1)}, u32[]{:S(2)}, u32[]{:S(2)}) collective-permute-start(bf16[816,128]{1,0:T(8,128)(2,1)S(1)} %shard_map.158.own), channel_id=1, source_target_pairs={{0,1},{1,0},{2,3},{3,2},{4,5},{5,4},{6,7},{7,6},{8,9},{9,8},{10,11... | collective-permute-start | bytes 626696 | tf_op jit(solution)/shard_map/ppermute | solution.py:574
  67.4 1.4 %collective-permute-done.6.near = bf16[816,128]{1,0:T(8,128)(2,1)S(1)} collective-permute-done((bf16[816,128]{1,0:T(8,128)(2,1)S(1)}, bf16[816,128]{1,0:T(8,128)(2,1)S(1)}, u32[]{:S(2)}, u32[]{:S(2)}) %collective-permute-start.6) | collective-permute-done | bytes 208928 | tf_op jit(solution)/shard_map/ppermute | solution.py:574
  68.8 1.3 %collective-permute-start.8 = (bf16[864,128]{1,0:T(8,128)(2,1)S(1)}, bf16[864,128]{1,0:T(8,128)(2,1)S(1)}, u32[]{:S(2)}, u32[]{:S(2)}) collective-permute-start(bf16[864,128]{1,0:T(8,128)(2,1)S(1)} %get-tuple-element.70), channel_id=1, source_target_pairs={{124,128},{126,130},{252,256},{254,258},{380,384},{382,386},{508,0... | collective-permute-start | bytes 663560 | tf_op jit(solution)/shard_map/ppermute | solution.py:587
  70.1 1.3 %collective-permute-start.7 = (bf16[384,128]{1,0:T(8,128)(2,1)S(1)}, bf16[384,128]{1,0:T(8,128)(2,1)S(1)}, u32[]{:S(2)}, u32[]{:S(2)}) collective-permute-start(bf16[384,128]{1,0:T(8,128)(2,1)S(1)} %get-tuple-element.67.pair), channel_id=1, source_target_pairs={{1,2},{3,0},{5,6},{7,4},{9,10},{11,8},{13,14},{15,12},{17,18},{19,... | collective-permute-start | bytes 294920 | tf_op jit(solution)/shard_map/ppermute | solution.py:586
  71.4 2.6 %all-to-all-done.1.parts = bf16[16,40,128]{2,1,0:T(8,128)(2,1)S(1)} async-done(((bf16[16,40,128]{2,1,0:T(8,128)(2,1)}), bf16[16,40,128]{2,1,0:T(8,128)(2,1)S(1)}, u32[]{:S(2)}, u32[]{:S(2)}) %all-to-all-start.1) | async-done | bytes 163872 | tf_op jit(solution)/shard_map/all_to_all | solution.py:576
  74.8 4.5 %all-to-all-start.2 = ((bf16[32,40,128]{2,1,0:T(8,128)(2,1)}), bf16[32,40,128]{2,1,0:T(8,128)(2,1)S(1)}, u32[]{:S(2)}, u32[]{:S(2)}) async-start(bf16[32,40,128]{2,1,0:T(8,128)(2,1)} %shard_map.162), calls=%async_computation.2 | async-start | bytes 655360 | tf_op jit(solution)/shard_map/all_to_all | solution.py:590
  79.3 5.5 %collective-permute-done.7.far = bf16[384,128]{1,0:T(8,128)(2,1)S(1)} collective-permute-done((bf16[384,128]{1,0:T(8,128)(2,1)S(1)}, bf16[384,128]{1,0:T(8,128)(2,1)S(1)}, u32[]{:S(2)}, u32[]{:S(2)}) %collective-permute-start.7) | collective-permute-done | bytes 98336 | tf_op jit(solution)/shard_map/ppermute | solution.py:586
  84.8 6.8 %collective-permute-done.8.across = bf16[864,128]{1,0:T(8,128)(2,1)S(1)} collective-permute-done((bf16[864,128]{1,0:T(8,128)(2,1)S(1)}, bf16[864,128]{1,0:T(8,128)(2,1)S(1)}, u32[]{:S(2)}, u32[]{:S(2)}) %collective-permute-start.8) | collective-permute-done | bytes 221216 | tf_op jit(solution)/shard_map/ppermute | solution.py:587
  92.1 1.3 %collective-permute-start.10 = (bf16[592,128]{1,0:T(8,128)(2,1)S(1)}, bf16[592,128]{1,0:T(8,128)(2,1)S(1)}, u32[]{:S(2)}, u32[]{:S(2)}) collective-permute-start(bf16[592,128]{1,0:T(8,128)(2,1)S(1)} %get-tuple-element.77.own), channel_id=1, source_target_pairs={{0,1},{2,3},{4,5},{6,7},{8,9},{10,11},{12,13},{14,15},{16,17},{18,... | collective-permute-start | bytes 454664 | tf_op jit(solution)/shard_map/ppermute | solution.py:612
  93.4 1.9 %collective-permute-start.9 = (bf16[432,128]{1,0:T(8,128)(2,1)S(1)}, bf16[432,128]{1,0:T(8,128)(2,1)S(1)}, u32[]{:S(2)}, u32[]{:S(2)}) collective-permute-start(bf16[432,128]{1,0:T(8,128)(2,1)S(1)} %get-tuple-element.76), channel_id=1, source_target_pairs={{0,4},{1,5},{2,6},{3,7},{4,8},{5,9},{6,10},{7,11},{8,12},{9,13},{1... | collective-permute-start | bytes 331784 | tf_op jit(solution)/shard_map/ppermute | solution.py:611
  95.3 0.9 shard_map.163
  96.3 8.6 %collective-permute-done.9.lat = bf16[432,128]{1,0:T(8,128)(2,1)S(1)} collective-permute-done((bf16[432,128]{1,0:T(8,128)(2,1)S(1)}, bf16[432,128]{1,0:T(8,128)(2,1)S(1)}, u32[]{:S(2)}, u32[]{:S(2)}) %collective-permute-start.9) | collective-permute-done | bytes 110624 | tf_op jit(solution)/shard_map/ppermute | solution.py:611
  (41 shorter events, 5.6 us)
Async XLA Ops:
  2.5 3.2 %collective-permute-start = (bf16[432,128]{1,0:T(8,128)(2,1)S(1)}, bf16[432,128]{1,0:T(8,128)(2,1)S(1)}, u32[]{:S(2)}, u32[]{:S(2)}) collective-permute-start(bf16[432,128]{1,0:T(8,128)(2,1)S(1)} %get-tuple-element.45), channel_id=1, source_target_pairs={{0,1},{1,0},{2,3},{3,2},{4,5},{5,4},{6,7},{7,6},{8,9},{9,8},{10,11... | collective-permute-start | bytes 331784 | tf_op jit(solution)/shard_map/ppermute | solution.py:507
  5.8 8.6 %copy-start.5 = (s32[144,144]{1,0:T(8,128)S(1)}, s32[144,144]{1,0:T(8,128)}, u32[]{:S(2)}) copy-start(s32[144,144]{1,0:T(8,128)} %pos.1) | copy-start | bytes 248836
  5.8 8.6 %copy-start.7 = (f32[1,6,3312]{2,0,1:T(1,128)S(1)}, f32[1,6,3312]{2,0,1:T(1,128)}, u32[]{:S(2)}) copy-start(f32[1,6,3312]{2,0,1:T(1,128)} %param.17) | copy-start | bytes 238468
  5.8 13.9 %collective-permute-start.1 = (bf16[288,128]{1,0:T(8,128)(2,1)S(1)}, bf16[288,128]{1,0:T(8,128)(2,1)S(1)}, u32[]{:S(2)}, u32[]{:S(2)}) collective-permute-start(bf16[288,128]{1,0:T(8,128)(2,1)S(1)} %get-tuple-element.48), channel_id=1, source_target_pairs={{0,3},{2,1},{4,7},{6,5},{8,11},{10,9},{12,15},{14,13},{16,19},{18,... | collective-permute-start | bytes 221192 | tf_op jit(solution)/shard_map/ppermute | solution.py:516
  9.9 9.8 %collective-permute-start.2 = (bf16[576,128]{1,0:T(8,128)(2,1)S(1)}, bf16[576,128]{1,0:T(8,128)(2,1)S(1)}, u32[]{:S(2)}, u32[]{:S(2)}) collective-permute-start(bf16[576,128]{1,0:T(8,128)(2,1)S(1)} %get-tuple-element.49), channel_id=1, source_target_pairs={{4,0},{5,1},{6,2},{7,3},{8,4},{9,5},{10,6},{11,7},{12,8},{13,9},{1... | collective-permute-start | bytes 442376 | tf_op jit(solution)/shard_map/ppermute | solution.py:518
  13.7 6.7 %collective-permute-start.3 = (bf16[1008,128]{1,0:T(8,128)(2,1)S(1)}, bf16[1008,128]{1,0:T(8,128)(2,1)S(1)}, u32[]{:S(2)}, u32[]{:S(2)}) collective-permute-start(bf16[1008,128]{1,0:T(8,128)(2,1)S(1)} %get-tuple-element.53), channel_id=1, source_target_pairs={{1,509},{3,511},{129,125},{131,127},{257,253},{259,255},{385,381},... | collective-permute-start | bytes 774152 | tf_op jit(solution)/shard_map/ppermute | solution.py:519
  14.4 6.7 %copy-start.1 = (bf16[2,6,24,192]{3,2,1,0:T(8,128)(2,1)S(1)}, bf16[2,6,24,192]{3,2,1,0:T(8,128)(2,1)}, u32[]{:S(2)}) copy-start(bf16[2,6,24,192]{3,2,1,0:T(8,128)(2,1)} %tokens.1) | copy-start | bytes 331780
  14.4 6.7 %copy-start.3 = (bf16[2,6,24,192]{3,2,1,0:T(8,128)(2,1)S(1)}, bf16[2,6,24,192]{3,2,1,0:T(8,128)(2,1)}, u32[]{:S(2)}) copy-start(bf16[2,6,24,192]{3,2,1,0:T(8,128)(2,1)} %d_out.1) | copy-start | bytes 331780
  14.4 6.7 %copy-start.4 = (bf16[192,576]{1,0:T(8,128)(2,1)S(1)}, bf16[192,576]{1,0:T(8,128)(2,1)}, u32[]{:S(2)}) copy-start(bf16[192,576]{1,0:T(8,128)(2,1)} %w_qkv.1) | copy-start | bytes 663556
  14.4 6.7 %copy-start.6 = (bf16[192,192]{1,0:T(8,128)(2,1)S(1)}, bf16[192,192]{1,0:T(8,128)(2,1)}, u32[]{:S(2)}) copy-start(bf16[192,192]{1,0:T(8,128)(2,1)} %wp.1) | copy-start | bytes 221188
  14.4 6.7 %copy-start.10 = (bf16[2,648,144]{2,1,0:T(8,128)(2,1)S(1)}, bf16[2,648,144]{2,1,0:T(8,128)(2,1)}, u32[]{:S(2)}) copy-start(bf16[2,648,144]{2,1,0:T(8,128)(2,1)} %constant.7.clone.back) | copy-start | bytes 1119748
  14.4 6.7 %copy-start.11 = (bf16[2,144,528]{2,1,0:T(8,128)(2,1)S(1)}, bf16[2,144,528]{2,1,0:T(8,128)(2,1)}, u32[]{:S(2)}) copy-start(bf16[2,144,528]{2,1,0:T(8,128)(2,1)} %constant.6.clone.pick) | copy-start | bytes 912388
  19.7 1.5 %copy-start.8 = (s32[2,6,24]{2,0,1:T(2,128)S(1)}, s32[2,6,24]{2,0,1:T(2,128)}, u32[]{:S(2)}) copy-start(s32[2,6,24]{2,0,1:T(2,128)} %param.12) | copy-start | bytes 3460
  19.7 0.7 collective-permute-start.4
  20.4 0.7 collective-permute-start.5
  27.8 24.8 %all-to-all-start = ((bf16[32,40,128]{2,1,0:T(8,128)(2,1)}), bf16[32,40,128]{2,1,0:T(8,128)(2,1)S(1)}, u32[]{:S(2)}, u32[]{:S(2)}) async-start(bf16[32,40,128]{2,1,0:T(8,128)(2,1)} %bitcast.5), calls=%async_computation | async-start | bytes 655360 | tf_op jit(solution)/shard_map/all_to_all | solution.py:561
  53.4 20.6 %all-to-all-start.1 = ((bf16[16,40,128]{2,1,0:T(8,128)(2,1)}), bf16[16,40,128]{2,1,0:T(8,128)(2,1)S(1)}, u32[]{:S(2)}, u32[]{:S(2)}) async-start(bf16[16,40,128]{2,1,0:T(8,128)(2,1)} %shard_map.159), calls=%async_computation.1 | async-start | bytes 327680 | tf_op jit(solution)/shard_map/all_to_all | solution.py:576
  65.4 3.3 %collective-permute-start.6 = (bf16[816,128]{1,0:T(8,128)(2,1)S(1)}, bf16[816,128]{1,0:T(8,128)(2,1)S(1)}, u32[]{:S(2)}, u32[]{:S(2)}) collective-permute-start(bf16[816,128]{1,0:T(8,128)(2,1)S(1)} %shard_map.158.own), channel_id=1, source_target_pairs={{0,1},{1,0},{2,3},{3,2},{4,5},{5,4},{6,7},{7,6},{8,9},{9,8},{10,11... | collective-permute-start | bytes 626696 | tf_op jit(solution)/shard_map/ppermute | solution.py:574
  68.8 22.8 %collective-permute-start.8 = (bf16[864,128]{1,0:T(8,128)(2,1)S(1)}, bf16[864,128]{1,0:T(8,128)(2,1)S(1)}, u32[]{:S(2)}, u32[]{:S(2)}) collective-permute-start(bf16[864,128]{1,0:T(8,128)(2,1)S(1)} %get-tuple-element.70), channel_id=1, source_target_pairs={{124,128},{126,130},{252,256},{254,258},{380,384},{382,386},{508,0... | collective-permute-start | bytes 663560 | tf_op jit(solution)/shard_map/ppermute | solution.py:587
  70.1 14.7 %collective-permute-start.7 = (bf16[384,128]{1,0:T(8,128)(2,1)S(1)}, bf16[384,128]{1,0:T(8,128)(2,1)S(1)}, u32[]{:S(2)}, u32[]{:S(2)}) collective-permute-start(bf16[384,128]{1,0:T(8,128)(2,1)S(1)} %get-tuple-element.67.pair), channel_id=1, source_target_pairs={{1,2},{3,0},{5,6},{7,4},{9,10},{11,8},{13,14},{15,12},{17,18},{19,... | collective-permute-start | bytes 294920 | tf_op jit(solution)/shard_map/ppermute | solution.py:586
  74.8 16.9 %copy-start.12 = (bf16[432,72]{1,0:T(8,128)(2,1)S(1)}, bf16[432,72]{1,0:T(8,128)(2,1)}, u32[]{:S(2)}) copy-start(bf16[432,72]{1,0:T(8,128)(2,1)} %constant.8.clone.place) | copy-start | bytes 186628
  74.8 20.5 %all-to-all-start.2 = ((bf16[32,40,128]{2,1,0:T(8,128)(2,1)}), bf16[32,40,128]{2,1,0:T(8,128)(2,1)S(1)}, u32[]{:S(2)}, u32[]{:S(2)}) async-start(bf16[32,40,128]{2,1,0:T(8,128)(2,1)} %shard_map.162), calls=%async_computation.2 | async-start | bytes 655360 | tf_op jit(solution)/shard_map/all_to_all | solution.py:590
  92.1 12.8 %collective-permute-start.10 = (bf16[592,128]{1,0:T(8,128)(2,1)S(1)}, bf16[592,128]{1,0:T(8,128)(2,1)S(1)}, u32[]{:S(2)}, u32[]{:S(2)}) collective-permute-start(bf16[592,128]{1,0:T(8,128)(2,1)S(1)} %get-tuple-element.77.own), channel_id=1, source_target_pairs={{0,1},{2,3},{4,5},{6,7},{8,9},{10,11},{12,13},{14,15},{16,17},{18,... | collective-permute-start | bytes 454664 | tf_op jit(solution)/shard_map/ppermute | solution.py:612
  93.4 11.5 %collective-permute-start.9 = (bf16[432,128]{1,0:T(8,128)(2,1)S(1)}, bf16[432,128]{1,0:T(8,128)(2,1)S(1)}, u32[]{:S(2)}, u32[]{:S(2)}) collective-permute-start(bf16[432,128]{1,0:T(8,128)(2,1)S(1)} %get-tuple-element.76), channel_id=1, source_target_pairs={{0,4},{1,5},{2,6},{3,7},{4,8},{5,9},{6,10},{7,11},{8,12},{9,13},{1... | collective-permute-start | bytes 331784 | tf_op jit(solution)/shard_map/ppermute | solution.py:611
  (3 other events, 2.5 us)

commit v4 on v3

--- a/solution.py
+++ b/solution.py
@@ -138,7 +138,7 @@
     return lax.broadcasted_iota(jnp.int32, (rows, 128), 0) * 0 + at == want
 
 
-def cut_kernel(tokens, d_out, to_core, lat, edge):
+def cut_kernel(tokens, d_out, to_core, lat, edge, to_diag):
     both = (tokens[...].astype(F32), d_out[...].astype(F32))
     top = fold(*(a[:, :HALF_LAT].reshape(N_LAT, C) for a in both))
     corner = fold(*(a[:, :HALF_LAT, :EDGE].reshape(N_EDGE, C) for a in both))
@@ -146,19 +146,17 @@
     side = jnp.concatenate([corner, lon], axis=0)
     lat[...] = top.astype(BF)
     edge[...] = side.astype(BF)
+    to_diag[...] = corner.astype(BF)
     spare = jnp.zeros((LAT_ROWS - SIDE_ROWS, 128), F32)
     to_core[...] = jnp.where(core_is(1, LAT_ROWS), jnp.concatenate([side, spare], axis=0), top).astype(BF)
 
 
-def join_kernel(lat, edge, sibling, to_lon, to_lat, to_line):
-    corner = edge[:CORNER_ROWS, :]
-    to_lon[...] = edge[...]
+def join_kernel(lat, corner, sibling, to_lat, to_line):
     to_lat[:LAT_ROWS, :] = lat[...]
-    theirs = sibling[:CORNER_ROWS, :].astype(F32)
-    to_lat[LAT_ROWS:, :] = jnp.where(band_is(True, CORNER_ROWS), corner.astype(F32), theirs).astype(BF)
+    to_lat[LAT_ROWS:, :] = sibling[:CORNER_ROWS, :]
     to_line[:LAT_ROWS, :] = lat[...]
     to_line[LAT_ROWS : 2 * LAT_ROWS, :] = sibling[...]
-    to_line[2 * LAT_ROWS :, :] = corner
+    to_line[2 * LAT_ROWS :, :] = corner[...]
 
 
 def tables_kernel(pos, table, bias, hi_out, lo_out, scr):
@@ -269,7 +267,7 @@
 
 
 def block_kernel(
-    own_x, own_d, sibling, from_lon, from_lat, from_line, from_side, from_corner, pick, back, gain, w_qkv, wp, mask, bias,
+    own_x, own_d, sibling, from_lon, from_lat, from_line, from_side, from_diag, pick, back, gain, w_qkv, wp, mask, bias,
     base_x, base_d, out_lat, out_corner, out_edge, grads, d_bias,
 ):
     f32 = lambda ref, start, size: ref[start : start + size, :].astype(F32)
@@ -277,9 +275,10 @@
     lat = unfold(jnp.where(band_is(False, LAT_ROWS), over, f32(from_lat, 0, LAT_ROWS)), N_LAT)
     lon = f32(sibling, CORNER_ROWS, CORNER_ROWS), f32(from_lon, CORNER_ROWS, CORNER_ROWS)
     lon = unfold(jnp.where(core_is(0, CORNER_ROWS), *lon), N_EDGE)
-    direct = core_is(0, CORNER_ROWS) != band_is(False, CORNER_ROWS)
-    diag = f32(from_side, 2 * LAT_ROWS, CORNER_ROWS) + f32(from_corner, 0, CORNER_ROWS)
-    diag = unfold(jnp.where(direct, f32(from_lat, LAT_ROWS, CORNER_ROWS), diag), N_EDGE)
+    inner = jnp.where(
+        band_is(False, CORNER_ROWS), f32(from_side, 2 * LAT_ROWS, CORNER_ROWS), f32(from_lat, LAT_ROWS, CORNER_ROWS)
+    )
+    diag = unfold(jnp.where(core_is(0, CORNER_ROWS), inner, f32(from_diag, 0, CORNER_ROWS)), N_EDGE)
     x_all, d_all = (
         jnp.concatenate([own[...], lat[i].astype(BF), lon[i].astype(BF), diag[i].astype(BF)], axis=0)
         for i, own in enumerate((own_x, own_d))
@@ -397,11 +396,18 @@
     out[MSG:, :] = lat[...]
 
 
-def pair_kernel(own, near, lat, corner, out, across):
+def pair_kernel(own, near, out):
     out[:EDGE_ROWS, :] = own[:EDGE_ROWS, :]
     out[EDGE_ROWS:, :] = (own[EDGE_ROWS:MSG, :].astype(F32) + near[EDGE_ROWS:MSG, :].astype(F32)).astype(BF)
+
+
+def line_kernel(near, lat, corner, across):
     across[:LAT_ROWS, :] = lat[...]
     across[LAT_ROWS:, :] = (near[MSG:, :].astype(F32) + corner[...].astype(F32)).astype(BF)
+
+
+def beside_kernel(across, out):
+    out[...] = across[LAT_ROWS:, :]
 
 
 def total_kernel(parts, out):
@@ -413,24 +419,24 @@
         out[i] = total
 
 
-def middle_kernel(pair, near, far, base_x, base_d, lat, corner, across, place, out_x, out_d, out_lat, out_near):
+def middle_kernel(pair, near, far, base_x, base_d, lat, corner, place, out_x, out_d, out_lat, out_near):
     edge = jnp.where(core_is(1, 3 * CUT), near[: 3 * CUT, :].astype(F32), far[: 3 * CUT, :].astype(F32))
     adds = [nn(place[...], e.astype(BF)) for e in unfold(edge, CUT)]
     for add, base, out in ((adds[0], base_x, out_x), (adds[1], base_d, out_d)):
         out[...] = (base[...].astype(F32) + add[:N_OWN]).astype(BF)
     whole = lat[...].astype(F32) + fold(adds[0][N_OWN:], adds[1][N_OWN:])
-    out_lat[...] = jnp.where(band_is(False, LAT_ROWS), corner[...].astype(F32), whole).astype(BF)
-    out_near[:LAT_ROWS, :] = across[LAT_ROWS:, :]
-    out_near[LAT_ROWS:, :] = (pair[EDGE_ROWS:, :].astype(F32) + far[EDGE_ROWS:, :].astype(F32)).astype(BF)
-
-
-def finish_kernel(base_x, base_d, lat, across, near, own, out_x, out_d, out_t):
-    got = lat[...].astype(F32) + across[:LAT_ROWS, :].astype(F32) + near[:LAT_ROWS, :].astype(F32)
+    out_lat[LAT_ROWS:, :] = jnp.zeros((16, 128), BF)
+    out_lat[:LAT_ROWS, :] = jnp.where(band_is(False, LAT_ROWS), corner[...].astype(F32), whole).astype(BF)
+    out_near[...] = (pair[EDGE_ROWS:, :].astype(F32) + far[EDGE_ROWS:, :].astype(F32)).astype(BF)
+
+
+def finish_kernel(base_x, base_d, lat, across, beside, near, own, out_x, out_d, out_t):
+    got = lat[:LAT_ROWS, :].astype(F32) + across[:LAT_ROWS, :].astype(F32) + beside[...].astype(F32)
     for add, base, out in zip(unfold(got, N_LAT), (base_x, base_d), (out_x, out_d)):
         out[:, HALF_LAT:] = base[:, HALF_LAT:]
         add = add.reshape(WPL, HALF_LAT, COLS, C)
         out[:, :HALF_LAT] = (base[:, :HALF_LAT].astype(F32) + add).astype(BF)
-    t = jnp.where(core_is(1, TAB_ROWS), near[LAT_ROWS:, :].astype(F32), own[LAT_ROWS:, :].astype(F32))
+    t = jnp.where(core_is(1, TAB_ROWS), near[...].astype(F32), own[...].astype(F32))
     for part in range(HI):
         width = min(128, NPOS - part * 128)
         for head in range(HEADS):
@@ -498,24 +504,29 @@
 
     def per_device(tokens, mask_ids, pos_index, norm_gain, w_qkv, w_proj, earth_bias, d_out):
         pick, back, place = (jnp.asarray(c) for c in constants())
-        to_core, lat, edge = call(
+        to_core, lat, edge, to_diag = call(
             cut_kernel,
-            (sds((LAT_ROWS, 128), BF), sds((LAT_ROWS, 128), BF), sds((SIDE_ROWS, 128), BF)),
+            (
+                sds((LAT_ROWS, 128), BF),
+                sds((LAT_ROWS, 128), BF),
+                sds((SIDE_ROWS, 128), BF),
+                sds((CORNER_ROWS, 128), BF),
+            ),
             tokens,
             d_out,
         )
         sibling = lax.ppermute(to_core, AXES, hop(lambda zh, c: (zh, 1 - c), (0, 1)))
-        to_lon, to_lat, to_line = call(
+        from_lon = lax.ppermute(edge, AXES, hop(lambda zh, c: (1 - zh, 1), (0,)))
+        from_diag = lax.ppermute(to_diag, AXES, [r for r in route(-1, -1) if r[0] % sizes[4] == 0])
+        to_lat, to_line = call(
             join_kernel,
-            (sds((SIDE_ROWS, 128), BF), sds((LAT_ROWS + CORNER_ROWS, 128), BF), sds((LINE_ROWS, 128), BF)),
+            (sds((LAT_ROWS + CORNER_ROWS, 128), BF), sds((LINE_ROWS, 128), BF)),
             lat,
-            edge,
+            to_diag,
             sibling,
         )
         south = route(-1, 0)
-        from_lon = lax.ppermute(to_lon, AXES, hop(lambda zh, c: (1 - zh, 1), (0,)))
-        corners = [r for r in route(-1, -1) if first(r) and r[0] % sizes[4] == 0]
-        from_lat = lax.ppermute(to_lat, AXES, [r for r in south if not first(r)] + corners)
+        from_lat = lax.ppermute(to_lat, AXES, [r for r in south if not first(r)])
         from_line = lax.ppermute(to_line, AXES, [r for r in south if first(r) and r[0] % sizes[4] == 1])
         bias, hi, lo = call(
             tables_kernel,
@@ -525,9 +536,8 @@
             scratch=[pltpu.VMEM((HEADS // 2, HI * 128), jnp.int32)],
             cost=(6 * 10**9, 10**6),
         )
-        from_lon, from_lat, bias = lax.optimization_barrier((from_lon, from_lat, bias))
-        from_corner = lax.ppermute(from_lon, AXES, [r for r in south if not first(r) and r[0] % sizes[4] == 1])
-        from_line, from_corner = lax.optimization_barrier((from_line, from_corner))
+        received = (from_line, from_lon, from_diag, from_lat, bias)
+        from_line, from_lon, from_diag, from_lat, bias = lax.optimization_barrier(received)
         from_side = lax.ppermute(from_line, AXES, [r for r in hop(lambda zh, c: (zh, 0), (1,)) if last(r)])
         base_x, base_d, out_lat, out_corner, out_edge, grads, d_bias = call(
             block_kernel,
@@ -547,7 +557,7 @@
             from_lat,
             from_line,
             from_side,
-            from_corner,
+            from_diag,
             pick,
             back,
             norm_gain.reshape(1, C),
@@ -574,16 +584,9 @@
         near = lax.ppermute(own, AXES, hop(lambda zh, c: (zh, 1 - c), (0, 1)))
         part = call(total_kernel, sds((n_line, piece, 128), BF), parts, cost=(10**9, 10**6))
         line = lax.all_to_all(part, LINE, 0, 0)
-        pair, across = call(
-            pair_kernel,
-            (sds((MSG, 128), BF), sds((2 * LAT_ROWS, 128), BF)),
-            own,
-            near,
-            out_lat,
-            out_corner,
-            cost=(10**9, 10**6),
-        )
+        pair = call(pair_kernel, sds((MSG, 128), BF), own, near, cost=(10**9, 10**6))
         far = lax.ppermute(pair, AXES, hop(lambda zh, c: (1 - zh, 0), (1,)))
+        across = call(line_kernel, sds((2 * LAT_ROWS, 128), BF), near, out_lat, out_corner, cost=(10**9, 10**6))
         across = lax.ppermute(across, AXES, [r for r in route(1, 0) if last(r) and r[0] % sizes[4] == 0])
         line, pair = lax.optimization_barrier((line, pair))
         total = call(total_kernel, sds((n_plane, piece, 128), BF), line, cost=(10**9, 10**6))
@@ -593,8 +596,8 @@
             (
                 sds((N_OWN, C), BF),
                 sds((N_OWN, C), BF),
-                sds((LAT_ROWS, 128), BF),
-                sds((LAT_ROWS + TAB_ROWS, 128), BF),
+                sds((LAT_ROWS + 16, 128), BF),
+                sds((TAB_ROWS, 128), BF),
             ),
             pair,
             near,
@@ -603,13 +606,15 @@
             base_d,
             out_lat,
             out_corner,
-            across,
             place,
             cost=(20 * 10**9, 10**6),
         )
         corners = [r for r in route(1, 1) if last(r) and r[0] % sizes[4] == 1]
         from_lat = lax.ppermute(to_lat, AXES, [r for r in route(1, 0) if not last(r)] + corners)
         from_near = lax.ppermute(to_near, AXES, hop(lambda zh, c: (zh, 1), (0,)))
+        across, from_near = lax.optimization_barrier((across, from_near))
+        beside = call(beside_kernel, sds((LAT_ROWS, 128), BF), across, cost=(10**9, 10**6))
+        beside = lax.ppermute(beside, AXES, [r for r in hop(lambda zh, c: (zh, 1), (0,)) if first(r)])
         scale = float(n_lat * n_lon * N_OWN) ** -0.5
         qkv, proj, gain = call(
             lambda g, a, b, c: unpack_kernel(g, scale, a, b, c),
@@ -628,6 +633,7 @@
             base_d.reshape(WPL, ROWS, COLS, C),
             from_lat,
             across,
+            beside,
             from_near,
             to_near,
             cost=(20 * 10**9, 10**6),

time: 106 us -> 103 us (0.972)
  the two profiles are of different devices: /device:TPU:256 before, /device:TPU:1 now
where the time goes in v4:
time: 103 us; the launch traced here: 101 us
  starting transfers between devices  68.7 us (67%)
  Pallas kernels  21.9 us (21%)
  waiting for transfers between devices  7.36 us (7%)
  local copies, waits for them, and re-layouts  2.48 us (2%)
  between operations  1.04 us (1%)
    pallas_call x13, Pallas kernels, call(): pl.pallas_call(kernel, out_shape=out_shape, scratch_shapes=list(scratch),...  21.9 us
    ppermute x1, starting transfers between devices, per_device(): lax.ppermute(to_line, AXES, [r for r in south if first(r) and r[0] % size...  13.2 us
    ppermute x1, starting transfers between devices, per_device(): far = lax.ppermute(pair, AXES, hop(lambda zh, c: (1 - zh, 0), (1,)))  12.4 us
    all_to_all x1, starting transfers between devices, per_device(): line = lax.all_to_all(part, LINE, 0, 0)  10.2 us
    ppermute x1, starting transfers between devices, per_device(): lax.ppermute(to_core, AXES, hop(lambda zh, c: (zh, 1 - c), (0, 1)))  8.92 us
    all_to_all x1, starting transfers between devices, per_device(): parts = lax.all_to_all(grads.reshape(n_plane, piece, 128), PLANE, 0, 0)  5.88 us
    all_to_all x1, starting transfers between devices, per_device(): whole = lax.all_to_all(total, PLANE, 0, 0)  4.74 us
    all_to_all x1, waiting for transfers between devices, per_device(): whole = lax.all_to_all(total, PLANE, 0, 0)  3.3 us
  transfers between devices with their start and end apart: 15, of which 3 were waited for; matrix products, arithmetic and copies ran while one was open for 0% of the time, Pallas kernels for 14%

profile of v4, /device:TPU:1, one launch (start us, length us, event | category | flops | bytes accessed | tf_op | source)
XLA Modules:
  0.0 101.5 jit_solution(15882217281222628062)
XLA Ops:
  0.6 0.9 copy-done
  1.5 0.9 copy-done.2
  2.6 8.9 %collective-permute-start = (bf16[432,128]{1,0:T(8,128)(2,1)S(1)}, bf16[432,128]{1,0:T(8,128)(2,1)S(1)}, u32[]{:S(2)}, u32[]{:S(2)}) collective-permute-start(bf16[432,128]{1,0:T(8,128)(2,1)S(1)} %get-tuple-element.45), channel_id=1, source_target_pairs={{0,1},{1,0},{2,3},{3,2},{4,5},{5,4},{6,7},{7,6},{8,9},{9,8},{10,11... | collective-permute-start | bytes 331784 | tf_op jit(solution)/shard_map/ppermute | solution.py:518
  11.5 1.3 %collective-permute-start.3 = (bf16[144,128]{1,0:T(8,128)(2,1)S(1)}, bf16[144,128]{1,0:T(8,128)(2,1)S(1)}, u32[]{:S(2)}, u32[]{:S(2)}) collective-permute-start(bf16[144,128]{1,0:T(8,128)(2,1)S(1)} %get-tuple-element.47.corner), channel_id=1, source_target_pairs={{0,511},{2,509},{4,3},{6,1},{8,7},{10,5},{12,11},{14,9},{16,15},{1... | collective-permute-start | bytes 110600 | tf_op jit(solution)/shard_map/ppermute | solution.py:520
  12.8 1.3 %collective-permute-start.2 = (bf16[288,128]{1,0:T(8,128)(2,1)S(1)}, bf16[288,128]{1,0:T(8,128)(2,1)S(1)}, u32[]{:S(2)}, u32[]{:S(2)}) collective-permute-start(bf16[288,128]{1,0:T(8,128)(2,1)S(1)} %get-tuple-element.49), channel_id=1, source_target_pairs={{0,3},{2,1},{4,7},{6,5},{8,11},{10,9},{12,15},{14,13},{16,19},{18,... | collective-permute-start | bytes 221192 | tf_op jit(solution)/shard_map/ppermute | solution.py:519
  14.2 1.3 %collective-permute-start.4 = (bf16[576,128]{1,0:T(8,128)(2,1)S(1)}, bf16[576,128]{1,0:T(8,128)(2,1)S(1)}, u32[]{:S(2)}, u32[]{:S(2)}) collective-permute-start(bf16[576,128]{1,0:T(8,128)(2,1)S(1)} %get-tuple-element.50), channel_id=1, source_target_pairs={{4,0},{5,1},{6,2},{7,3},{8,4},{9,5},{10,6},{11,7},{12,8},{13,9},{1... | collective-permute-start | bytes 442376 | tf_op jit(solution)/shard_map/ppermute | solution.py:529
  15.5 13.2 %collective-permute-start.1 = (bf16[1008,128]{1,0:T(8,128)(2,1)S(1)}, bf16[1008,128]{1,0:T(8,128)(2,1)S(1)}, u32[]{:S(2)}, u32[]{:S(2)}) collective-permute-start(bf16[1008,128]{1,0:T(8,128)(2,1)S(1)} %get-tuple-element.48), channel_id=1, source_target_pairs={{1,509},{3,511},{129,125},{131,127},{257,253},{259,255},{385,381},... | collective-permute-start | bytes 774152 | tf_op jit(solution)/shard_map/ppermute | solution.py:530
  28.8 5.2 %shard_map.156 = (f32[144,896]{1,0:T(8,128)S(1)}, s32[144,256]{1,0:T(8,128)S(1)}, s32[144,256]{1,0:T(8,128)S(1)}) custom-call(s32[144,144]{1,0:T(8,128)S(1)} %copy-done.5, f32[6,1,3312]{2,1,0:T(1,128)S(1)} %bitcast.14), custom_call_target="tpu_custom_call" | custom-call | flops 6000000000 | bytes 1000000 | tf_op jit(solution)/shard_map/pallas_call | solution.py:463
  35.5 6.0 %shard_map.157 = (bf16[288,192]{1,0:T(8,128)(2,1)S(1)}, bf16[288,192]{1,0:T(8,128)(2,1)S(1)}, bf16[432,128]{1,0:T(8,128)(2,1)S(1)}, bf16[432,128]{1,0:T(8,128)(2...) custom-call(bf16[288,192]{1,0:T(8,128)(2,1)S(1)} %bitcast.12, ...), custom_call_target="tpu_custom_call" | custom-call | flops 6000000000 | bytes 1000000 | tf_op jit(solution)/shard_map/pallas_call | solution.py:463
  41.5 5.9 %all-to-all-start = ((bf16[32,40,128]{2,1,0:T(8,128)(2,1)}), bf16[32,40,128]{2,1,0:T(8,128)(2,1)S(1)}, u32[]{:S(2)}, u32[]{:S(2)}) async-start(bf16[32,40,128]{2,1,0:T(8,128)(2,1)} %bitcast.5), calls=%async_computation | async-start | bytes 655360 | tf_op jit(solution)/shard_map/all_to_all | solution.py:571
  47.4 6.8 %shard_map.158.own = bf16[816,128]{1,0:T(8,128)(2,1)S(1)} custom-call(f32[144,896]{1,0:T(8,128)S(1)} %get-tuple-element.58.d_bias, s32[144,256]{1,0:T(8,128)S(1)} %get-tuple-element.59.hi, s32[144,256]{1,0:T(8,128)S(1)} %get-tuple-element.60.lo, bf16[224,128]{1,0:T(8,128)(2,1)S(1)} %get-tuple-element.61.edge, bf16[432,128]{1,0:T(8,128)(2,1)S(1)} %get-tuple-element.62.lat), custom_call_target="tpu_custom_call" | custom-call | flops 8000000000 | bytes 1000000 | tf_op jit(solution)/shard_map/pallas_call | solution.py:463
  54.2 2.9 %all-to-all-done.parts = bf16[32,40,128]{2,1,0:T(8,128)(2,1)S(1)} async-done(((bf16[32,40,128]{2,1,0:T(8,128)(2,1)}), bf16[32,40,128]{2,1,0:T(8,128)(2,1)S(1)}, u32[]{:S(2)}, u32[]{:S(2)}) %all-to-all-start) | async-done | bytes 327712 | tf_op jit(solution)/shard_map/all_to_all | solution.py:571
  57.8 10.2 %all-to-all-start.1 = ((bf16[16,40,128]{2,1,0:T(8,128)(2,1)}), bf16[16,40,128]{2,1,0:T(8,128)(2,1)S(1)}, u32[]{:S(2)}, u32[]{:S(2)}) async-start(bf16[16,40,128]{2,1,0:T(8,128)(2,1)} %shard_map.159), calls=%async_computation.1 | async-start | bytes 327680 | tf_op jit(solution)/shard_map/all_to_all | solution.py:586
  68.0 2.2 %collective-permute-start.6 = (bf16[816,128]{1,0:T(8,128)(2,1)S(1)}, bf16[816,128]{1,0:T(8,128)(2,1)S(1)}, u32[]{:S(2)}, u32[]{:S(2)}) collective-permute-start(bf16[816,128]{1,0:T(8,128)(2,1)S(1)} %shard_map.158.own), channel_id=1, source_target_pairs={{0,1},{1,0},{2,3},{3,2},{4,5},{5,4},{6,7},{7,6},{8,9},{9,8},{10,11... | collective-permute-start | bytes 626696 | tf_op jit(solution)/shard_map/ppermute | solution.py:584
  70.2 1.1 %collective-permute-done.6.near = bf16[816,128]{1,0:T(8,128)(2,1)S(1)} collective-permute-done((bf16[816,128]{1,0:T(8,128)(2,1)S(1)}, bf16[816,128]{1,0:T(8,128)(2,1)S(1)}, u32[]{:S(2)}, u32[]{:S(2)}) %collective-permute-start.6) | collective-permute-done | bytes 208928 | tf_op jit(solution)/shard_map/ppermute | solution.py:584
  71.4 12.4 %collective-permute-start.7 = (bf16[384,128]{1,0:T(8,128)(2,1)S(1)}, bf16[384,128]{1,0:T(8,128)(2,1)S(1)}, u32[]{:S(2)}, u32[]{:S(2)}) collective-permute-start(bf16[384,128]{1,0:T(8,128)(2,1)S(1)} %shard_map.160.pair), channel_id=1, source_target_pairs={{1,2},{3,0},{5,6},{7,4},{9,10},{11,8},{13,14},{15,12},{17,18},{19,... | collective-permute-start | bytes 294920 | tf_op jit(solution)/shard_map/ppermute | solution.py:588
  84.5 0.8 shard_map.162
  85.3 4.7 %all-to-all-start.2 = ((bf16[32,40,128]{2,1,0:T(8,128)(2,1)}), bf16[32,40,128]{2,1,0:T(8,128)(2,1)S(1)}, u32[]{:S(2)}, u32[]{:S(2)}) async-start(bf16[32,40,128]{2,1,0:T(8,128)(2,1)} %shard_map.162), calls=%async_computation.2 | async-start | bytes 655360 | tf_op jit(solution)/shard_map/all_to_all | solution.py:593
  90.5 1.3 %collective-permute-start.10 = (bf16[160,128]{1,0:T(8,128)(2,1)S(1)}, bf16[160,128]{1,0:T(8,128)(2,1)S(1)}, u32[]{:S(2)}, u32[]{:S(2)}) collective-permute-start(bf16[160,128]{1,0:T(8,128)(2,1)S(1)} %get-tuple-element.75.own), channel_id=1, source_target_pairs={{0,1},{2,3},{4,5},{6,7},{8,9},{10,11},{12,13},{14,15},{16,17},{18,... | collective-permute-start | bytes 122888 | tf_op jit(solution)/shard_map/ppermute | solution.py:614
  91.8 3.3 %collective-permute-start.8 = (bf16[448,128]{1,0:T(8,128)(2,1)S(1)}, bf16[448,128]{1,0:T(8,128)(2,1)S(1)}, u32[]{:S(2)}, u32[]{:S(2)}) collective-permute-start(bf16[448,128]{1,0:T(8,128)(2,1)S(1)} %get-tuple-element.74), channel_id=1, source_target_pairs={{0,4},{1,5},{2,6},{3,7},{4,8},{5,9},{6,10},{7,11},{8,12},{9,13},{1... | collective-permute-start | bytes 344072 | tf_op jit(solution)/shard_map/ppermute | solution.py:613
  95.1 1.3 %collective-permute-start.11 = (bf16[432,128]{1,0:T(8,128)(2,1)S(1)}, bf16[432,128]{1,0:T(8,128)(2,1)S(1)}, u32[]{:S(2)}, u32[]{:S(2)}) collective-permute-start(bf16[432,128]{1,0:T(8,128)(2,1)S(1)} %shard_map.165), channel_id=1, source_target_pairs={{0,1},{2,3},{128,129},{130,131},{256,257},{258,259},{384,385},{386... | collective-permute-start | bytes 331784 | tf_op jit(solution)/shard_map/ppermute | solution.py:617
  96.4 3.3 %all-to-all-done.2 = bf16[32,40,128]{2,1,0:T(8,128)(2,1)S(1)} async-done(((bf16[32,40,128]{2,1,0:T(8,128)(2,1)}), bf16[32,40,128]{2,1,0:T(8,128)(2,1)S(1)}, u32[]{:S(2)}, u32[]{:S(2)}) %all-to-all-start.2) | async-done | bytes 327712 | tf_op jit(solution)/shard_map/all_to_all | solution.py:593
  99.7 0.9 shard_map.163
  100.7 0.8 shard_map.166
  (45 shorter events, 3.4 us)
Async XLA Ops:
  2.5 26.2 %copy-start.5 = (s32[144,144]{1,0:T(8,128)S(1)}, s32[144,144]{1,0:T(8,128)}, u32[]{:S(2)}) copy-start(s32[144,144]{1,0:T(8,128)} %pos.1) | copy-start | bytes 248836
  2.6 11.5 %collective-permute-start = (bf16[432,128]{1,0:T(8,128)(2,1)S(1)}, bf16[432,128]{1,0:T(8,128)(2,1)S(1)}, u32[]{:S(2)}, u32[]{:S(2)}) collective-permute-start(bf16[432,128]{1,0:T(8,128)(2,1)S(1)} %get-tuple-element.45), channel_id=1, source_target_pairs={{0,1},{1,0},{2,3},{3,2},{4,5},{5,4},{6,7},{7,6},{8,9},{9,8},{10,11... | collective-permute-start | bytes 331784 | tf_op jit(solution)/shard_map/ppermute | solution.py:518
  11.5 22.6 %collective-permute-start.3 = (bf16[144,128]{1,0:T(8,128)(2,1)S(1)}, bf16[144,128]{1,0:T(8,128)(2,1)S(1)}, u32[]{:S(2)}, u32[]{:S(2)}) collective-permute-start(bf16[144,128]{1,0:T(8,128)(2,1)S(1)} %get-tuple-element.47.corner), channel_id=1, source_target_pairs={{0,511},{2,509},{4,3},{6,1},{8,7},{10,5},{12,11},{14,9},{16,15},{1... | collective-permute-start | bytes 110600 | tf_op jit(solution)/shard_map/ppermute | solution.py:520
  12.8 21.3 %collective-permute-start.2 = (bf16[288,128]{1,0:T(8,128)(2,1)S(1)}, bf16[288,128]{1,0:T(8,128)(2,1)S(1)}, u32[]{:S(2)}, u32[]{:S(2)}) collective-permute-start(bf16[288,128]{1,0:T(8,128)(2,1)S(1)} %get-tuple-element.49), channel_id=1, source_target_pairs={{0,3},{2,1},{4,7},{6,5},{8,11},{10,9},{12,15},{14,13},{16,19},{18,... | collective-permute-start | bytes 221192 | tf_op jit(solution)/shard_map/ppermute | solution.py:519
  14.1 14.6 %copy-start.7 = (f32[1,6,3312]{2,0,1:T(1,128)S(1)}, f32[1,6,3312]{2,0,1:T(1,128)}, u32[]{:S(2)}) copy-start(f32[1,6,3312]{2,0,1:T(1,128)} %param.17) | copy-start | bytes 238468
  14.2 19.9 %collective-permute-start.4 = (bf16[576,128]{1,0:T(8,128)(2,1)S(1)}, bf16[576,128]{1,0:T(8,128)(2,1)S(1)}, u32[]{:S(2)}, u32[]{:S(2)}) collective-permute-start(bf16[576,128]{1,0:T(8,128)(2,1)S(1)} %get-tuple-element.50), channel_id=1, source_target_pairs={{4,0},{5,1},{6,2},{7,3},{8,4},{9,5},{10,6},{11,7},{12,8},{13,9},{1... | collective-permute-start | bytes 442376 | tf_op jit(solution)/shard_map/ppermute | solution.py:529
  15.5 18.6 %collective-permute-start.1 = (bf16[1008,128]{1,0:T(8,128)(2,1)S(1)}, bf16[1008,128]{1,0:T(8,128)(2,1)S(1)}, u32[]{:S(2)}, u32[]{:S(2)}) collective-permute-start(bf16[1008,128]{1,0:T(8,128)(2,1)S(1)} %get-tuple-element.48), channel_id=1, source_target_pairs={{1,509},{3,511},{129,125},{131,127},{257,253},{259,255},{385,381},... | collective-permute-start | bytes 774152 | tf_op jit(solution)/shard_map/ppermute | solution.py:530
  28.7 6.1 %copy-start.1 = (bf16[2,6,24,192]{3,2,1,0:T(8,128)(2,1)S(1)}, bf16[2,6,24,192]{3,2,1,0:T(8,128)(2,1)}, u32[]{:S(2)}) copy-start(bf16[2,6,24,192]{3,2,1,0:T(8,128)(2,1)} %tokens.1) | copy-start | bytes 331780
  28.8 6.1 %copy-start.3 = (bf16[2,6,24,192]{3,2,1,0:T(8,128)(2,1)S(1)}, bf16[2,6,24,192]{3,2,1,0:T(8,128)(2,1)}, u32[]{:S(2)}) copy-start(bf16[2,6,24,192]{3,2,1,0:T(8,128)(2,1)} %d_out.1) | copy-start | bytes 331780
  28.8 6.1 %copy-start.4 = (bf16[192,576]{1,0:T(8,128)(2,1)S(1)}, bf16[192,576]{1,0:T(8,128)(2,1)}, u32[]{:S(2)}) copy-start(bf16[192,576]{1,0:T(8,128)(2,1)} %w_qkv.1) | copy-start | bytes 663556
  28.8 6.1 %copy-start.6 = (bf16[192,192]{1,0:T(8,128)(2,1)S(1)}, bf16[192,192]{1,0:T(8,128)(2,1)}, u32[]{:S(2)}) copy-start(bf16[192,192]{1,0:T(8,128)(2,1)} %wp.1) | copy-start | bytes 221188
  28.8 6.1 %copy-start.10 = (bf16[2,648,144]{2,1,0:T(8,128)(2,1)S(1)}, bf16[2,648,144]{2,1,0:T(8,128)(2,1)}, u32[]{:S(2)}) copy-start(bf16[2,648,144]{2,1,0:T(8,128)(2,1)} %constant.7.clone.back) | copy-start | bytes 1119748
  28.8 6.1 %copy-start.11 = (bf16[2,144,528]{2,1,0:T(8,128)(2,1)S(1)}, bf16[2,144,528]{2,1,0:T(8,128)(2,1)}, u32[]{:S(2)}) copy-start(bf16[2,144,528]{2,1,0:T(8,128)(2,1)} %constant.6.clone.pick) | copy-start | bytes 912388
  34.1 0.7 collective-permute-start.5
  41.5 15.5 %all-to-all-start = ((bf16[32,40,128]{2,1,0:T(8,128)(2,1)}), bf16[32,40,128]{2,1,0:T(8,128)(2,1)S(1)}, u32[]{:S(2)}, u32[]{:S(2)}) async-start(bf16[32,40,128]{2,1,0:T(8,128)(2,1)} %bitcast.5), calls=%async_computation | async-start | bytes 655360 | tf_op jit(solution)/shard_map/all_to_all | solution.py:571
  57.8 26.7 %all-to-all-start.1 = ((bf16[16,40,128]{2,1,0:T(8,128)(2,1)}), bf16[16,40,128]{2,1,0:T(8,128)(2,1)S(1)}, u32[]{:S(2)}, u32[]{:S(2)}) async-start(bf16[16,40,128]{2,1,0:T(8,128)(2,1)} %shard_map.159), calls=%async_computation.1 | async-start | bytes 327680 | tf_op jit(solution)/shard_map/all_to_all | solution.py:586
  68.0 3.4 %collective-permute-start.6 = (bf16[816,128]{1,0:T(8,128)(2,1)S(1)}, bf16[816,128]{1,0:T(8,128)(2,1)S(1)}, u32[]{:S(2)}, u32[]{:S(2)}) collective-permute-start(bf16[816,128]{1,0:T(8,128)(2,1)S(1)} %shard_map.158.own), channel_id=1, source_target_pairs={{0,1},{1,0},{2,3},{3,2},{4,5},{5,4},{6,7},{7,6},{8,9},{9,8},{10,11... | collective-permute-start | bytes 626696 | tf_op jit(solution)/shard_map/ppermute | solution.py:584
  71.4 18.7 %collective-permute-start.7 = (bf16[384,128]{1,0:T(8,128)(2,1)S(1)}, bf16[384,128]{1,0:T(8,128)(2,1)S(1)}, u32[]{:S(2)}, u32[]{:S(2)}) collective-permute-start(bf16[384,128]{1,0:T(8,128)(2,1)S(1)} %shard_map.160.pair), channel_id=1, source_target_pairs={{1,2},{3,0},{5,6},{7,4},{9,10},{11,8},{13,14},{15,12},{17,18},{19,... | collective-permute-start | bytes 294920 | tf_op jit(solution)/shard_map/ppermute | solution.py:588
  83.8 11.3 %collective-permute-start.9 = (bf16[864,128]{1,0:T(8,128)(2,1)S(1)}, bf16[864,128]{1,0:T(8,128)(2,1)S(1)}, u32[]{:S(2)}, u32[]{:S(2)}) collective-permute-start(bf16[864,128]{1,0:T(8,128)(2,1)S(1)} %shard_map.164), channel_id=1, source_target_pairs={{124,128},{126,130},{252,256},{254,258},{380,384},{382,386},{508,0... | collective-permute-start | bytes 663560 | tf_op jit(solution)/shard_map/ppermute | solution.py:590
  85.3 4.8 %copy-start.12 = (bf16[432,72]{1,0:T(8,128)(2,1)S(1)}, bf16[432,72]{1,0:T(8,128)(2,1)}, u32[]{:S(2)}) copy-start(bf16[432,72]{1,0:T(8,128)(2,1)} %constant.8.clone.place) | copy-start | bytes 186628
  85.3 14.4 %all-to-all-start.2 = ((bf16[32,40,128]{2,1,0:T(8,128)(2,1)}), bf16[32,40,128]{2,1,0:T(8,128)(2,1)S(1)}, u32[]{:S(2)}, u32[]{:S(2)}) async-start(bf16[32,40,128]{2,1,0:T(8,128)(2,1)} %shard_map.162), calls=%async_computation.2 | async-start | bytes 655360 | tf_op jit(solution)/shard_map/all_to_all | solution.py:593
  90.5 4.6 %collective-permute-start.10 = (bf16[160,128]{1,0:T(8,128)(2,1)S(1)}, bf16[160,128]{1,0:T(8,128)(2,1)S(1)}, u32[]{:S(2)}, u32[]{:S(2)}) collective-permute-start(bf16[160,128]{1,0:T(8,128)(2,1)S(1)} %get-tuple-element.75.own), channel_id=1, source_target_pairs={{0,1},{2,3},{4,5},{6,7},{8,9},{10,11},{12,13},{14,15},{16,17},{18,... | collective-permute-start | bytes 122888 | tf_op jit(solution)/shard_map/ppermute | solution.py:614
  91.8 8.9 %collective-permute-start.8 = (bf16[448,128]{1,0:T(8,128)(2,1)S(1)}, bf16[448,128]{1,0:T(8,128)(2,1)S(1)}, u32[]{:S(2)}, u32[]{:S(2)}) collective-permute-start(bf16[448,128]{1,0:T(8,128)(2,1)S(1)} %get-tuple-element.74), channel_id=1, source_target_pairs={{0,4},{1,5},{2,6},{3,7},{4,8},{5,9},{6,10},{7,11},{8,12},{9,13},{1... | collective-permute-start | bytes 344072 | tf_op jit(solution)/shard_map/ppermute | solution.py:613
  95.1 5.5 %collective-permute-start.11 = (bf16[432,128]{1,0:T(8,128)(2,1)S(1)}, bf16[432,128]{1,0:T(8,128)(2,1)S(1)}, u32[]{:S(2)}, u32[]{:S(2)}) collective-permute-start(bf16[432,128]{1,0:T(8,128)(2,1)S(1)} %shard_map.165), channel_id=1, source_target_pairs={{0,1},{2,3},{128,129},{130,131},{256,257},{258,259},{384,385},{386... | collective-permute-start | bytes 331784 | tf_op jit(solution)/shard_map/ppermute | solution.py:617
  (4 other events, 3.3 us)

commit v5 on v4

--- a/solution.py
+++ b/solution.py
@@ -39,7 +39,6 @@
 LAT_ROWS = 3 * N_LAT
 CORNER_ROWS = 3 * N_EDGE
 SIDE_ROWS = 2 * CORNER_ROWS
-LINE_ROWS = 2 * LAT_ROWS + CORNER_ROWS
 
 SPLIT = (4, 8, 4, 2, 2)
 AXES = ("x", "zl", "y", "zh", "c")
@@ -138,25 +137,27 @@
     return lax.broadcasted_iota(jnp.int32, (rows, 128), 0) * 0 + at == want
 
 
-def cut_kernel(tokens, d_out, to_core, lat, edge, to_diag):
+def cut_kernel(tokens, d_out, to_core, lat, to_lon, to_diag):
     both = (tokens[...].astype(F32), d_out[...].astype(F32))
     top = fold(*(a[:, :HALF_LAT].reshape(N_LAT, C) for a in both))
     corner = fold(*(a[:, :HALF_LAT, :EDGE].reshape(N_EDGE, C) for a in both))
     lon = fold(*(a[:, HALF_LAT:, :EDGE].reshape(N_EDGE, C) for a in both))
     side = jnp.concatenate([corner, lon], axis=0)
     lat[...] = top.astype(BF)
-    edge[...] = side.astype(BF)
+    to_lon[...] = lon.astype(BF)
     to_diag[...] = corner.astype(BF)
     spare = jnp.zeros((LAT_ROWS - SIDE_ROWS, 128), F32)
     to_core[...] = jnp.where(core_is(1, LAT_ROWS), jnp.concatenate([side, spare], axis=0), top).astype(BF)
 
 
-def join_kernel(lat, corner, sibling, to_lat, to_line):
+def join_kernel(lat, sibling, to_lat):
     to_lat[:LAT_ROWS, :] = lat[...]
     to_lat[LAT_ROWS:, :] = sibling[:CORNER_ROWS, :]
-    to_line[:LAT_ROWS, :] = lat[...]
-    to_line[LAT_ROWS : 2 * LAT_ROWS, :] = sibling[...]
-    to_line[2 * LAT_ROWS :, :] = corner[...]
+
+
+def border_kernel(lon, diag, to_lon, to_diag):
+    to_lon[...] = lon[...]
+    to_diag[...] = diag[...]
 
 
 def tables_kernel(pos, table, bias, hi_out, lo_out, scr):
@@ -267,18 +268,15 @@
 
 
 def block_kernel(
-    own_x, own_d, sibling, from_lon, from_lat, from_line, from_side, from_diag, pick, back, gain, w_qkv, wp, mask, bias,
+    own_x, own_d, sibling, from_lon, from_lat, from_diag, pick, back, gain, w_qkv, wp, mask, bias,
     base_x, base_d, out_lat, out_corner, out_edge, grads, d_bias,
 ):
     f32 = lambda ref, start, size: ref[start : start + size, :].astype(F32)
-    over = f32(from_line, 0, LAT_ROWS) + f32(from_side, LAT_ROWS, LAT_ROWS)
-    lat = unfold(jnp.where(band_is(False, LAT_ROWS), over, f32(from_lat, 0, LAT_ROWS)), N_LAT)
-    lon = f32(sibling, CORNER_ROWS, CORNER_ROWS), f32(from_lon, CORNER_ROWS, CORNER_ROWS)
+    lat = unfold(f32(from_lat, 0, LAT_ROWS), N_LAT)
+    lon = f32(sibling, CORNER_ROWS, CORNER_ROWS), f32(from_lon, 0, CORNER_ROWS)
     lon = unfold(jnp.where(core_is(0, CORNER_ROWS), *lon), N_EDGE)
-    inner = jnp.where(
-        band_is(False, CORNER_ROWS), f32(from_side, 2 * LAT_ROWS, CORNER_ROWS), f32(from_lat, LAT_ROWS, CORNER_ROWS)
-    )
-    diag = unfold(jnp.where(core_is(0, CORNER_ROWS), inner, f32(from_diag, 0, CORNER_ROWS)), N_EDGE)
+    diag = f32(from_lat, LAT_ROWS, CORNER_ROWS), f32(from_diag, 0, CORNER_ROWS)
+    diag = unfold(jnp.where(core_is(0, CORNER_ROWS), *diag), N_EDGE)
     x_all, d_all = (
         jnp.concatenate([own[...], lat[i].astype(BF), lon[i].astype(BF), diag[i].astype(BF)], axis=0)
         for i, own in enumerate((own_x, own_d))
@@ -504,30 +502,24 @@
 
     def per_device(tokens, mask_ids, pos_index, norm_gain, w_qkv, w_proj, earth_bias, d_out):
         pick, back, place = (jnp.asarray(c) for c in constants())
-        to_core, lat, edge, to_diag = call(
+        to_core, lat, to_lon, to_diag = call(
             cut_kernel,
             (
                 sds((LAT_ROWS, 128), BF),
                 sds((LAT_ROWS, 128), BF),
-                sds((SIDE_ROWS, 128), BF),
+                sds((CORNER_ROWS, 128), BF),
                 sds((CORNER_ROWS, 128), BF),
             ),
             tokens,
             d_out,
         )
         sibling = lax.ppermute(to_core, AXES, hop(lambda zh, c: (zh, 1 - c), (0, 1)))
-        from_lon = lax.ppermute(edge, AXES, hop(lambda zh, c: (1 - zh, 1), (0,)))
+        to_lat = call(join_kernel, sds((LAT_ROWS + CORNER_ROWS, 128), BF), lat, sibling)
+        from_lat = lax.ppermute(to_lat, AXES, route(-1, 0))
+        to_lat, to_lon, to_diag = lax.optimization_barrier((to_lat, to_lon, to_diag))
+        to_lon, to_diag = call(border_kernel, (sds((CORNER_ROWS, 128), BF), sds((CORNER_ROWS, 128), BF)), to_lon, to_diag, cost=(10**10, 10**6))
+        from_lon = lax.ppermute(to_lon, AXES, hop(lambda zh, c: (1 - zh, 1), (0,)))
         from_diag = lax.ppermute(to_diag, AXES, [r for r in route(-1, -1) if r[0] % sizes[4] == 0])
-        to_lat, to_line = call(
-            join_kernel,
-            (sds((LAT_ROWS + CORNER_ROWS, 128), BF), sds((LINE_ROWS, 128), BF)),
-            lat,
-            to_diag,
-            sibling,
-        )
-        south = route(-1, 0)
-        from_lat = lax.ppermute(to_lat, AXES, [r for r in south if not first(r)])
-        from_line = lax.ppermute(to_line, AXES, [r for r in south if first(r) and r[0] % sizes[4] == 1])
         bias, hi, lo = call(
             tables_kernel,
             (sds((WIN, PAIRS), F32), sds((WIN, 256), jnp.int32), sds((WIN, 256), jnp.int32)),
@@ -536,9 +528,8 @@
             scratch=[pltpu.VMEM((HEADS // 2, HI * 128), jnp.int32)],
             cost=(6 * 10**9, 10**6),
         )
-        received = (from_line, from_lon, from_diag, from_lat, bias)
-        from_line, from_lon, from_diag, from_lat, bias = lax.optimization_barrier(received)
-        from_side = lax.ppermute(from_line, AXES, [r for r in hop(lambda zh, c: (zh, 0), (1,)) if last(r)])
+        from_lat, bias = lax.optimization_barrier((from_lat, bias))
+        from_lon, from_diag, bias = lax.optimization_barrier((from_lon, from_diag, bias))
         base_x, base_d, out_lat, out_corner, out_edge, grads, d_bias = call(
             block_kernel,
             (
@@ -555,8 +546,6 @@
             sibling,
             from_lon,
             from_lat,
-            from_line,
-            from_side,
             from_diag,
             pick,
             back,

time: 103 us -> 103 us (level)
  starting transfers between devices: 68.7 us -> 60.6 us
  waiting for transfers between devices: 7.36 us -> 15.3 us
    ppermute x4 -> x2, waiting for transfers between devices: 0.01 us -> 7.07 us  [the longest x1 7.07 us: per_device(): from_lon = lax.ppermute(to_lon, AXES, hop(lambda zh, c: (1 - zh, 1), (0,)))]
    ppermute x4 -> x2, starting transfers between devices: 16.5 us -> 13.6 us  [the longest x1 12.2 us: per_device(): from_lat = lax.ppermute(to_lat, AXES, route(-1, 0))]
    all_to_all x1, starting transfers between devices: 10.2 us -> 7.32 us  [per_device(): line = lax.all_to_all(part, LINE, 0, 0)]
    all_to_all x1, starting transfers between devices: 5.88 us -> 3.66 us  [per_device(): parts = lax.all_to_all(grads.reshape(n_plane, piece, 128), PLANE, 0, 0)]
    all_to_all x1, waiting for transfers between devices: 2.88 us -> 1.37 us  [per_device(): parts = lax.all_to_all(grads.reshape(n_plane, piece, 128), PLANE, 0, 0)]
    ppermute x1, waiting for transfers between devices: 0.01 us -> 1.49 us  [per_device(): lax.ppermute(to_diag, AXES, [r for r in route(-1, -1) if r[0] % sizes[4]...]
    pallas_call x13 -> x14, Pallas kernels: 21.9 us -> 21.9 us  [call(): pl.pallas_call(kernel, out_shape=out_shape, scratch_shapes=list(scratch),...]
  transfers between devices with their start and end apart: 15 -> 13, of which waited for: 3 -> 6; matrix products, arithmetic and copies ran while one was open for 0% -> 0% of each run, Pallas kernels for 14% -> 14%
where the time goes in v5:
time: 103 us; the launch traced here: 101 us
  starting transfers between devices  60.6 us (59%)
  Pallas kernels  21.9 us (21%)
  waiting for transfers between devices  15.3 us (15%)
  local copies, waits for them, and re-layouts  2.5 us (2%)
    pallas_call x14, Pallas kernels, call(): pl.pallas_call(kernel, out_shape=out_shape, scratch_shapes=list(scratch),...  21.9 us
    ppermute x1, starting transfers between devices, per_device(): far = lax.ppermute(pair, AXES, hop(lambda zh, c: (1 - zh, 0), (1,)))  12.4 us
    ppermute x1, starting transfers between devices, per_device(): from_lat = lax.ppermute(to_lat, AXES, route(-1, 0))  12.2 us
    ppermute x1, starting transfers between devices, per_device(): lax.ppermute(to_core, AXES, hop(lambda zh, c: (zh, 1 - c), (0, 1)))  8.79 us
    all_to_all x1, starting transfers between devices, per_device(): line = lax.all_to_all(part, LINE, 0, 0)  7.32 us
    ppermute x1, waiting for transfers between devices, per_device(): from_lon = lax.ppermute(to_lon, AXES, hop(lambda zh, c: (1 - zh, 1), (0,)))  7.07 us
    all_to_all x1, starting transfers between devices, per_device(): whole = lax.all_to_all(total, PLANE, 0, 0)  4.75 us
    all_to_all x1, starting transfers between devices, per_device(): parts = lax.all_to_all(grads.reshape(n_plane, piece, 128), PLANE, 0, 0)  3.66 us
  transfers between devices with their start and end apart: 13, of which 6 were waited for; matrix products, arithmetic and copies ran while one was open for 0% of the time, Pallas kernels for 14%

profile of v5, /device:TPU:1, one launch (start us, length us, event | category | flops | bytes accessed | tf_op | source)
XLA Modules:
  0.0 101.2 jit_solution(4379425984323365703)
XLA Ops:
  0.6 0.9 copy-done
  1.5 0.9 copy-done.2
  2.5 8.8 %collective-permute-start = (bf16[432,128]{1,0:T(8,128)(2,1)S(1)}, bf16[432,128]{1,0:T(8,128)(2,1)S(1)}, u32[]{:S(2)}, u32[]{:S(2)}) collective-permute-start(bf16[432,128]{1,0:T(8,128)(2,1)S(1)} %get-tuple-element.47), channel_id=1, source_target_pairs={{0,1},{1,0},{2,3},{3,2},{4,5},{5,4},{6,7},{7,6},{8,9},{9,8},{10,11... | collective-permute-start | bytes 331784 | tf_op jit(solution)/shard_map/ppermute | solution.py:516
  11.3 0.9 collective-permute-done.sibling
  12.3 12.2 %collective-permute-start.3 = (bf16[576,128]{1,0:T(8,128)(2,1)S(1)}, bf16[576,128]{1,0:T(8,128)(2,1)S(1)}, u32[]{:S(2)}, u32[]{:S(2)}) collective-permute-start(bf16[576,128]{1,0:T(8,128)(2,1)S(1)} %shard_map.155), channel_id=1, source_target_pairs={{0,508},{1,509},{2,510},{3,511},{4,0},{5,1},{6,2},{7,3},{8,4},{9,5... | collective-permute-start | bytes 442376 | tf_op jit(solution)/shard_map/ppermute | solution.py:518
  24.5 1.4 %collective-permute-start.1 = (bf16[144,128]{1,0:T(8,128)(2,1)S(1)}, bf16[144,128]{1,0:T(8,128)(2,1)S(1)}, u32[]{:S(2)}, u32[]{:S(2)}) collective-permute-start(bf16[144,128]{1,0:T(8,128)(2,1)S(1)} %get-tuple-element.53), channel_id=1, source_target_pairs={{0,3},{2,1},{4,7},{6,5},{8,11},{10,9},{12,15},{14,13},{16,19},{18,... | collective-permute-start | bytes 110600 | tf_op jit(solution)/shard_map/ppermute | solution.py:521
  25.9 1.3 %collective-permute-start.2 = (bf16[144,128]{1,0:T(8,128)(2,1)S(1)}, bf16[144,128]{1,0:T(8,128)(2,1)S(1)}, u32[]{:S(2)}, u32[]{:S(2)}) collective-permute-start(bf16[144,128]{1,0:T(8,128)(2,1)S(1)} %get-tuple-element.54), channel_id=1, source_target_pairs={{0,511},{2,509},{4,3},{6,1},{8,7},{10,5},{12,11},{14,9},{16,15},{1... | collective-permute-start | bytes 110600 | tf_op jit(solution)/shard_map/ppermute | solution.py:522
  27.3 5.2 %shard_map.157 = (f32[144,896]{1,0:T(8,128)S(1)}, s32[144,256]{1,0:T(8,128)S(1)}, s32[144,256]{1,0:T(8,128)S(1)}) custom-call(s32[144,144]{1,0:T(8,128)S(1)} %copy-done.5, f32[6,1,3312]{2,1,0:T(1,128)S(1)} %bitcast.14), custom_call_target="tpu_custom_call" | custom-call | flops 6000000000 | bytes 1000000 | tf_op jit(solution)/shard_map/pallas_call | solution.py:461
  32.6 7.1 %collective-permute-done.1.from_lon = bf16[144,128]{1,0:T(8,128)(2,1)S(1)} collective-permute-done((bf16[144,128]{1,0:T(8,128)(2,1)S(1)}, bf16[144,128]{1,0:T(8,128)(2,1)S(1)}, u32[]{:S(2)}, u32[]{:S(2)}) %collective-permute-start.1) | collective-permute-done | bytes 36896 | tf_op jit(solution)/shard_map/ppermute | solution.py:521
  39.6 1.5 %collective-permute-done.2.from_diag = bf16[144,128]{1,0:T(8,128)(2,1)S(1)} collective-permute-done((bf16[144,128]{1,0:T(8,128)(2,1)S(1)}, bf16[144,128]{1,0:T(8,128)(2,1)S(1)}, u32[]{:S(2)}, u32[]{:S(2)}) %collective-permute-start.2) | collective-permute-done | bytes 36896 | tf_op jit(solution)/shard_map/ppermute | solution.py:522
  41.8 6.1 %shard_map.158 = (bf16[288,192]{1,0:T(8,128)(2,1)S(1)}, bf16[288,192]{1,0:T(8,128)(2,1)S(1)}, bf16[432,128]{1,0:T(8,128)(2,1)S(1)}, bf16[432,128]{1,0:T(8,128)(2...) custom-call(bf16[288,192]{1,0:T(8,128)(2,1)S(1)} %bitcast.12, ...), custom_call_target="tpu_custom_call" | custom-call | flops 6000000000 | bytes 1000000 | tf_op jit(solution)/shard_map/pallas_call | solution.py:461
  47.9 3.7 %all-to-all-start = ((bf16[32,40,128]{2,1,0:T(8,128)(2,1)}), bf16[32,40,128]{2,1,0:T(8,128)(2,1)S(1)}, u32[]{:S(2)}, u32[]{:S(2)}) async-start(bf16[32,40,128]{2,1,0:T(8,128)(2,1)} %bitcast.5), calls=%async_computation | async-start | bytes 655360 | tf_op jit(solution)/shard_map/all_to_all | solution.py:560
  51.5 6.8 %shard_map.159.own = bf16[816,128]{1,0:T(8,128)(2,1)S(1)} custom-call(f32[144,896]{1,0:T(8,128)S(1)} %get-tuple-element.62.d_bias, s32[144,256]{1,0:T(8,128)S(1)} %get-tuple-element.63.hi, s32[144,256]{1,0:T(8,128)S(1)} %get-tuple-element.64.lo, bf16[224,128]{1,0:T(8,128)(2,1)S(1)} %get-tuple-element.65.edge, bf16[432,128]{1,0:T(8,128)(2,1)S(1)} %get-tuple-element.66.lat), custom_call_target="tpu_custom_call" | custom-call | flops 8000000000 | bytes 1000000 | tf_op jit(solution)/shard_map/pallas_call | solution.py:461
  58.3 1.4 %all-to-all-done.parts = bf16[32,40,128]{2,1,0:T(8,128)(2,1)S(1)} async-done(((bf16[32,40,128]{2,1,0:T(8,128)(2,1)}), bf16[32,40,128]{2,1,0:T(8,128)(2,1)S(1)}, u32[]{:S(2)}, u32[]{:S(2)}) %all-to-all-start) | async-done | bytes 327712 | tf_op jit(solution)/shard_map/all_to_all | solution.py:560
  60.4 7.3 %all-to-all-start.1 = ((bf16[16,40,128]{2,1,0:T(8,128)(2,1)}), bf16[16,40,128]{2,1,0:T(8,128)(2,1)S(1)}, u32[]{:S(2)}, u32[]{:S(2)}) async-start(bf16[16,40,128]{2,1,0:T(8,128)(2,1)} %shard_map.160), calls=%async_computation.1 | async-start | bytes 327680 | tf_op jit(solution)/shard_map/all_to_all | solution.py:575
  67.7 2.2 %collective-permute-start.4 = (bf16[816,128]{1,0:T(8,128)(2,1)S(1)}, bf16[816,128]{1,0:T(8,128)(2,1)S(1)}, u32[]{:S(2)}, u32[]{:S(2)}) collective-permute-start(bf16[816,128]{1,0:T(8,128)(2,1)S(1)} %shard_map.159.own), channel_id=1, source_target_pairs={{0,1},{1,0},{2,3},{3,2},{4,5},{5,4},{6,7},{7,6},{8,9},{9,8},{10,11... | collective-permute-start | bytes 626696 | tf_op jit(solution)/shard_map/ppermute | solution.py:573
  69.9 1.1 %collective-permute-done.4.near = bf16[816,128]{1,0:T(8,128)(2,1)S(1)} collective-permute-done((bf16[816,128]{1,0:T(8,128)(2,1)S(1)}, bf16[816,128]{1,0:T(8,128)(2,1)S(1)}, u32[]{:S(2)}, u32[]{:S(2)}) %collective-permute-start.4) | collective-permute-done | bytes 208928 | tf_op jit(solution)/shard_map/ppermute | solution.py:573
  71.1 12.4 %collective-permute-start.5 = (bf16[384,128]{1,0:T(8,128)(2,1)S(1)}, bf16[384,128]{1,0:T(8,128)(2,1)S(1)}, u32[]{:S(2)}, u32[]{:S(2)}) collective-permute-start(bf16[384,128]{1,0:T(8,128)(2,1)S(1)} %shard_map.161.pair), channel_id=1, source_target_pairs={{1,2},{3,0},{5,6},{7,4},{9,10},{11,8},{13,14},{15,12},{17,18},{19,... | collective-permute-start | bytes 294920 | tf_op jit(solution)/shard_map/ppermute | solution.py:577
  85.1 4.7 %all-to-all-start.2 = ((bf16[32,40,128]{2,1,0:T(8,128)(2,1)}), bf16[32,40,128]{2,1,0:T(8,128)(2,1)S(1)}, u32[]{:S(2)}, u32[]{:S(2)}) async-start(bf16[32,40,128]{2,1,0:T(8,128)(2,1)} %shard_map.163), calls=%async_computation.2 | async-start | bytes 655360 | tf_op jit(solution)/shard_map/all_to_all | solution.py:582
  90.2 1.3 %collective-permute-start.8 = (bf16[160,128]{1,0:T(8,128)(2,1)S(1)}, bf16[160,128]{1,0:T(8,128)(2,1)S(1)}, u32[]{:S(2)}, u32[]{:S(2)}) collective-permute-start(bf16[160,128]{1,0:T(8,128)(2,1)S(1)} %get-tuple-element.79.own), channel_id=1, source_target_pairs={{0,1},{2,3},{4,5},{6,7},{8,9},{10,11},{12,13},{14,15},{16,17},{18,... | collective-permute-start | bytes 122888 | tf_op jit(solution)/shard_map/ppermute | solution.py:603
  91.5 3.3 %collective-permute-start.6 = (bf16[448,128]{1,0:T(8,128)(2,1)S(1)}, bf16[448,128]{1,0:T(8,128)(2,1)S(1)}, u32[]{:S(2)}, u32[]{:S(2)}) collective-permute-start(bf16[448,128]{1,0:T(8,128)(2,1)S(1)} %get-tuple-element.78), channel_id=1, source_target_pairs={{0,4},{1,5},{2,6},{3,7},{4,8},{5,9},{6,10},{7,11},{8,12},{9,13},{1... | collective-permute-start | bytes 344072 | tf_op jit(solution)/shard_map/ppermute | solution.py:602
  94.9 1.3 %collective-permute-start.9 = (bf16[432,128]{1,0:T(8,128)(2,1)S(1)}, bf16[432,128]{1,0:T(8,128)(2,1)S(1)}, u32[]{:S(2)}, u32[]{:S(2)}) collective-permute-start(bf16[432,128]{1,0:T(8,128)(2,1)S(1)} %shard_map.166), channel_id=1, source_target_pairs={{0,1},{2,3},{128,129},{130,131},{256,257},{258,259},{384,385},{386... | collective-permute-start | bytes 331784 | tf_op jit(solution)/shard_map/ppermute | solution.py:606
  96.2 3.3 %all-to-all-done.2 = bf16[32,40,128]{2,1,0:T(8,128)(2,1)S(1)} async-done(((bf16[32,40,128]{2,1,0:T(8,128)(2,1)}), bf16[32,40,128]{2,1,0:T(8,128)(2,1)S(1)}, u32[]{:S(2)}, u32[]{:S(2)}) %all-to-all-start.2) | async-done | bytes 327712 | tf_op jit(solution)/shard_map/all_to_all | solution.py:582
  99.5 0.9 shard_map.164
  (42 shorter events, 4.3 us)
Async XLA Ops:
  0.6 0.9 copy-start
  2.5 9.7 %collective-permute-start = (bf16[432,128]{1,0:T(8,128)(2,1)S(1)}, bf16[432,128]{1,0:T(8,128)(2,1)S(1)}, u32[]{:S(2)}, u32[]{:S(2)}) collective-permute-start(bf16[432,128]{1,0:T(8,128)(2,1)S(1)} %get-tuple-element.47), channel_id=1, source_target_pairs={{0,1},{1,0},{2,3},{3,2},{4,5},{5,4},{6,7},{7,6},{8,9},{9,8},{10,11... | collective-permute-start | bytes 331784 | tf_op jit(solution)/shard_map/ppermute | solution.py:516
  12.3 20.3 %collective-permute-start.3 = (bf16[576,128]{1,0:T(8,128)(2,1)S(1)}, bf16[576,128]{1,0:T(8,128)(2,1)S(1)}, u32[]{:S(2)}, u32[]{:S(2)}) collective-permute-start(bf16[576,128]{1,0:T(8,128)(2,1)S(1)} %shard_map.155), channel_id=1, source_target_pairs={{0,508},{1,509},{2,510},{3,511},{4,0},{5,1},{6,2},{7,3},{8,4},{9,5... | collective-permute-start | bytes 442376 | tf_op jit(solution)/shard_map/ppermute | solution.py:518
  24.5 2.8 %copy-start.5 = (s32[144,144]{1,0:T(8,128)S(1)}, s32[144,144]{1,0:T(8,128)}, u32[]{:S(2)}) copy-start(s32[144,144]{1,0:T(8,128)} %pos.1) | copy-start | bytes 248836
  24.5 2.8 %copy-start.7 = (f32[1,6,3312]{2,0,1:T(1,128)S(1)}, f32[1,6,3312]{2,0,1:T(1,128)}, u32[]{:S(2)}) copy-start(f32[1,6,3312]{2,0,1:T(1,128)} %param.17) | copy-start | bytes 238468
  24.5 15.2 %collective-permute-start.1 = (bf16[144,128]{1,0:T(8,128)(2,1)S(1)}, bf16[144,128]{1,0:T(8,128)(2,1)S(1)}, u32[]{:S(2)}, u32[]{:S(2)}) collective-permute-start(bf16[144,128]{1,0:T(8,128)(2,1)S(1)} %get-tuple-element.53), channel_id=1, source_target_pairs={{0,3},{2,1},{4,7},{6,5},{8,11},{10,9},{12,15},{14,13},{16,19},{18,... | collective-permute-start | bytes 110600 | tf_op jit(solution)/shard_map/ppermute | solution.py:521
  25.9 15.2 %collective-permute-start.2 = (bf16[144,128]{1,0:T(8,128)(2,1)S(1)}, bf16[144,128]{1,0:T(8,128)(2,1)S(1)}, u32[]{:S(2)}, u32[]{:S(2)}) collective-permute-start(bf16[144,128]{1,0:T(8,128)(2,1)S(1)} %get-tuple-element.54), channel_id=1, source_target_pairs={{0,511},{2,509},{4,3},{6,1},{8,7},{10,5},{12,11},{14,9},{16,15},{1... | collective-permute-start | bytes 110600 | tf_op jit(solution)/shard_map/ppermute | solution.py:522
  27.2 13.9 %copy-start.1 = (bf16[2,6,24,192]{3,2,1,0:T(8,128)(2,1)S(1)}, bf16[2,6,24,192]{3,2,1,0:T(8,128)(2,1)}, u32[]{:S(2)}) copy-start(bf16[2,6,24,192]{3,2,1,0:T(8,128)(2,1)} %tokens.1) | copy-start | bytes 331780
  27.3 13.9 %copy-start.3 = (bf16[2,6,24,192]{3,2,1,0:T(8,128)(2,1)S(1)}, bf16[2,6,24,192]{3,2,1,0:T(8,128)(2,1)}, u32[]{:S(2)}) copy-start(bf16[2,6,24,192]{3,2,1,0:T(8,128)(2,1)} %d_out.1) | copy-start | bytes 331780
  27.3 13.9 %copy-start.4 = (bf16[192,576]{1,0:T(8,128)(2,1)S(1)}, bf16[192,576]{1,0:T(8,128)(2,1)}, u32[]{:S(2)}) copy-start(bf16[192,576]{1,0:T(8,128)(2,1)} %w_qkv.1) | copy-start | bytes 663556
  27.3 13.9 %copy-start.6 = (bf16[192,192]{1,0:T(8,128)(2,1)S(1)}, bf16[192,192]{1,0:T(8,128)(2,1)}, u32[]{:S(2)}) copy-start(bf16[192,192]{1,0:T(8,128)(2,1)} %wp.1) | copy-start | bytes 221188
  27.3 13.9 %copy-start.10 = (bf16[2,648,144]{2,1,0:T(8,128)(2,1)S(1)}, bf16[2,648,144]{2,1,0:T(8,128)(2,1)}, u32[]{:S(2)}) copy-start(bf16[2,648,144]{2,1,0:T(8,128)(2,1)} %constant.7.clone.back) | copy-start | bytes 1119748
  27.3 13.9 %copy-start.11 = (bf16[2,144,528]{2,1,0:T(8,128)(2,1)S(1)}, bf16[2,144,528]{2,1,0:T(8,128)(2,1)}, u32[]{:S(2)}) copy-start(bf16[2,144,528]{2,1,0:T(8,128)(2,1)} %constant.6.clone.pick) | copy-start | bytes 912388
  32.6 8.6 %copy-start.8 = (s32[2,6,24]{2,0,1:T(2,128)S(1)}, s32[2,6,24]{2,0,1:T(2,128)}, u32[]{:S(2)}) copy-start(s32[2,6,24]{2,0,1:T(2,128)} %param.12) | copy-start | bytes 3460
  47.9 11.8 %all-to-all-start = ((bf16[32,40,128]{2,1,0:T(8,128)(2,1)}), bf16[32,40,128]{2,1,0:T(8,128)(2,1)S(1)}, u32[]{:S(2)}, u32[]{:S(2)}) async-start(bf16[32,40,128]{2,1,0:T(8,128)(2,1)} %bitcast.5), calls=%async_computation | async-start | bytes 655360 | tf_op jit(solution)/shard_map/all_to_all | solution.py:560
  60.4 23.9 %all-to-all-start.1 = ((bf16[16,40,128]{2,1,0:T(8,128)(2,1)}), bf16[16,40,128]{2,1,0:T(8,128)(2,1)S(1)}, u32[]{:S(2)}, u32[]{:S(2)}) async-start(bf16[16,40,128]{2,1,0:T(8,128)(2,1)} %shard_map.160), calls=%async_computation.1 | async-start | bytes 327680 | tf_op jit(solution)/shard_map/all_to_all | solution.py:575
  67.7 3.4 %collective-permute-start.4 = (bf16[816,128]{1,0:T(8,128)(2,1)S(1)}, bf16[816,128]{1,0:T(8,128)(2,1)S(1)}, u32[]{:S(2)}, u32[]{:S(2)}) collective-permute-start(bf16[816,128]{1,0:T(8,128)(2,1)S(1)} %shard_map.159.own), channel_id=1, source_target_pairs={{0,1},{1,0},{2,3},{3,2},{4,5},{5,4},{6,7},{7,6},{8,9},{9,8},{10,11... | collective-permute-start | bytes 626696 | tf_op jit(solution)/shard_map/ppermute | solution.py:573
  71.1 18.7 %collective-permute-start.5 = (bf16[384,128]{1,0:T(8,128)(2,1)S(1)}, bf16[384,128]{1,0:T(8,128)(2,1)S(1)}, u32[]{:S(2)}, u32[]{:S(2)}) collective-permute-start(bf16[384,128]{1,0:T(8,128)(2,1)S(1)} %shard_map.161.pair), channel_id=1, source_target_pairs={{1,2},{3,0},{5,6},{7,4},{9,10},{11,8},{13,14},{15,12},{17,18},{19,... | collective-permute-start | bytes 294920 | tf_op jit(solution)/shard_map/ppermute | solution.py:577
  83.6 11.3 %collective-permute-start.7 = (bf16[864,128]{1,0:T(8,128)(2,1)S(1)}, bf16[864,128]{1,0:T(8,128)(2,1)S(1)}, u32[]{:S(2)}, u32[]{:S(2)}) collective-permute-start(bf16[864,128]{1,0:T(8,128)(2,1)S(1)} %shard_map.165), channel_id=1, source_target_pairs={{124,128},{126,130},{252,256},{254,258},{380,384},{382,386},{508,0... | collective-permute-start | bytes 663560 | tf_op jit(solution)/shard_map/ppermute | solution.py:579
  85.1 4.8 %copy-start.12 = (bf16[432,72]{1,0:T(8,128)(2,1)S(1)}, bf16[432,72]{1,0:T(8,128)(2,1)}, u32[]{:S(2)}) copy-start(bf16[432,72]{1,0:T(8,128)(2,1)} %constant.8.clone.place) | copy-start | bytes 186628
  85.1 14.4 %all-to-all-start.2 = ((bf16[32,40,128]{2,1,0:T(8,128)(2,1)}), bf16[32,40,128]{2,1,0:T(8,128)(2,1)S(1)}, u32[]{:S(2)}, u32[]{:S(2)}) async-start(bf16[32,40,128]{2,1,0:T(8,128)(2,1)} %shard_map.163), calls=%async_computation.2 | async-start | bytes 655360 | tf_op jit(solution)/shard_map/all_to_all | solution.py:582
  90.2 4.6 %collective-permute-start.8 = (bf16[160,128]{1,0:T(8,128)(2,1)S(1)}, bf16[160,128]{1,0:T(8,128)(2,1)S(1)}, u32[]{:S(2)}, u32[]{:S(2)}) collective-permute-start(bf16[160,128]{1,0:T(8,128)(2,1)S(1)} %get-tuple-element.79.own), channel_id=1, source_target_pairs={{0,1},{2,3},{4,5},{6,7},{8,9},{10,11},{12,13},{14,15},{16,17},{18,... | collective-permute-start | bytes 122888 | tf_op jit(solution)/shard_map/ppermute | solution.py:603
  91.5 8.9 %collective-permute-start.6 = (bf16[448,128]{1,0:T(8,128)(2,1)S(1)}, bf16[448,128]{1,0:T(8,128)(2,1)S(1)}, u32[]{:S(2)}, u32[]{:S(2)}) collective-permute-start(bf16[448,128]{1,0:T(8,128)(2,1)S(1)} %get-tuple-element.78), channel_id=1, source_target_pairs={{0,4},{1,5},{2,6},{3,7},{4,8},{5,9},{6,10},{7,11},{8,12},{9,13},{1... | collective-permute-start | bytes 344072 | tf_op jit(solution)/shard_map/ppermute | solution.py:602
  94.9 5.5 %collective-permute-start.9 = (bf16[432,128]{1,0:T(8,128)(2,1)S(1)}, bf16[432,128]{1,0:T(8,128)(2,1)S(1)}, u32[]{:S(2)}, u32[]{:S(2)}) collective-permute-start(bf16[432,128]{1,0:T(8,128)(2,1)S(1)} %shard_map.166), channel_id=1, source_target_pairs={{0,1},{2,3},{128,129},{130,131},{256,257},{258,259},{384,385},{386... | collective-permute-start | bytes 331784 | tf_op jit(solution)/shard_map/ppermute | solution.py:606
  (2 other events, 1.6 us)

commit v6 on v5

--- a/solution.py
+++ b/solution.py
@@ -604,13 +604,6 @@
         across, from_near = lax.optimization_barrier((across, from_near))
         beside = call(beside_kernel, sds((LAT_ROWS, 128), BF), across, cost=(10**9, 10**6))
         beside = lax.ppermute(beside, AXES, [r for r in hop(lambda zh, c: (zh, 1), (0,)) if first(r)])
-        scale = float(n_lat * n_lon * N_OWN) ** -0.5
-        qkv, proj, gain = call(
-            lambda g, a, b, c: unpack_kernel(g, scale, a, b, c),
-            (sds((C, 3 * C), F32), sds((C, C), F32), sds((1, C), F32)),
-            whole.reshape(G_ROWS, 128),
-        )
-        base_x, qkv = lax.optimization_barrier((base_x, qkv))
         updated, d_tokens, d_table = call(
             finish_kernel,
             (
@@ -625,7 +618,14 @@
             beside,
             from_near,
             to_near,
-            cost=(20 * 10**9, 10**6),
+            cost=(10**8, 10**5),
+        )
+        whole, updated = lax.optimization_barrier((whole, updated))
+        scale = float(n_lat * n_lon * N_OWN) ** -0.5
+        qkv, proj, gain = call(
+            lambda g, a, b, c: unpack_kernel(g, scale, a, b, c),
+            (sds((C, 3 * C), F32), sds((C, C), F32), sds((1, C), F32)),
+            whole.reshape(G_ROWS, 128),
         )
         return updated, d_tokens, qkv, proj, gain.reshape(C), d_table.transpose(1, 0, 2)
 

time: 103 us -> 104 us (level)
  the two profiles are of different devices: /device:TPU:1 before, /device:TPU:2 now
where the time goes in v6:
time: 104 us; the launch traced here: 103 us
  starting transfers between devices  59.6 us (57%)
  Pallas kernels  21.9 us (21%)
  waiting for transfers between devices  18.5 us (18%)
  local copies, waits for them, and re-layouts  2.49 us (2%)
    pallas_call x14, Pallas kernels, call(): pl.pallas_call(kernel, out_shape=out_shape, scratch_shapes=list(scratch),...  21.9 us
    ppermute x1, starting transfers between devices, per_device(): from_lat = lax.ppermute(to_lat, AXES, route(-1, 0))  15.6 us
    all_to_all x1, waiting for transfers between devices, per_device(): line = lax.all_to_all(part, LINE, 0, 0)  8.74 us
    ppermute x1, starting transfers between devices, per_device(): from_lon = lax.ppermute(to_lon, AXES, hop(lambda zh, c: (1 - zh, 1), (0,)))  7.82 us
    all_to_all x1, starting transfers between devices, per_device(): whole = lax.all_to_all(total, PLANE, 0, 0)  7.68 us
    all_to_all x1, starting transfers between devices, per_device(): line = lax.all_to_all(part, LINE, 0, 0)  7.6 us
    all_to_all x1, starting transfers between devices, per_device(): parts = lax.all_to_all(grads.reshape(n_plane, piece, 128), PLANE, 0, 0)  6.33 us
    ppermute x1, waiting for transfers between devices, per_device(): lax.ppermute(to_lat, AXES, [r for r in route(1, 0) if not last(r)] + corn...  5.61 us
  transfers between devices with their start and end apart: 13, of which 5 were waited for; matrix products, arithmetic and copies ran while one was open for 0% of the time, Pallas kernels for 14%

profile of v6, /device:TPU:2, one launch (start us, length us, event | category | flops | bytes accessed | tf_op | source)
XLA Modules:
  0.0 103.4 jit_solution(17071963906811018493)
XLA Ops:
  0.6 0.9 copy-done
  1.5 0.9 copy-done.2
  2.5 1.9 %collective-permute-start = (bf16[432,128]{1,0:T(8,128)(2,1)S(1)}, bf16[432,128]{1,0:T(8,128)(2,1)S(1)}, u32[]{:S(2)}, u32[]{:S(2)}) collective-permute-start(bf16[432,128]{1,0:T(8,128)(2,1)S(1)} %get-tuple-element.47), channel_id=1, source_target_pairs={{0,1},{1,0},{2,3},{3,2},{4,5},{5,4},{6,7},{7,6},{8,9},{9,8},{10,11... | collective-permute-start | bytes 331784 | tf_op jit(solution)/shard_map/ppermute | solution.py:516
  4.5 1.3 %collective-permute-done.sibling = bf16[432,128]{1,0:T(8,128)(2,1)S(1)} collective-permute-done((bf16[432,128]{1,0:T(8,128)(2,1)S(1)}, bf16[432,128]{1,0:T(8,128)(2,1)S(1)}, u32[]{:S(2)}, u32[]{:S(2)}) %collective-permute-start) | collective-permute-done | bytes 110624 | tf_op jit(solution)/shard_map/ppermute | solution.py:516
  5.8 15.6 %collective-permute-start.3 = (bf16[576,128]{1,0:T(8,128)(2,1)S(1)}, bf16[576,128]{1,0:T(8,128)(2,1)S(1)}, u32[]{:S(2)}, u32[]{:S(2)}) collective-permute-start(bf16[576,128]{1,0:T(8,128)(2,1)S(1)} %shard_map.155), channel_id=1, source_target_pairs={{0,508},{1,509},{2,510},{3,511},{4,0},{5,1},{6,2},{7,3},{8,4},{9,5... | collective-permute-start | bytes 442376 | tf_op jit(solution)/shard_map/ppermute | solution.py:518
  21.4 7.8 %collective-permute-start.1 = (bf16[144,128]{1,0:T(8,128)(2,1)S(1)}, bf16[144,128]{1,0:T(8,128)(2,1)S(1)}, u32[]{:S(2)}, u32[]{:S(2)}) collective-permute-start(bf16[144,128]{1,0:T(8,128)(2,1)S(1)} %get-tuple-element.53), channel_id=1, source_target_pairs={{0,3},{2,1},{4,7},{6,5},{8,11},{10,9},{12,15},{14,13},{16,19},{18,... | collective-permute-start | bytes 110600 | tf_op jit(solution)/shard_map/ppermute | solution.py:521
  29.2 1.3 %collective-permute-start.2 = (bf16[144,128]{1,0:T(8,128)(2,1)S(1)}, bf16[144,128]{1,0:T(8,128)(2,1)S(1)}, u32[]{:S(2)}, u32[]{:S(2)}) collective-permute-start(bf16[144,128]{1,0:T(8,128)(2,1)S(1)} %get-tuple-element.54), channel_id=1, source_target_pairs={{0,511},{2,509},{4,3},{6,1},{8,7},{10,5},{12,11},{14,9},{16,15},{1... | collective-permute-start | bytes 110600 | tf_op jit(solution)/shard_map/ppermute | solution.py:522
  30.6 5.2 %shard_map.157 = (f32[144,896]{1,0:T(8,128)S(1)}, s32[144,256]{1,0:T(8,128)S(1)}, s32[144,256]{1,0:T(8,128)S(1)}) custom-call(s32[144,144]{1,0:T(8,128)S(1)} %copy-done.5, f32[6,1,3312]{2,1,0:T(1,128)S(1)} %bitcast.16), custom_call_target="tpu_custom_call" | custom-call | flops 6000000000 | bytes 1000000 | tf_op jit(solution)/shard_map/pallas_call | solution.py:461
  36.6 6.1 %shard_map.158 = (bf16[288,192]{1,0:T(8,128)(2,1)S(1)}, bf16[288,192]{1,0:T(8,128)(2,1)S(1)}, bf16[432,128]{1,0:T(8,128)(2,1)S(1)}, bf16[432,128]{1,0:T(8,128)(2...) custom-call(bf16[288,192]{1,0:T(8,128)(2,1)S(1)} %bitcast.14, ...), custom_call_target="tpu_custom_call" | custom-call | flops 6000000000 | bytes 1000000 | tf_op jit(solution)/shard_map/pallas_call | solution.py:461
  42.6 6.3 %all-to-all-start = ((bf16[32,40,128]{2,1,0:T(8,128)(2,1)}), bf16[32,40,128]{2,1,0:T(8,128)(2,1)S(1)}, u32[]{:S(2)}, u32[]{:S(2)}) async-start(bf16[32,40,128]{2,1,0:T(8,128)(2,1)} %bitcast.5), calls=%async_computation | async-start | bytes 655360 | tf_op jit(solution)/shard_map/all_to_all | solution.py:560
  49.0 6.8 %shard_map.159.own = bf16[816,128]{1,0:T(8,128)(2,1)S(1)} custom-call(f32[144,896]{1,0:T(8,128)S(1)} %get-tuple-element.62.d_bias, s32[144,256]{1,0:T(8,128)S(1)} %get-tuple-element.63.hi, s32[144,256]{1,0:T(8,128)S(1)} %get-tuple-element.64.lo, bf16[224,128]{1,0:T(8,128)(2,1)S(1)} %get-tuple-element.65.edge, bf16[432,128]{1,0:T(8,128)(2,1)S(1)} %get-tuple-element.66.lat), custom_call_target="tpu_custom_call" | custom-call | flops 8000000000 | bytes 1000000 | tf_op jit(solution)/shard_map/pallas_call | solution.py:461
  55.8 1.5 %all-to-all-done.parts = bf16[32,40,128]{2,1,0:T(8,128)(2,1)S(1)} async-done(((bf16[32,40,128]{2,1,0:T(8,128)(2,1)}), bf16[32,40,128]{2,1,0:T(8,128)(2,1)S(1)}, u32[]{:S(2)}, u32[]{:S(2)}) %all-to-all-start) | async-done | bytes 327712 | tf_op jit(solution)/shard_map/all_to_all | solution.py:560
  58.0 7.6 %all-to-all-start.1 = ((bf16[16,40,128]{2,1,0:T(8,128)(2,1)}), bf16[16,40,128]{2,1,0:T(8,128)(2,1)S(1)}, u32[]{:S(2)}, u32[]{:S(2)}) async-start(bf16[16,40,128]{2,1,0:T(8,128)(2,1)} %shard_map.160), calls=%async_computation.1 | async-start | bytes 327680 | tf_op jit(solution)/shard_map/all_to_all | solution.py:575
  65.6 2.1 %collective-permute-start.4 = (bf16[816,128]{1,0:T(8,128)(2,1)S(1)}, bf16[816,128]{1,0:T(8,128)(2,1)S(1)}, u32[]{:S(2)}, u32[]{:S(2)}) collective-permute-start(bf16[816,128]{1,0:T(8,128)(2,1)S(1)} %shard_map.159.own), channel_id=1, source_target_pairs={{0,1},{1,0},{2,3},{3,2},{4,5},{5,4},{6,7},{7,6},{8,9},{9,8},{10,11... | collective-permute-start | bytes 626696 | tf_op jit(solution)/shard_map/ppermute | solution.py:573
  67.7 1.3 %collective-permute-done.4.near = bf16[816,128]{1,0:T(8,128)(2,1)S(1)} collective-permute-done((bf16[816,128]{1,0:T(8,128)(2,1)S(1)}, bf16[816,128]{1,0:T(8,128)(2,1)S(1)}, u32[]{:S(2)}, u32[]{:S(2)}) %collective-permute-start.4) | collective-permute-done | bytes 208928 | tf_op jit(solution)/shard_map/ppermute | solution.py:573
  69.0 1.3 %collective-permute-start.5 = (bf16[384,128]{1,0:T(8,128)(2,1)S(1)}, bf16[384,128]{1,0:T(8,128)(2,1)S(1)}, u32[]{:S(2)}, u32[]{:S(2)}) collective-permute-start(bf16[384,128]{1,0:T(8,128)(2,1)S(1)} %shard_map.161.pair), channel_id=1, source_target_pairs={{1,2},{3,0},{5,6},{7,4},{9,10},{11,8},{13,14},{15,12},{17,18},{19,... | collective-permute-start | bytes 294920 | tf_op jit(solution)/shard_map/ppermute | solution.py:577
  70.4 1.3 %collective-permute-start.7 = (bf16[864,128]{1,0:T(8,128)(2,1)S(1)}, bf16[864,128]{1,0:T(8,128)(2,1)S(1)}, u32[]{:S(2)}, u32[]{:S(2)}) collective-permute-start(bf16[864,128]{1,0:T(8,128)(2,1)S(1)} %shard_map.164), channel_id=1, source_target_pairs={{124,128},{126,130},{252,256},{254,258},{380,384},{382,386},{508,0... | collective-permute-start | bytes 663560 | tf_op jit(solution)/shard_map/ppermute | solution.py:579
  71.7 8.7 %all-to-all-done.1.parts = bf16[16,40,128]{2,1,0:T(8,128)(2,1)S(1)} async-done(((bf16[16,40,128]{2,1,0:T(8,128)(2,1)}), bf16[16,40,128]{2,1,0:T(8,128)(2,1)S(1)}, u32[]{:S(2)}, u32[]{:S(2)}) %all-to-all-start.1) | async-done | bytes 163872 | tf_op jit(solution)/shard_map/all_to_all | solution.py:575
  81.2 7.7 %all-to-all-start.2 = ((bf16[32,40,128]{2,1,0:T(8,128)(2,1)}), bf16[32,40,128]{2,1,0:T(8,128)(2,1)S(1)}, u32[]{:S(2)}, u32[]{:S(2)}) async-start(bf16[32,40,128]{2,1,0:T(8,128)(2,1)} %shard_map.162), calls=%async_computation.2 | async-start | bytes 655360 | tf_op jit(solution)/shard_map/all_to_all | solution.py:582
  89.3 2.1 %collective-permute-start.8 = (bf16[160,128]{1,0:T(8,128)(2,1)S(1)}, bf16[160,128]{1,0:T(8,128)(2,1)S(1)}, u32[]{:S(2)}, u32[]{:S(2)}) collective-permute-start(bf16[160,128]{1,0:T(8,128)(2,1)S(1)} %get-tuple-element.77.own), channel_id=1, source_target_pairs={{0,1},{2,3},{4,5},{6,7},{8,9},{10,11},{12,13},{14,15},{16,17},{18,... | collective-permute-start | bytes 122888 | tf_op jit(solution)/shard_map/ppermute | solution.py:603
  91.3 3.4 %collective-permute-start.6 = (bf16[448,128]{1,0:T(8,128)(2,1)S(1)}, bf16[448,128]{1,0:T(8,128)(2,1)S(1)}, u32[]{:S(2)}, u32[]{:S(2)}) collective-permute-start(bf16[448,128]{1,0:T(8,128)(2,1)S(1)} %get-tuple-element.76), channel_id=1, source_target_pairs={{0,4},{1,5},{2,6},{3,7},{4,8},{5,9},{6,10},{7,11},{8,12},{9,13},{1... | collective-permute-start | bytes 344072 | tf_op jit(solution)/shard_map/ppermute | solution.py:602
  94.8 1.3 %collective-permute-start.9 = (bf16[432,128]{1,0:T(8,128)(2,1)S(1)}, bf16[432,128]{1,0:T(8,128)(2,1)S(1)}, u32[]{:S(2)}, u32[]{:S(2)}) collective-permute-start(bf16[432,128]{1,0:T(8,128)(2,1)S(1)} %shard_map.165), channel_id=1, source_target_pairs={{0,1},{2,3},{128,129},{130,131},{256,257},{258,259},{384,385},{386... | collective-permute-start | bytes 331784 | tf_op jit(solution)/shard_map/ppermute | solution.py:606
  96.1 5.6 %collective-permute-done.6.lat = bf16[448,128]{1,0:T(8,128)(2,1)S(1)} collective-permute-done((bf16[448,128]{1,0:T(8,128)(2,1)S(1)}, bf16[448,128]{1,0:T(8,128)(2,1)S(1)}, u32[]{:S(2)}, u32[]{:S(2)}) %collective-permute-start.6) | collective-permute-done | bytes 114720 | tf_op jit(solution)/shard_map/ppermute | solution.py:602
  102.5 0.9 shard_map.167
  (42 shorter events, 3.6 us)
Async XLA Ops:
  0.6 0.9 copy-start
  1.5 0.9 copy-start.2
  2.5 3.2 %collective-permute-start = (bf16[432,128]{1,0:T(8,128)(2,1)S(1)}, bf16[432,128]{1,0:T(8,128)(2,1)S(1)}, u32[]{:S(2)}, u32[]{:S(2)}) collective-permute-start(bf16[432,128]{1,0:T(8,128)(2,1)S(1)} %get-tuple-element.47), channel_id=1, source_target_pairs={{0,1},{1,0},{2,3},{3,2},{4,5},{5,4},{6,7},{7,6},{8,9},{9,8},{10,11... | collective-permute-start | bytes 331784 | tf_op jit(solution)/shard_map/ppermute | solution.py:516
  5.8 30.1 %collective-permute-start.3 = (bf16[576,128]{1,0:T(8,128)(2,1)S(1)}, bf16[576,128]{1,0:T(8,128)(2,1)S(1)}, u32[]{:S(2)}, u32[]{:S(2)}) collective-permute-start(bf16[576,128]{1,0:T(8,128)(2,1)S(1)} %shard_map.155), channel_id=1, source_target_pairs={{0,508},{1,509},{2,510},{3,511},{4,0},{5,1},{6,2},{7,3},{8,4},{9,5... | collective-permute-start | bytes 442376 | tf_op jit(solution)/shard_map/ppermute | solution.py:518
  21.4 9.2 %copy-start.5 = (s32[144,144]{1,0:T(8,128)S(1)}, s32[144,144]{1,0:T(8,128)}, u32[]{:S(2)}) copy-start(s32[144,144]{1,0:T(8,128)} %pos.1) | copy-start | bytes 248836
  21.4 9.2 %copy-start.7 = (f32[1,6,3312]{2,0,1:T(1,128)S(1)}, f32[1,6,3312]{2,0,1:T(1,128)}, u32[]{:S(2)}) copy-start(f32[1,6,3312]{2,0,1:T(1,128)} %param.17) | copy-start | bytes 238468
  21.4 14.5 %collective-permute-start.1 = (bf16[144,128]{1,0:T(8,128)(2,1)S(1)}, bf16[144,128]{1,0:T(8,128)(2,1)S(1)}, u32[]{:S(2)}, u32[]{:S(2)}) collective-permute-start(bf16[144,128]{1,0:T(8,128)(2,1)S(1)} %get-tuple-element.53), channel_id=1, source_target_pairs={{0,3},{2,1},{4,7},{6,5},{8,11},{10,9},{12,15},{14,13},{16,19},{18,... | collective-permute-start | bytes 110600 | tf_op jit(solution)/shard_map/ppermute | solution.py:521
  29.2 6.7 %collective-permute-start.2 = (bf16[144,128]{1,0:T(8,128)(2,1)S(1)}, bf16[144,128]{1,0:T(8,128)(2,1)S(1)}, u32[]{:S(2)}, u32[]{:S(2)}) collective-permute-start(bf16[144,128]{1,0:T(8,128)(2,1)S(1)} %get-tuple-element.54), channel_id=1, source_target_pairs={{0,511},{2,509},{4,3},{6,1},{8,7},{10,5},{12,11},{14,9},{16,15},{1... | collective-permute-start | bytes 110600 | tf_op jit(solution)/shard_map/ppermute | solution.py:522
  30.6 5.4 %copy-start.1 = (bf16[2,6,24,192]{3,2,1,0:T(8,128)(2,1)S(1)}, bf16[2,6,24,192]{3,2,1,0:T(8,128)(2,1)}, u32[]{:S(2)}) copy-start(bf16[2,6,24,192]{3,2,1,0:T(8,128)(2,1)} %tokens.1) | copy-start | bytes 331780
  30.6 5.4 %copy-start.3 = (bf16[2,6,24,192]{3,2,1,0:T(8,128)(2,1)S(1)}, bf16[2,6,24,192]{3,2,1,0:T(8,128)(2,1)}, u32[]{:S(2)}) copy-start(bf16[2,6,24,192]{3,2,1,0:T(8,128)(2,1)} %d_out.1) | copy-start | bytes 331780
  30.6 5.4 %copy-start.4 = (bf16[192,576]{1,0:T(8,128)(2,1)S(1)}, bf16[192,576]{1,0:T(8,128)(2,1)}, u32[]{:S(2)}) copy-start(bf16[192,576]{1,0:T(8,128)(2,1)} %w_qkv.1) | copy-start | bytes 663556
  30.6 5.4 %copy-start.6 = (bf16[192,192]{1,0:T(8,128)(2,1)S(1)}, bf16[192,192]{1,0:T(8,128)(2,1)}, u32[]{:S(2)}) copy-start(bf16[192,192]{1,0:T(8,128)(2,1)} %wp.1) | copy-start | bytes 221188
  30.6 5.4 %copy-start.10 = (bf16[2,648,144]{2,1,0:T(8,128)(2,1)S(1)}, bf16[2,648,144]{2,1,0:T(8,128)(2,1)}, u32[]{:S(2)}) copy-start(bf16[2,648,144]{2,1,0:T(8,128)(2,1)} %constant.7.clone.back) | copy-start | bytes 1119748
  30.6 5.4 %copy-start.11 = (bf16[2,144,528]{2,1,0:T(8,128)(2,1)S(1)}, bf16[2,144,528]{2,1,0:T(8,128)(2,1)}, u32[]{:S(2)}) copy-start(bf16[2,144,528]{2,1,0:T(8,128)(2,1)} %constant.6.clone.pick) | copy-start | bytes 912388
  42.6 14.6 %all-to-all-start = ((bf16[32,40,128]{2,1,0:T(8,128)(2,1)}), bf16[32,40,128]{2,1,0:T(8,128)(2,1)S(1)}, u32[]{:S(2)}, u32[]{:S(2)}) async-start(bf16[32,40,128]{2,1,0:T(8,128)(2,1)} %bitcast.5), calls=%async_computation | async-start | bytes 655360 | tf_op jit(solution)/shard_map/all_to_all | solution.py:560
  58.0 22.4 %all-to-all-start.1 = ((bf16[16,40,128]{2,1,0:T(8,128)(2,1)}), bf16[16,40,128]{2,1,0:T(8,128)(2,1)S(1)}, u32[]{:S(2)}, u32[]{:S(2)}) async-start(bf16[16,40,128]{2,1,0:T(8,128)(2,1)} %shard_map.160), calls=%async_computation.1 | async-start | bytes 327680 | tf_op jit(solution)/shard_map/all_to_all | solution.py:575
  65.6 3.4 %collective-permute-start.4 = (bf16[816,128]{1,0:T(8,128)(2,1)S(1)}, bf16[816,128]{1,0:T(8,128)(2,1)S(1)}, u32[]{:S(2)}, u32[]{:S(2)}) collective-permute-start(bf16[816,128]{1,0:T(8,128)(2,1)S(1)} %shard_map.159.own), channel_id=1, source_target_pairs={{0,1},{1,0},{2,3},{3,2},{4,5},{5,4},{6,7},{7,6},{8,9},{9,8},{10,11... | collective-permute-start | bytes 626696 | tf_op jit(solution)/shard_map/ppermute | solution.py:573
  69.0 19.8 %collective-permute-start.5 = (bf16[384,128]{1,0:T(8,128)(2,1)S(1)}, bf16[384,128]{1,0:T(8,128)(2,1)S(1)}, u32[]{:S(2)}, u32[]{:S(2)}) collective-permute-start(bf16[384,128]{1,0:T(8,128)(2,1)S(1)} %shard_map.161.pair), channel_id=1, source_target_pairs={{1,2},{3,0},{5,6},{7,4},{9,10},{11,8},{13,14},{15,12},{17,18},{19,... | collective-permute-start | bytes 294920 | tf_op jit(solution)/shard_map/ppermute | solution.py:577
  70.4 24.4 %collective-permute-start.7 = (bf16[864,128]{1,0:T(8,128)(2,1)S(1)}, bf16[864,128]{1,0:T(8,128)(2,1)S(1)}, u32[]{:S(2)}, u32[]{:S(2)}) collective-permute-start(bf16[864,128]{1,0:T(8,128)(2,1)S(1)} %shard_map.164), channel_id=1, source_target_pairs={{124,128},{126,130},{252,256},{254,258},{380,384},{382,386},{508,0... | collective-permute-start | bytes 663560 | tf_op jit(solution)/shard_map/ppermute | solution.py:579
  81.2 7.7 %copy-start.12 = (bf16[432,72]{1,0:T(8,128)(2,1)S(1)}, bf16[432,72]{1,0:T(8,128)(2,1)}, u32[]{:S(2)}) copy-start(bf16[432,72]{1,0:T(8,128)(2,1)} %constant.8.clone.place) | copy-start | bytes 186628
  81.2 21.3 %all-to-all-start.2 = ((bf16[32,40,128]{2,1,0:T(8,128)(2,1)}), bf16[32,40,128]{2,1,0:T(8,128)(2,1)S(1)}, u32[]{:S(2)}, u32[]{:S(2)}) async-start(bf16[32,40,128]{2,1,0:T(8,128)(2,1)} %shard_map.162), calls=%async_computation.2 | async-start | bytes 655360 | tf_op jit(solution)/shard_map/all_to_all | solution.py:582
  89.3 5.5 %collective-permute-start.8 = (bf16[160,128]{1,0:T(8,128)(2,1)S(1)}, bf16[160,128]{1,0:T(8,128)(2,1)S(1)}, u32[]{:S(2)}, u32[]{:S(2)}) collective-permute-start(bf16[160,128]{1,0:T(8,128)(2,1)S(1)} %get-tuple-element.77.own), channel_id=1, source_target_pairs={{0,1},{2,3},{4,5},{6,7},{8,9},{10,11},{12,13},{14,15},{16,17},{18,... | collective-permute-start | bytes 122888 | tf_op jit(solution)/shard_map/ppermute | solution.py:603
  91.3 10.3 %collective-permute-start.6 = (bf16[448,128]{1,0:T(8,128)(2,1)S(1)}, bf16[448,128]{1,0:T(8,128)(2,1)S(1)}, u32[]{:S(2)}, u32[]{:S(2)}) collective-permute-start(bf16[448,128]{1,0:T(8,128)(2,1)S(1)} %get-tuple-element.76), channel_id=1, source_target_pairs={{0,4},{1,5},{2,6},{3,7},{4,8},{5,9},{6,10},{7,11},{8,12},{9,13},{1... | collective-permute-start | bytes 344072 | tf_op jit(solution)/shard_map/ppermute | solution.py:602
  94.8 6.9 %collective-permute-start.9 = (bf16[432,128]{1,0:T(8,128)(2,1)S(1)}, bf16[432,128]{1,0:T(8,128)(2,1)S(1)}, u32[]{:S(2)}, u32[]{:S(2)}) collective-permute-start(bf16[432,128]{1,0:T(8,128)(2,1)S(1)} %shard_map.165), channel_id=1, source_target_pairs={{0,1},{2,3},{128,129},{130,131},{256,257},{258,259},{384,385},{386... | collective-permute-start | bytes 331784 | tf_op jit(solution)/shard_map/ppermute | solution.py:606
  (2 other events, 1.4 us)

commit v7 on v4

--- a/solution.py
+++ b/solution.py
@@ -138,14 +138,14 @@
     return lax.broadcasted_iota(jnp.int32, (rows, 128), 0) * 0 + at == want
 
 
-def cut_kernel(tokens, d_out, to_core, lat, edge, to_diag):
+def cut_kernel(tokens, d_out, to_core, lat, to_lon, to_diag):
     both = (tokens[...].astype(F32), d_out[...].astype(F32))
     top = fold(*(a[:, :HALF_LAT].reshape(N_LAT, C) for a in both))
     corner = fold(*(a[:, :HALF_LAT, :EDGE].reshape(N_EDGE, C) for a in both))
     lon = fold(*(a[:, HALF_LAT:, :EDGE].reshape(N_EDGE, C) for a in both))
     side = jnp.concatenate([corner, lon], axis=0)
     lat[...] = top.astype(BF)
-    edge[...] = side.astype(BF)
+    to_lon[...] = lon.astype(BF)
     to_diag[...] = corner.astype(BF)
     spare = jnp.zeros((LAT_ROWS - SIDE_ROWS, 128), F32)
     to_core[...] = jnp.where(core_is(1, LAT_ROWS), jnp.concatenate([side, spare], axis=0), top).astype(BF)
@@ -273,7 +273,7 @@
     f32 = lambda ref, start, size: ref[start : start + size, :].astype(F32)
     over = f32(from_line, 0, LAT_ROWS) + f32(from_side, LAT_ROWS, LAT_ROWS)
     lat = unfold(jnp.where(band_is(False, LAT_ROWS), over, f32(from_lat, 0, LAT_ROWS)), N_LAT)
-    lon = f32(sibling, CORNER_ROWS, CORNER_ROWS), f32(from_lon, CORNER_ROWS, CORNER_ROWS)
+    lon = f32(sibling, CORNER_ROWS, CORNER_ROWS), f32(from_lon, 0, CORNER_ROWS)
     lon = unfold(jnp.where(core_is(0, CORNER_ROWS), *lon), N_EDGE)
     inner = jnp.where(
         band_is(False, CORNER_ROWS), f32(from_side, 2 * LAT_ROWS, CORNER_ROWS), f32(from_lat, LAT_ROWS, CORNER_ROWS)
@@ -504,19 +504,19 @@
 
     def per_device(tokens, mask_ids, pos_index, norm_gain, w_qkv, w_proj, earth_bias, d_out):
         pick, back, place = (jnp.asarray(c) for c in constants())
-        to_core, lat, edge, to_diag = call(
+        to_core, lat, to_lon, to_diag = call(
             cut_kernel,
             (
                 sds((LAT_ROWS, 128), BF),
                 sds((LAT_ROWS, 128), BF),
-                sds((SIDE_ROWS, 128), BF),
+                sds((CORNER_ROWS, 128), BF),
                 sds((CORNER_ROWS, 128), BF),
             ),
             tokens,
             d_out,
         )
         sibling = lax.ppermute(to_core, AXES, hop(lambda zh, c: (zh, 1 - c), (0, 1)))
-        from_lon = lax.ppermute(edge, AXES, hop(lambda zh, c: (1 - zh, 1), (0,)))
+        from_lon = lax.ppermute(to_lon, AXES, hop(lambda zh, c: (1 - zh, 1), (0,)))
         from_diag = lax.ppermute(to_diag, AXES, [r for r in route(-1, -1) if r[0] % sizes[4] == 0])
         to_lat, to_line = call(
             join_kernel,

time: 103 us -> 103 us (level)
  no operation moved by 1% of the time
where the time goes in v7:
time: 103 us; the launch traced here: 101 us
  starting transfers between devices  68.7 us (67%)
  Pallas kernels  21.9 us (21%)
  waiting for transfers between devices  7.36 us (7%)
  local copies, waits for them, and re-layouts  2.48 us (2%)
  between operations  1.04 us (1%)
    pallas_call x13, Pallas kernels, call(): pl.pallas_call(kernel, out_shape=out_shape, scratch_shapes=list(scratch),...  21.9 us
    ppermute x1, starting transfers between devices, per_device(): lax.ppermute(to_line, AXES, [r for r in south if first(r) and r[0] % size...  13.2 us
    ppermute x1, starting transfers between devices, per_device(): far = lax.ppermute(pair, AXES, hop(lambda zh, c: (1 - zh, 0), (1,)))  12.4 us
    all_to_all x1, starting transfers between devices, per_device(): line = lax.all_to_all(part, LINE, 0, 0)  10.6 us
    ppermute x1, starting transfers between devices, per_device(): lax.ppermute(to_core, AXES, hop(lambda zh, c: (zh, 1 - c), (0, 1)))  8.92 us
    all_to_all x1, starting transfers between devices, per_device(): parts = lax.all_to_all(grads.reshape(n_plane, piece, 128), PLANE, 0, 0)  5.46 us
    all_to_all x1, starting transfers between devices, per_device(): whole = lax.all_to_all(total, PLANE, 0, 0)  4.75 us
    all_to_all x1, waiting for transfers between devices, per_device(): whole = lax.all_to_all(total, PLANE, 0, 0)  3.3 us
  transfers between devices with their start and end apart: 15, of which 3 were waited for; matrix products, arithmetic and copies ran while one was open for 0% of the time, Pallas kernels for 14%

profile of v7, /device:TPU:1, one launch (start us, length us, event | category | flops | bytes accessed | tf_op | source)
XLA Modules:
  0.0 101.5 jit_solution(18060715515224270746)
XLA Ops:
  0.6 0.9 copy-done
  1.5 0.9 copy-done.2
  2.6 8.9 %collective-permute-start = (bf16[432,128]{1,0:T(8,128)(2,1)S(1)}, bf16[432,128]{1,0:T(8,128)(2,1)S(1)}, u32[]{:S(2)}, u32[]{:S(2)}) collective-permute-start(bf16[432,128]{1,0:T(8,128)(2,1)S(1)} %get-tuple-element.45), channel_id=1, source_target_pairs={{0,1},{1,0},{2,3},{3,2},{4,5},{5,4},{6,7},{7,6},{8,9},{9,8},{10,11... | collective-permute-start | bytes 331784 | tf_op jit(solution)/shard_map/ppermute | solution.py:518
  11.5 1.3 %collective-permute-start.2 = (bf16[144,128]{1,0:T(8,128)(2,1)S(1)}, bf16[144,128]{1,0:T(8,128)(2,1)S(1)}, u32[]{:S(2)}, u32[]{:S(2)}) collective-permute-start(bf16[144,128]{1,0:T(8,128)(2,1)S(1)} %get-tuple-element.49), channel_id=1, source_target_pairs={{0,3},{2,1},{4,7},{6,5},{8,11},{10,9},{12,15},{14,13},{16,19},{18,... | collective-permute-start | bytes 110600 | tf_op jit(solution)/shard_map/ppermute | solution.py:519
  12.8 1.3 %collective-permute-start.3 = (bf16[144,128]{1,0:T(8,128)(2,1)S(1)}, bf16[144,128]{1,0:T(8,128)(2,1)S(1)}, u32[]{:S(2)}, u32[]{:S(2)}) collective-permute-start(bf16[144,128]{1,0:T(8,128)(2,1)S(1)} %get-tuple-element.47.corner), channel_id=1, source_target_pairs={{0,511},{2,509},{4,3},{6,1},{8,7},{10,5},{12,11},{14,9},{16,15},{1... | collective-permute-start | bytes 110600 | tf_op jit(solution)/shard_map/ppermute | solution.py:520
  14.2 1.3 %collective-permute-start.4 = (bf16[576,128]{1,0:T(8,128)(2,1)S(1)}, bf16[576,128]{1,0:T(8,128)(2,1)S(1)}, u32[]{:S(2)}, u32[]{:S(2)}) collective-permute-start(bf16[576,128]{1,0:T(8,128)(2,1)S(1)} %get-tuple-element.50), channel_id=1, source_target_pairs={{4,0},{5,1},{6,2},{7,3},{8,4},{9,5},{10,6},{11,7},{12,8},{13,9},{1... | collective-permute-start | bytes 442376 | tf_op jit(solution)/shard_map/ppermute | solution.py:529
  15.5 13.2 %collective-permute-start.1 = (bf16[1008,128]{1,0:T(8,128)(2,1)S(1)}, bf16[1008,128]{1,0:T(8,128)(2,1)S(1)}, u32[]{:S(2)}, u32[]{:S(2)}) collective-permute-start(bf16[1008,128]{1,0:T(8,128)(2,1)S(1)} %get-tuple-element.48), channel_id=1, source_target_pairs={{1,509},{3,511},{129,125},{131,127},{257,253},{259,255},{385,381},... | collective-permute-start | bytes 774152 | tf_op jit(solution)/shard_map/ppermute | solution.py:530
  28.8 5.2 %shard_map.156 = (f32[144,896]{1,0:T(8,128)S(1)}, s32[144,256]{1,0:T(8,128)S(1)}, s32[144,256]{1,0:T(8,128)S(1)}) custom-call(s32[144,144]{1,0:T(8,128)S(1)} %copy-done.5, f32[6,1,3312]{2,1,0:T(1,128)S(1)} %bitcast.14), custom_call_target="tpu_custom_call" | custom-call | flops 6000000000 | bytes 1000000 | tf_op jit(solution)/shard_map/pallas_call | solution.py:463
  35.5 6.0 %shard_map.157 = (bf16[288,192]{1,0:T(8,128)(2,1)S(1)}, bf16[288,192]{1,0:T(8,128)(2,1)S(1)}, bf16[432,128]{1,0:T(8,128)(2,1)S(1)}, bf16[432,128]{1,0:T(8,128)(2...) custom-call(bf16[288,192]{1,0:T(8,128)(2,1)S(1)} %bitcast.12, ...), custom_call_target="tpu_custom_call" | custom-call | flops 6000000000 | bytes 1000000 | tf_op jit(solution)/shard_map/pallas_call | solution.py:463
  41.5 5.5 %all-to-all-start = ((bf16[32,40,128]{2,1,0:T(8,128)(2,1)}), bf16[32,40,128]{2,1,0:T(8,128)(2,1)S(1)}, u32[]{:S(2)}, u32[]{:S(2)}) async-start(bf16[32,40,128]{2,1,0:T(8,128)(2,1)} %bitcast.5), calls=%async_computation | async-start | bytes 655360 | tf_op jit(solution)/shard_map/all_to_all | solution.py:571
  47.0 6.8 %shard_map.158.own = bf16[816,128]{1,0:T(8,128)(2,1)S(1)} custom-call(f32[144,896]{1,0:T(8,128)S(1)} %get-tuple-element.58.d_bias, s32[144,256]{1,0:T(8,128)S(1)} %get-tuple-element.59.hi, s32[144,256]{1,0:T(8,128)S(1)} %get-tuple-element.60.lo, bf16[224,128]{1,0:T(8,128)(2,1)S(1)} %get-tuple-element.61.edge, bf16[432,128]{1,0:T(8,128)(2,1)S(1)} %get-tuple-element.62.lat), custom_call_target="tpu_custom_call" | custom-call | flops 8000000000 | bytes 1000000 | tf_op jit(solution)/shard_map/pallas_call | solution.py:463
  53.7 2.9 %all-to-all-done.parts = bf16[32,40,128]{2,1,0:T(8,128)(2,1)S(1)} async-done(((bf16[32,40,128]{2,1,0:T(8,128)(2,1)}), bf16[32,40,128]{2,1,0:T(8,128)(2,1)S(1)}, u32[]{:S(2)}, u32[]{:S(2)}) %all-to-all-start) | async-done | bytes 327712 | tf_op jit(solution)/shard_map/all_to_all | solution.py:571
  57.4 10.6 %all-to-all-start.1 = ((bf16[16,40,128]{2,1,0:T(8,128)(2,1)}), bf16[16,40,128]{2,1,0:T(8,128)(2,1)S(1)}, u32[]{:S(2)}, u32[]{:S(2)}) async-start(bf16[16,40,128]{2,1,0:T(8,128)(2,1)} %shard_map.159), calls=%async_computation.1 | async-start | bytes 327680 | tf_op jit(solution)/shard_map/all_to_all | solution.py:586
  68.0 2.2 %collective-permute-start.6 = (bf16[816,128]{1,0:T(8,128)(2,1)S(1)}, bf16[816,128]{1,0:T(8,128)(2,1)S(1)}, u32[]{:S(2)}, u32[]{:S(2)}) collective-permute-start(bf16[816,128]{1,0:T(8,128)(2,1)S(1)} %shard_map.158.own), channel_id=1, source_target_pairs={{0,1},{1,0},{2,3},{3,2},{4,5},{5,4},{6,7},{7,6},{8,9},{9,8},{10,11... | collective-permute-start | bytes 626696 | tf_op jit(solution)/shard_map/ppermute | solution.py:584
  70.2 1.1 %collective-permute-done.6.near = bf16[816,128]{1,0:T(8,128)(2,1)S(1)} collective-permute-done((bf16[816,128]{1,0:T(8,128)(2,1)S(1)}, bf16[816,128]{1,0:T(8,128)(2,1)S(1)}, u32[]{:S(2)}, u32[]{:S(2)}) %collective-permute-start.6) | collective-permute-done | bytes 208928 | tf_op jit(solution)/shard_map/ppermute | solution.py:584
  71.3 12.4 %collective-permute-start.7 = (bf16[384,128]{1,0:T(8,128)(2,1)S(1)}, bf16[384,128]{1,0:T(8,128)(2,1)S(1)}, u32[]{:S(2)}, u32[]{:S(2)}) collective-permute-start(bf16[384,128]{1,0:T(8,128)(2,1)S(1)} %shard_map.160.pair), channel_id=1, source_target_pairs={{1,2},{3,0},{5,6},{7,4},{9,10},{11,8},{13,14},{15,12},{17,18},{19,... | collective-permute-start | bytes 294920 | tf_op jit(solution)/shard_map/ppermute | solution.py:588
  84.5 0.8 shard_map.162
  85.3 4.7 %all-to-all-start.2 = ((bf16[32,40,128]{2,1,0:T(8,128)(2,1)}), bf16[32,40,128]{2,1,0:T(8,128)(2,1)S(1)}, u32[]{:S(2)}, u32[]{:S(2)}) async-start(bf16[32,40,128]{2,1,0:T(8,128)(2,1)} %shard_map.162), calls=%async_computation.2 | async-start | bytes 655360 | tf_op jit(solution)/shard_map/all_to_all | solution.py:593
  90.5 1.3 %collective-permute-start.10 = (bf16[160,128]{1,0:T(8,128)(2,1)S(1)}, bf16[160,128]{1,0:T(8,128)(2,1)S(1)}, u32[]{:S(2)}, u32[]{:S(2)}) collective-permute-start(bf16[160,128]{1,0:T(8,128)(2,1)S(1)} %get-tuple-element.75.own), channel_id=1, source_target_pairs={{0,1},{2,3},{4,5},{6,7},{8,9},{10,11},{12,13},{14,15},{16,17},{18,... | collective-permute-start | bytes 122888 | tf_op jit(solution)/shard_map/ppermute | solution.py:614
  91.8 3.3 %collective-permute-start.8 = (bf16[448,128]{1,0:T(8,128)(2,1)S(1)}, bf16[448,128]{1,0:T(8,128)(2,1)S(1)}, u32[]{:S(2)}, u32[]{:S(2)}) collective-permute-start(bf16[448,128]{1,0:T(8,128)(2,1)S(1)} %get-tuple-element.74), channel_id=1, source_target_pairs={{0,4},{1,5},{2,6},{3,7},{4,8},{5,9},{6,10},{7,11},{8,12},{9,13},{1... | collective-permute-start | bytes 344072 | tf_op jit(solution)/shard_map/ppermute | solution.py:613
  95.1 1.3 %collective-permute-start.11 = (bf16[432,128]{1,0:T(8,128)(2,1)S(1)}, bf16[432,128]{1,0:T(8,128)(2,1)S(1)}, u32[]{:S(2)}, u32[]{:S(2)}) collective-permute-start(bf16[432,128]{1,0:T(8,128)(2,1)S(1)} %shard_map.165), channel_id=1, source_target_pairs={{0,1},{2,3},{128,129},{130,131},{256,257},{258,259},{384,385},{386... | collective-permute-start | bytes 331784 | tf_op jit(solution)/shard_map/ppermute | solution.py:617
  96.4 3.3 %all-to-all-done.2 = bf16[32,40,128]{2,1,0:T(8,128)(2,1)S(1)} async-done(((bf16[32,40,128]{2,1,0:T(8,128)(2,1)}), bf16[32,40,128]{2,1,0:T(8,128)(2,1)S(1)}, u32[]{:S(2)}, u32[]{:S(2)}) %all-to-all-start.2) | async-done | bytes 327712 | tf_op jit(solution)/shard_map/all_to_all | solution.py:593
  99.7 0.9 shard_map.163
  100.7 0.8 shard_map.166
  (45 shorter events, 3.4 us)
Async XLA Ops:
  2.5 26.2 %copy-start.5 = (s32[144,144]{1,0:T(8,128)S(1)}, s32[144,144]{1,0:T(8,128)}, u32[]{:S(2)}) copy-start(s32[144,144]{1,0:T(8,128)} %pos.1) | copy-start | bytes 248836
  2.6 11.5 %collective-permute-start = (bf16[432,128]{1,0:T(8,128)(2,1)S(1)}, bf16[432,128]{1,0:T(8,128)(2,1)S(1)}, u32[]{:S(2)}, u32[]{:S(2)}) collective-permute-start(bf16[432,128]{1,0:T(8,128)(2,1)S(1)} %get-tuple-element.45), channel_id=1, source_target_pairs={{0,1},{1,0},{2,3},{3,2},{4,5},{5,4},{6,7},{7,6},{8,9},{9,8},{10,11... | collective-permute-start | bytes 331784 | tf_op jit(solution)/shard_map/ppermute | solution.py:518
  11.5 22.6 %collective-permute-start.2 = (bf16[144,128]{1,0:T(8,128)(2,1)S(1)}, bf16[144,128]{1,0:T(8,128)(2,1)S(1)}, u32[]{:S(2)}, u32[]{:S(2)}) collective-permute-start(bf16[144,128]{1,0:T(8,128)(2,1)S(1)} %get-tuple-element.49), channel_id=1, source_target_pairs={{0,3},{2,1},{4,7},{6,5},{8,11},{10,9},{12,15},{14,13},{16,19},{18,... | collective-permute-start | bytes 110600 | tf_op jit(solution)/shard_map/ppermute | solution.py:519
  12.8 21.3 %collective-permute-start.3 = (bf16[144,128]{1,0:T(8,128)(2,1)S(1)}, bf16[144,128]{1,0:T(8,128)(2,1)S(1)}, u32[]{:S(2)}, u32[]{:S(2)}) collective-permute-start(bf16[144,128]{1,0:T(8,128)(2,1)S(1)} %get-tuple-element.47.corner), channel_id=1, source_target_pairs={{0,511},{2,509},{4,3},{6,1},{8,7},{10,5},{12,11},{14,9},{16,15},{1... | collective-permute-start | bytes 110600 | tf_op jit(solution)/shard_map/ppermute | solution.py:520
  14.1 14.6 %copy-start.7 = (f32[1,6,3312]{2,0,1:T(1,128)S(1)}, f32[1,6,3312]{2,0,1:T(1,128)}, u32[]{:S(2)}) copy-start(f32[1,6,3312]{2,0,1:T(1,128)} %param.17) | copy-start | bytes 238468
  14.2 19.9 %collective-permute-start.4 = (bf16[576,128]{1,0:T(8,128)(2,1)S(1)}, bf16[576,128]{1,0:T(8,128)(2,1)S(1)}, u32[]{:S(2)}, u32[]{:S(2)}) collective-permute-start(bf16[576,128]{1,0:T(8,128)(2,1)S(1)} %get-tuple-element.50), channel_id=1, source_target_pairs={{4,0},{5,1},{6,2},{7,3},{8,4},{9,5},{10,6},{11,7},{12,8},{13,9},{1... | collective-permute-start | bytes 442376 | tf_op jit(solution)/shard_map/ppermute | solution.py:529
  15.5 18.6 %collective-permute-start.1 = (bf16[1008,128]{1,0:T(8,128)(2,1)S(1)}, bf16[1008,128]{1,0:T(8,128)(2,1)S(1)}, u32[]{:S(2)}, u32[]{:S(2)}) collective-permute-start(bf16[1008,128]{1,0:T(8,128)(2,1)S(1)} %get-tuple-element.48), channel_id=1, source_target_pairs={{1,509},{3,511},{129,125},{131,127},{257,253},{259,255},{385,381},... | collective-permute-start | bytes 774152 | tf_op jit(solution)/shard_map/ppermute | solution.py:530
  28.7 6.1 %copy-start.1 = (bf16[2,6,24,192]{3,2,1,0:T(8,128)(2,1)S(1)}, bf16[2,6,24,192]{3,2,1,0:T(8,128)(2,1)}, u32[]{:S(2)}) copy-start(bf16[2,6,24,192]{3,2,1,0:T(8,128)(2,1)} %tokens.1) | copy-start | bytes 331780
  28.8 6.1 %copy-start.3 = (bf16[2,6,24,192]{3,2,1,0:T(8,128)(2,1)S(1)}, bf16[2,6,24,192]{3,2,1,0:T(8,128)(2,1)}, u32[]{:S(2)}) copy-start(bf16[2,6,24,192]{3,2,1,0:T(8,128)(2,1)} %d_out.1) | copy-start | bytes 331780
  28.8 6.1 %copy-start.4 = (bf16[192,576]{1,0:T(8,128)(2,1)S(1)}, bf16[192,576]{1,0:T(8,128)(2,1)}, u32[]{:S(2)}) copy-start(bf16[192,576]{1,0:T(8,128)(2,1)} %w_qkv.1) | copy-start | bytes 663556
  28.8 6.1 %copy-start.6 = (bf16[192,192]{1,0:T(8,128)(2,1)S(1)}, bf16[192,192]{1,0:T(8,128)(2,1)}, u32[]{:S(2)}) copy-start(bf16[192,192]{1,0:T(8,128)(2,1)} %wp.1) | copy-start | bytes 221188
  28.8 6.1 %copy-start.10 = (bf16[2,648,144]{2,1,0:T(8,128)(2,1)S(1)}, bf16[2,648,144]{2,1,0:T(8,128)(2,1)}, u32[]{:S(2)}) copy-start(bf16[2,648,144]{2,1,0:T(8,128)(2,1)} %constant.7.clone.back) | copy-start | bytes 1119748
  28.8 6.1 %copy-start.11 = (bf16[2,144,528]{2,1,0:T(8,128)(2,1)S(1)}, bf16[2,144,528]{2,1,0:T(8,128)(2,1)}, u32[]{:S(2)}) copy-start(bf16[2,144,528]{2,1,0:T(8,128)(2,1)} %constant.6.clone.pick) | copy-start | bytes 912388
  34.1 0.7 collective-permute-start.5
  41.5 15.1 %all-to-all-start = ((bf16[32,40,128]{2,1,0:T(8,128)(2,1)}), bf16[32,40,128]{2,1,0:T(8,128)(2,1)S(1)}, u32[]{:S(2)}, u32[]{:S(2)}) async-start(bf16[32,40,128]{2,1,0:T(8,128)(2,1)} %bitcast.5), calls=%async_computation | async-start | bytes 655360 | tf_op jit(solution)/shard_map/all_to_all | solution.py:571
  57.4 27.1 %all-to-all-start.1 = ((bf16[16,40,128]{2,1,0:T(8,128)(2,1)}), bf16[16,40,128]{2,1,0:T(8,128)(2,1)S(1)}, u32[]{:S(2)}, u32[]{:S(2)}) async-start(bf16[16,40,128]{2,1,0:T(8,128)(2,1)} %shard_map.159), calls=%async_computation.1 | async-start | bytes 327680 | tf_op jit(solution)/shard_map/all_to_all | solution.py:586
  68.0 3.4 %collective-permute-start.6 = (bf16[816,128]{1,0:T(8,128)(2,1)S(1)}, bf16[816,128]{1,0:T(8,128)(2,1)S(1)}, u32[]{:S(2)}, u32[]{:S(2)}) collective-permute-start(bf16[816,128]{1,0:T(8,128)(2,1)S(1)} %shard_map.158.own), channel_id=1, source_target_pairs={{0,1},{1,0},{2,3},{3,2},{4,5},{5,4},{6,7},{7,6},{8,9},{9,8},{10,11... | collective-permute-start | bytes 626696 | tf_op jit(solution)/shard_map/ppermute | solution.py:584
  71.3 18.7 %collective-permute-start.7 = (bf16[384,128]{1,0:T(8,128)(2,1)S(1)}, bf16[384,128]{1,0:T(8,128)(2,1)S(1)}, u32[]{:S(2)}, u32[]{:S(2)}) collective-permute-start(bf16[384,128]{1,0:T(8,128)(2,1)S(1)} %shard_map.160.pair), channel_id=1, source_target_pairs={{1,2},{3,0},{5,6},{7,4},{9,10},{11,8},{13,14},{15,12},{17,18},{19,... | collective-permute-start | bytes 294920 | tf_op jit(solution)/shard_map/ppermute | solution.py:588
  83.8 11.3 %collective-permute-start.9 = (bf16[864,128]{1,0:T(8,128)(2,1)S(1)}, bf16[864,128]{1,0:T(8,128)(2,1)S(1)}, u32[]{:S(2)}, u32[]{:S(2)}) collective-permute-start(bf16[864,128]{1,0:T(8,128)(2,1)S(1)} %shard_map.164), channel_id=1, source_target_pairs={{124,128},{126,130},{252,256},{254,258},{380,384},{382,386},{508,0... | collective-permute-start | bytes 663560 | tf_op jit(solution)/shard_map/ppermute | solution.py:590
  85.3 4.8 %copy-start.12 = (bf16[432,72]{1,0:T(8,128)(2,1)S(1)}, bf16[432,72]{1,0:T(8,128)(2,1)}, u32[]{:S(2)}) copy-start(bf16[432,72]{1,0:T(8,128)(2,1)} %constant.8.clone.place) | copy-start | bytes 186628
  85.3 14.4 %all-to-all-start.2 = ((bf16[32,40,128]{2,1,0:T(8,128)(2,1)}), bf16[32,40,128]{2,1,0:T(8,128)(2,1)S(1)}, u32[]{:S(2)}, u32[]{:S(2)}) async-start(bf16[32,40,128]{2,1,0:T(8,128)(2,1)} %shard_map.162), calls=%async_computation.2 | async-start | bytes 655360 | tf_op jit(solution)/shard_map/all_to_all | solution.py:593
  90.5 4.6 %collective-permute-start.10 = (bf16[160,128]{1,0:T(8,128)(2,1)S(1)}, bf16[160,128]{1,0:T(8,128)(2,1)S(1)}, u32[]{:S(2)}, u32[]{:S(2)}) collective-permute-start(bf16[160,128]{1,0:T(8,128)(2,1)S(1)} %get-tuple-element.75.own), channel_id=1, source_target_pairs={{0,1},{2,3},{4,5},{6,7},{8,9},{10,11},{12,13},{14,15},{16,17},{18,... | collective-permute-start | bytes 122888 | tf_op jit(solution)/shard_map/ppermute | solution.py:614
  91.8 8.9 %collective-permute-start.8 = (bf16[448,128]{1,0:T(8,128)(2,1)S(1)}, bf16[448,128]{1,0:T(8,128)(2,1)S(1)}, u32[]{:S(2)}, u32[]{:S(2)}) collective-permute-start(bf16[448,128]{1,0:T(8,128)(2,1)S(1)} %get-tuple-element.74), channel_id=1, source_target_pairs={{0,4},{1,5},{2,6},{3,7},{4,8},{5,9},{6,10},{7,11},{8,12},{9,13},{1... | collective-permute-start | bytes 344072 | tf_op jit(solution)/shard_map/ppermute | solution.py:613
  95.1 5.5 %collective-permute-start.11 = (bf16[432,128]{1,0:T(8,128)(2,1)S(1)}, bf16[432,128]{1,0:T(8,128)(2,1)S(1)}, u32[]{:S(2)}, u32[]{:S(2)}) collective-permute-start(bf16[432,128]{1,0:T(8,128)(2,1)S(1)} %shard_map.165), channel_id=1, source_target_pairs={{0,1},{2,3},{128,129},{130,131},{256,257},{258,259},{384,385},{386... | collective-permute-start | bytes 331784 | tf_op jit(solution)/shard_map/ppermute | solution.py:617
  (4 other events, 3.3 us)
